TPU v7x, 512 devices: a whole 4x4x16 slice. The times are simulated.
512 devices in a mesh: child: 8 (over z_lo), prow: 8 (over z_hi, x), pcol: 8 (over y, core).
Axes of the slice: x: 4, y: 4, z: 16 (z_hi: 2, z_lo: 8; z = z_hi * 8 + z_lo), core: 2. Of those that a mesh axis runs over, the one named last changes fastest.
Arguments:
- parent_inverse: float32 [8, 8, 128, 8, 8, 128], P('child', 'prow', None, None, 'pcol'), may hold values from -6 to 6
- child_blocks: int32 [8, 32], replicated, may hold values from -1 to 63, as said below
- factor_rows: float32 [8, 4, 8, 128, 2048], P('child', None, 'prow', None, 'pcol'), may hold values from -0.09375 to 0.09375
- diag_inverse: float32 [8, 2048, 2048], P('child', 'prow', 'pcol'), may hold values from -6 to 6
Outputs:
- inverse_rows: float32 [8, 4, 8, 128, 2048], P('child', None, 'prow', None, 'pcol')
- inverse_diag: float32 [8, 2048, 2048], P('child', 'prow', 'pcol')
Inputs may be any that keep to these rules, and one draw needn't show every extreme that they name: `child_blocks`: entry j of a child's list is -1 (padding) or a parent block congruent to j modulo 8; no child names a block twice.
All inputs are finite; a program needn't handle non-finite values.
Results may differ from a plain program's by a relative error of at most 0.0003.
Values sent between devices are 32-bit elements; how exact they have to be, the bound alone decides.
No kernel may reach another device: no remote copies, remote signals or barrier semaphores. Data moves between devices by JAX's collectives and lax.ppermute only.
A program may use at most 64 MiB of HBM per device.

v0:
```python
import jax
import jax.numpy as jnp
from jax import lax
from jax.sharding import PartitionSpec as P


def on_device(parent_inverse, child_blocks, factor_rows, diag_inverse):
    grid_rows = lax.axis_size("prow")
    grid_cols = lax.axis_size("pcol")
    child_index = lax.axis_index("child")
    row_index = lax.axis_index("prow")
    col_index = lax.axis_index("pcol")
    slot_count = child_blocks.shape[1]
    row_slots = factor_rows.shape[1]
    block_size = factor_rows.shape[3]
    local_width = factor_rows.shape[4]
    col_slots = slot_count // grid_cols
    held_rows = parent_inverse.shape[0]
    class_blocks = parent_inverse.shape[3]
    own_list = lax.dynamic_index_in_dim(child_blocks, child_index, 0, keepdims=False)
    row_names = lax.dynamic_index_in_dim(
        own_list.reshape(row_slots, grid_rows), row_index, 1, keepdims=False
    )
    col_names = lax.dynamic_index_in_dim(
        own_list.reshape(col_slots, grid_cols), col_index, 1, keepdims=False
    )
    row_alive = row_names >= 0
    col_alive = col_names >= 0
    row_place = jnp.where(row_alive, row_names, 0) // grid_rows
    col_place = jnp.where(col_alive, col_names, 0) // grid_cols
    local_parent = parent_inverse.reshape(held_rows, block_size, class_blocks, block_size)
    whole_panel = lax.all_gather(local_parent, "child", axis=0, tiled=True)
    picked = jnp.take(jnp.take(whole_panel, row_place, axis=0), col_place, axis=2)
    alive_pair = row_alive[:, None, None, None] & col_alive[None, None, :, None]
    restricted = jnp.where(alive_pair, picked, 0.0).reshape(
        row_slots * block_size, col_slots, 1, block_size
    )
    lower_panel = lax.all_gather(factor_rows, "prow", axis=2, tiled=True)
    panel_cols = lower_panel.reshape(col_slots, grid_cols, block_size, local_width)
    product = jnp.einsum(
        "xunb,unbk->xk",
        lax.all_gather(restricted, "pcol", axis=2, tiled=True),
        panel_cols,
        precision=lax.Precision.HIGHEST,
        preferred_element_type=jnp.float32,
    )
    inverse_local = -product
    lower_all = lax.all_gather(factor_rows, "pcol", axis=4, tiled=True).reshape(
        row_slots * block_size, -1
    )
    reduced = lax.psum_scatter(
        jnp.einsum(
            "ik,il->kl",
            lower_all,
            inverse_local,
            precision=lax.Precision.HIGHEST,
            preferred_element_type=jnp.float32,
        ),
        "prow",
        scatter_dimension=0,
        tiled=True,
    )
    inverse_diag = diag_inverse - reduced[None]
    return (inverse_local.reshape(1, row_slots, 1, block_size, local_width), inverse_diag)


def solution(mesh):
    in_specs = (
        P("child", "prow", None, None, "pcol", None),
        P(),
        P("child", None, "prow", None, "pcol"),
        P("child", "prow", "pcol"),
    )
    out_specs = (P("child", None, "prow", None, "pcol"), P("child", "prow", "pcol"))
    return jax.shard_map(
        on_device, mesh=mesh, in_specs=in_specs, out_specs=out_specs, check_vma=False
    )
```

profile of v0, /device:TPU:16, one launch (start us, length us, event | category | flops | bytes accessed | tf_op | source)
XLA Modules:
  0.0 550.6 jit_solution(6416273581757610740)
XLA Ops:
  7.2 0.0 copy-start
  7.2 0.0 all-gather.12.cloned.1.call-start
  7.2 0.7 all-gather.12.cloned.1.call-update
  7.9 0.0 all-gather.8.cloned.1.call-start
  8.0 0.7 all-gather.8.cloned.1.call-update
  8.7 0.0 all-gather.6.cloned.1.call-start
  8.8 0.1 reshape.91
  8.8 0.2 compare_reduce_fusion
  9.1 0.1 reduce.5
  9.2 0.1 reduce.6
  9.3 0.1 broadcast_and_fusion
  9.4 0.1 broadcast_bitcast_fusion
  9.5 109.4 %all-gather.12.cloned.1.call-done = f32[8,1,128,8,1,128]{5,3,4,2,1,0:T(8,128)} async-done(((f32[1,1,128,8,1,128]{5,3,4,2,1,0:T(8,128)}), f32[8,1,128,8,1,128]{5,3,4,2,1,0:T(8,128)}) %all-gather.12.cloned.1.call-update) | async-done | bytes 4194320 | tf_op jit(solution)/shard_map/all_gather | solution.py:32
  118.9 2.9 gather_fusion
  121.8 0.2 broadcast_select_fusion
  122.0 0.4 copy.22
  122.4 0.6 gather_fusion.1
  123.0 1.3 fusion.8
  124.4 0.0 all-gather.6.cloned.1.call-update
  124.4 0.0 all-gather.10.cloned.1.call-start
  124.4 0.5 all-gather.10.cloned.1.call-update
  125.0 0.0 reduce-scatter.2.cloned.1.call-start
  125.0 170.5 %all-gather.8.cloned.1.call-done = f32[1,4,8,128,256]{4,3,1,0,2:T(8,128)} async-done(((f32[1,4,1,128,256]{4,3,1,0,2:T(8,128)}), f32[1,4,8,128,256]{4,3,1,0,2:T(8,128)}) %all-gather.8.cloned.1.call-update) | async-done | bytes 4194320 | tf_op jit(solution)/shard_map/all_gather | solution.py:38
  295.5 48.9 %all-gather.6.cloned.1.call-done = f32[512,4,8,128]{3,0,1,2:T(8,128)} async-done(((f32[512,4,1,128]{3,0,1,2:T(8,128)}), f32[512,4,8,128]{3,0,1,2:T(8,128)}) %all-gather.6.cloned.1.call-update) | async-done | bytes 8388624 | tf_op jit(solution)/shard_map/all_gather | solution.py:42
  344.4 9.8 %fusion.5 = f32[512,256]{1,0:T(8,128)S(1)} fusion(f32[512,4,8,128]{3,0,1,2:T(8,128)} %all-gather.6.cloned.1.call-done, f32[1,4,8,128,256]{4,3,1,0,2:T(8,128)} %all-gather.8.cloned.1.call-done), kind=kOutput, calls=%fused_computation.6 | convolution fusion | flops 6442582016 | bytes 13107200 | tf_op jit(solution)/shard_map/xunb,unbk->xk/dot_general | solution.py:40
  354.2 32.0 %all-gather.10.cloned.1.call-done = f32[1,4,1,128,2048]{4,3,2,1,0:T(8,128)} async-done(((f32[1,4,1,128,256]{4,3,2,1,0:T(8,128)}), f32[1,4,1,128,2048]{4,3,2,1,0:T(8,128)}) %all-gather.10.cloned.1.call-update) | async-done | bytes 4194320 | tf_op jit(solution)/shard_map/all_gather | solution.py:48
  386.2 7.3 %convolution_bitcast_fusion = f32[2048,256]{0,1:T(8,128)} fusion(f32[512,256]{1,0:T(8,128)S(1)} %fusion.5, f32[512,2048]{1,0:T(8,128)} %bitcast.40), kind=kOutput, calls=%fused_computation.4 | convolution fusion | flops 3221225472 | bytes 6815744 | tf_op jit(solution)/shard_map/ik,il->kl/dot_general | solution.py:52
  393.5 0.0 reduce-scatter.2.cloned.1.call-update
  393.5 0.1 copy.24
  393.7 148.6 %reduce-scatter.2.cloned.1.call-done = f32[256,256]{0,1:T(8,128)} async-done(((f32[2048,256]{0,1:T(8,128)}), f32[256,256]{0,1:T(8,128)}) %reduce-scatter.2.cloned.1.call-update) | async-done | bytes 262160 | tf_op jit(solution)/shard_map/reduce_scatter | solution.py:51
  542.3 1.0 bitcast_subtract_fusion
  543.3 0.8 copy.26
  (9 shorter events, 0.1 us)
Async XLA Ops:
  7.2 1.6 copy-start
  7.2 111.8 %all-gather.12.cloned.1.call-start = ((), (), s32[]{:S(2)}) async-start(), calls=%async_computation.5 | async-start | bytes 4718592 | tf_op jit(solution)/shard_map/all_gather | solution.py:32
  7.9 287.6 %all-gather.8.cloned.1.call-start = ((), (), s32[]{:S(2)}) async-start(), calls=%async_computation.2 | async-start | bytes 4718592 | tf_op jit(solution)/shard_map/all_gather | solution.py:38
  8.7 335.7 %all-gather.6.cloned.1.call-start = ((), (), s32[]{:S(2)}) async-start(), calls=%async_computation.1 | async-start | bytes 9437184 | tf_op jit(solution)/shard_map/all_gather | solution.py:42
  124.4 261.8 %all-gather.10.cloned.1.call-start = ((), (), s32[]{:S(2)}) async-start(), calls=%async_computation.3 | async-start | bytes 4718592 | tf_op jit(solution)/shard_map/all_gather | solution.py:48
  125.0 417.3 %reduce-scatter.2.cloned.1.call-start = ((), (), s32[]{:S(2)}) async-start(), calls=%async_computation.4 | async-start | bytes 2359296 | tf_op jit(solution)/shard_map/reduce_scatter | solution.py:51
  354.2 39.3 %copy-start.1 = (f32[512,256]{1,0:T(8,128)}, f32[512,256]{1,0:T(8,128)S(1)}, u32[]{:S(2)}) copy-start(f32[512,256]{1,0:T(8,128)S(1)} %fusion.5) | copy-start | bytes 1572868
  386.2 7.3 %copy-start.2 = (f32[1,256,256]{2,1,0:T(8,128)S(1)}, f32[1,256,256]{2,1,0:T(8,128)}, u32[]{:S(2)}) copy-start(f32[1,256,256]{2,1,0:T(8,128)} %param.7) | copy-start | bytes 786436
Sparse Core Ops, SparseCore 0:
  10.1 108.8 all-gather.11
  122.1 173.2 all-gather.7
  297.6 46.6 all-gather.5
  346.3 39.8 all-gather.9
  393.6 148.5 reduce-scatter.1
where the time goes:
time: 551 us
  waiting for transfers between devices  511 us (93%)
  matrix products  17.1 us (3%)
  between operations  13.9 us (3%)
    all_gather x1, waiting for transfers between devices, on_device(): lower_panel = lax.all_gather(factor_rows, 'prow', axis=2, tiled=True)  170 us
    reduce_scatter x1, waiting for transfers between devices, on_device(): lax.psum_scatter(jnp.einsum('ik,il->kl', lower_all, inverse_local, precis...  149 us
    all_gather x1, waiting for transfers between devices, on_device(): whole_panel = lax.all_gather(local_parent, 'child', axis=0, tiled=True)  109 us
    all_gather x1, waiting for transfers between devices, on_device(): lax.all_gather(restricted, 'pcol', axis=2, tiled=True)  48.9 us
    all_gather x1, waiting for transfers between devices, on_device(): lax.all_gather(factor_rows, 'pcol', axis=4, tiled=True)  32 us
  transfers between devices with their start and end apart: 5, of which 5 were waited for; matrix products, arithmetic and copies ran while one was open for 3% of the time, Pallas kernels for 0%

commit v1 on v0

v1 whole, which is shorter than its diff:
```python
import jax
import jax.numpy as jnp
from jax import lax
from jax.experimental import pallas as pl
from jax.experimental.pallas import tpu as pltpu
from jax.sharding import Mesh, PartitionSpec as P

def shift(value, axis, count, step):
    return lax.ppermute(value, axis, [(i, (i - step) % count) for i in range(count)])


def dot(left, right, contract):
    return lax.dot_general(
        left,
        right,
        (contract, ((), ())),
        precision=lax.Precision.HIGH,
        preferred_element_type=jnp.float32,
    )


def pick_kernel(info, row, out):
    slot = pl.program_id(0)
    block = row[0]
    lane = lax.broadcasted_iota(jnp.int32, block.shape, 1)
    for col in range(4):
        place = info[4 + slot * 4 + col]
        out[0, :, col * 128 : (col + 1) * 128] = jnp.sum(
            jnp.where(lane == place, block, 0.0), axis=1
        )


def pick(rows, row_place, places):
    info = jnp.concatenate([row_place, places.reshape(-1)]).astype(jnp.int32)
    return pl.pallas_call(
        pick_kernel,
        out_shape=jax.ShapeDtypeStruct((4, 128, 512), jnp.float32),
        grid_spec=pltpu.PrefetchScalarGridSpec(
            num_scalar_prefetch=1,
            grid=(4,),
            in_specs=[pl.BlockSpec((1, 128, 8, 128), lambda i, info: (info[i], 0, 0, 0))],
            out_specs=pl.BlockSpec((1, 128, 512), lambda i, info: (i, 0, 0)),
        ),
        compiler_params=pltpu.CompilerParams(vmem_limit_bytes=16 << 20),
        cost_estimate=pl.CostEstimate(flops=0, bytes_accessed=3 << 20, transcendentals=0),
        name="pick",
    )(info, rows)


def on_device(parent_inverse, child_blocks, factor_rows, diag_inverse):
    child, half, x, y, core = (
        lax.axis_index(name) for name in ("zl", "zh", "x", "y", "core")
    )
    row_index, col_index = half * 4 + x, y * 2 + core
    own_list = lax.dynamic_index_in_dim(child_blocks, child, 0, keepdims=False).reshape(4, 8)
    row_names = lax.dynamic_index_in_dim(own_list, row_index, 1, keepdims=False)
    col_names = lax.dynamic_index_in_dim(own_list, col_index, 1, keepdims=False)
    row_alive, col_alive = row_names >= 0, col_names >= 0
    row_place = jnp.where(row_alive, row_names, 0) // 8
    col_place = col_names // 8
    places = jnp.where(row_alive[:, None] & col_alive[None], col_place[None], -1)

    factor = factor_rows.reshape(512, 256)
    parent = parent_inverse.reshape(128, 8, 128)
    gathered = lax.all_gather(parent, "zl", axis=0)

    other = shift(factor, "zh", 2, 1)
    lower = jnp.stack([factor] + [shift(factor, "y", 4, j) for j in (1, 2, 3)])
    near = [factor] + [shift(factor, "x", 4, j) for j in (1, 2, 3)]
    lower = jnp.concatenate([lower, shift(lower, "core", 2, 1)])
    far = [other] + [shift(other, "x", 4, j) for j in (1, 2, 3)]

    met = [2 * ((y + j) % 4) + (core + k) % 2 for j in (0, 1, 3, 2) for k in (0, 1)]
    met = jnp.stack(met)
    place = jnp.where(met // 4 == half, 0, 4) + (met % 4 - x) % 4
    panel = jnp.take(jnp.stack(near + far), place, axis=0)

    to_x = jnp.stack([(x + j) % 4 for j in range(4)])
    block = jnp.concatenate([(1 - half) * 4 + to_x, half * 4 + to_x])
    block_place = jnp.where(block % 2 == core, 0, 4) + (block // 2 - y) % 4
    lower = jnp.take(lower, block_place, axis=0)

    restricted = pick(gathered, row_place, places)
    top, bottom = restricted[:2].reshape(256, 512), restricted[2:].reshape(256, 512)
    top_next, bottom_last = shift(top, "y", 4, 1), shift(bottom, "y", 4, 3)
    bottom_next, top_last = shift(bottom, "y", 4, 1), shift(top, "y", 4, 3)
    top_across, bottom_across = shift(top_next, "y", 4, 1), shift(bottom_last, "y", 4, 3)

    def product(pieces):
        total = None
        for i, piece in enumerate(pieces):
            for k, one in enumerate((piece, shift(piece, "core", 2, 1))):
                term = dot(one, panel[2 * i + k], ((1,), (0,)))
                total = term if total is None else total + term
        return -total

    inverse_local = jnp.concatenate(
        [
            product([top, top_next, top_last, top_across]),
            product([bottom, bottom_next, bottom_last, bottom_across]),
        ]
    )

    def spread(first):
        share = [dot(lower[first + j], inverse_local, ((0,), (0,))) for j in range(4)]
        return share[0] + sum(shift(share[j], "x", 4, -j) for j in (1, 2, 3))

    other_half = shift(spread(0), "zh", 2, 1)
    reduced = spread(4) + other_half
    inverse_diag = diag_inverse - reduced[None]
    return inverse_local.reshape(1, 4, 1, 128, 256), inverse_diag


def solution(mesh):
    fine = Mesh(mesh.devices.reshape(8, 2, 4, 4, 2), ("zl", "zh", "x", "y", "core"))
    rows, cols = ("zh", "x"), ("y", "core")
    in_specs = (
        P("zl", rows, None, None, cols, None),
        P(),
        P("zl", None, rows, None, cols),
        P("zl", rows, cols),
    )
    out_specs = (P("zl", None, rows, None, cols), P("zl", rows, cols))
    return jax.shard_map(
        on_device, mesh=fine, in_specs=in_specs, out_specs=out_specs, check_vma=False
    )
```

time: 551 us -> 284 us (0.52)
  the two profiles are of different devices: /device:TPU:16 before, /device:TPU:32 now
where the time goes in v1:
time: 284 us; the launch traced here: 282 us
  waiting for transfers between devices  109 us (38%)
  starting transfers between devices  102 us (36%)
  local copies, waits for them, and re-layouts  33.1 us (12%)
  between operations  14.8 us (5%)
  matrix products  11.8 us (4%)
  other arithmetic  9.15 us (3%)
    ppermute x32, starting transfers between devices, shift(): lax.ppermute(value, axis, [(i, (i - step) % count) for i in range(count)])  102 us
    ppermute x32, waiting for transfers between devices, shift(): lax.ppermute(value, axis, [(i, (i - step) % count) for i in range(count)])  93.2 us
    unnamed x27, local copies, waits for them, and re-layouts  20.1 us
    all_gather x1, waiting for transfers between devices, on_device(): gathered = lax.all_gather(parent, 'zl', axis=0)  14.7 us
    dot_general x24, matrix products, dot(): lax.dot_general(left, right, (contract, ((), ())), precision=lax.Precisio...  11.8 us
  transfers between devices with their start and end apart: 33, of which 12 were waited for; matrix products, arithmetic and copies ran while one was open for 17% of the time, Pallas kernels for 0%

profile of v1, /device:TPU:32, one launch (start us, length us, event | category | flops | bytes accessed | tf_op | source)
XLA Modules:
  0.0 282.3 jit_solution(15675672808575954048)
XLA Ops:
  7.9 4.7 %collective-permute-start = (f32[512,256]{1,0:T(8,128)}, f32[512,256]{1,0:T(8,128)}, u32[]{:S(2)}, u32[]{:S(2)}) collective-permute-start(f32[512,256]{1,0:T(8,128)} %bitcast.136), channel_id=1, source_target_pairs={{0,24},{8,0},{16,8},{24,16},{1,25},{9,1},{17,9},{25,17},{2,26},{10... | collective-permute-start | bytes 1572872 | tf_op jit(solution)/shard_map/ppermute | solution.py:9
  12.6 14.8 %collective-permute-start.3 = (f32[512,256]{1,0:T(8,128)}, f32[512,256]{1,0:T(8,128)}, u32[]{:S(2)}, u32[]{:S(2)}) collective-permute-start(f32[512,256]{1,0:T(8,128)} %bitcast.137), channel_id=1, source_target_pairs={{0,32},{32,0},{1,33},{33,1},{2,34},{34,2},{3,35},{35,3},{4,36},{36... | collective-permute-start | bytes 1572872 | tf_op jit(solution)/shard_map/ppermute | solution.py:9
  27.4 4.9 %collective-permute-start.21 = (f32[512,256]{1,0:T(8,128)}, f32[512,256]{1,0:T(8,128)}, u32[]{:S(2)}, u32[]{:S(2)}) collective-permute-start(f32[512,256]{1,0:T(8,128)} %bitcast.138), channel_id=1, source_target_pairs={{0,6},{2,0},{4,2},{6,4},{1,7},{3,1},{5,3},{7,5},{8,14},{10,8},{12,... | collective-permute-start | bytes 1572872 | tf_op jit(solution)/shard_map/ppermute | solution.py:9
  32.4 2.5 collective-permute-start.22
  34.9 2.9 %collective-permute-start.23 = (f32[512,256]{1,0:T(8,128)}, f32[512,256]{1,0:T(8,128)S(1)}, u32[]{:S(2)}, u32[]{:S(2)}) collective-permute-start(f32[512,256]{1,0:T(8,128)} %bitcast.140), channel_id=1, source_target_pairs={{0,2},{2,4},{4,6},{6,0},{1,3},{3,5},{5,7},{7,1},{8,10},{10,12},{12... | collective-permute-start | bytes 1572872 | tf_op jit(solution)/shard_map/ppermute | solution.py:9
  40.7 4.5 %copy.19 = f32[8,512,256]{2,1,0:T(8,128)} copy(f32[8,512,256]{2,1,0:T(8,128)} %constant_dynamic-update-slice_fusion) | data formatting | bytes 8388608
  45.5 9.1 %collective-permute-done.21 = f32[512,256]{1,0:T(8,128)} collective-permute-done((f32[512,256]{1,0:T(8,128)}, f32[512,256]{1,0:T(8,128)}, u32[]{:S(2)}, u32[]{:S(2)}) %collective-permute-start.21) | collective-permute-done | bytes 524320 | tf_op jit(solution)/shard_map/ppermute | solution.py:9
  54.5 2.7 collective-permute-start.1
  57.2 2.8 collective-permute-start.2
  60.8 2.6 pad_maximum_fusion
  65.5 29.3 %collective-permute-done.3 = f32[512,256]{1,0:T(8,128)} collective-permute-done((f32[512,256]{1,0:T(8,128)}, f32[512,256]{1,0:T(8,128)}, u32[]{:S(2)}, u32[]{:S(2)}) %collective-permute-start.3) | collective-permute-done | bytes 524320 | tf_op jit(solution)/shard_map/ppermute | solution.py:9
  94.8 2.8 collective-permute-start.4
  103.8 2.8 collective-permute-start.6
  112.6 2.5 collective-permute-done.5
  115.9 4.6 %collective-permute-done.6 = f32[512,256]{1,0:T(8,128)S(1)} collective-permute-done((f32[512,256]{1,0:T(8,128)}, f32[512,256]{1,0:T(8,128)S(1)}, u32[]{:S(2)}, u32[]{:S(2)}) %collective-permute-start.6) | collective-permute-done | bytes 524320 | tf_op jit(solution)/shard_map/ppermute | solution.py:9
  121.4 5.0 %gather_fusion = f32[8,512,256]{2,1,0:T(8,128)} fusion(f32[8,512,256]{2,1,0:T(8,128)} %bitcast_dynamic-update-slice_fusion, s32[1024]{0:T(1024)S(1)} %pad_clamp_fusion.1), kind=kCustom, calls=%fused_computation.clone | custom fusion | bytes 8388640 | tf_op jit(solution)/shard_map/jit(_take)/gather | solution.py:76
  126.4 4.7 %broadcast_select_fusion.1 = f32[8,512,256]{2,1,0:T(8,128)} fusion(f32[8,512,256]{2,1,0:T(8,128)} %gather_fusion, pred[8]{0:T(512)(128)(4,1)S(1)} %get-tuple-element.15), kind=kLoop, calls=%fused_computation.4 | loop fusion | flops 1048576 | bytes 8388616 | tf_op jit(solution)/shard_map/jit(_take)/select_n | solution.py:76
  132.6 5.1 %gather_fusion.1 = f32[8,512,256]{2,1,0:T(8,128)} fusion(f32[8,512,256]{2,1,0:T(8,128)} %constant_dynamic-update-slice_fusion.1, s32[1024]{0:T(1024)S(1)} %pad_clamp_fusion), kind=kCustom, calls=%fused_computation.1.clone | custom fusion | bytes 8388640 | tf_op jit(solution)/shard_map/jit(_take)/gather | solution.py:81
  137.7 14.7 %all-gather.3.cloned.1.call-done = f32[8,1,128,8,1,128]{5,3,4,2,1,0:T(8,128)} async-done(((f32[1,1,128,8,1,128]{5,3,4,2,1,0:T(8,128)}), f32[8,1,128,8,1,128]{5,3,4,2,1,0:T(8,128)}) %all-gather.3.cloned.1.call-update) | async-done | bytes 4194320 | tf_op jit(solution)/shard_map/all_gather | solution.py:65
  154.6 2.8 pick.1
  159.4 4.9 %collective-permute-start.8 = (f32[256,512]{1,0:T(8,128)S(1)}, f32[256,512]{1,0:T(8,128)S(1)}, u32[]{:S(2)}, u32[]{:S(2)}) collective-permute-start(f32[256,512]{1,0:T(8,128)S(1)} %bitcast.133), channel_id=1, source_target_pairs={{0,6},{2,0},{4,2},{6,4},{1,7},{3,1},{5,3},{7,5},{8,14},{10,8},{12,... | collective-permute-start | bytes 1572872 | tf_op jit(solution)/shard_map/ppermute | solution.py:9
  169.1 5.0 %collective-permute-start.15 = (f32[256,512]{1,0:T(8,128)S(1)}, f32[256,512]{1,0:T(8,128)S(1)}, u32[]{:S(2)}, u32[]{:S(2)}) collective-permute-start(f32[256,512]{1,0:T(8,128)S(1)} %bitcast.129), channel_id=1, source_target_pairs={{0,6},{2,0},{4,2},{6,4},{1,7},{3,1},{5,3},{7,5},{8,14},{10,8},{12,... | collective-permute-start | bytes 1572872 | tf_op jit(solution)/shard_map/ppermute | solution.py:9
  179.3 3.6 %collective-permute-done.10 = f32[256,512]{1,0:T(8,128)S(1)} collective-permute-done((f32[256,512]{1,0:T(8,128)S(1)}, f32[256,512]{1,0:T(8,128)S(1)}, u32[]{:S(2)}, u32[]{:S(2)}) %collective-permute-start.10) | collective-permute-done | bytes 524320 | tf_op jit(solution)/shard_map/ppermute | solution.py:9
  190.0 3.4 %collective-permute-done.17 = f32[256,512]{1,0:T(8,128)S(1)} collective-permute-done((f32[256,512]{1,0:T(8,128)S(1)}, f32[256,512]{1,0:T(8,128)S(1)}, u32[]{:S(2)}, u32[]{:S(2)}) %collective-permute-start.17) | collective-permute-done | bytes 524320 | tf_op jit(solution)/shard_map/ppermute | solution.py:9
  200.9 8.8 %collective-permute-done.19 = f32[256,512]{1,0:T(8,128)S(1)} collective-permute-done((f32[256,512]{1,0:T(8,128)S(1)}, f32[256,512]{1,0:T(8,128)S(1)}, u32[]{:S(2)}, u32[]{:S(2)}) %collective-permute-start.19) | collective-permute-done | bytes 524320 | tf_op jit(solution)/shard_map/ppermute | solution.py:9
  217.5 2.7 collective-permute-start.29
  220.2 2.8 collective-permute-start.28
  223.0 4.3 %collective-permute-start.30 = (f32[256,256]{1,0:T(8,128)S(1)}, f32[256,256]{1,0:T(8,128)S(1)}, u32[]{:S(2)}, u32[]{:S(2)}) collective-permute-start(f32[256,256]{1,0:T(8,128)S(1)} %fusion.6), channel_id=1, source_target_pairs={{0,24},{8,0},{16,8},{24,16},{1,25},{9,1},{17,9},{25,17},{2,26},{10... | collective-permute-start | bytes 786440 | tf_op jit(solution)/shard_map/ppermute | solution.py:9
  227.9 3.4 %collective-permute-start.26 = (f32[256,256]{1,0:T(8,128)S(1)}, f32[256,256]{1,0:T(8,128)S(1)}, u32[]{:S(2)}, u32[]{:S(2)}) collective-permute-start(f32[256,256]{1,0:T(8,128)S(1)} %fusion.12), channel_id=1, source_target_pairs={{0,16},{8,24},{16,0},{24,8},{1,17},{9,25},{17,1},{25,9},{2,18},{10... | collective-permute-start | bytes 786440 | tf_op jit(solution)/shard_map/ppermute | solution.py:9
  233.8 5.1 %collective-permute-start.27 = (f32[256,256]{1,0:T(8,128)S(1)}, f32[256,256]{1,0:T(8,128)S(1)}, u32[]{:S(2)}, u32[]{:S(2)}) collective-permute-start(f32[256,256]{1,0:T(8,128)S(1)} %fusion.11), channel_id=1, source_target_pairs={{0,24},{8,0},{16,8},{24,16},{1,25},{9,1},{17,9},{25,17},{2,26},{10... | collective-permute-start | bytes 786440 | tf_op jit(solution)/shard_map/ppermute | solution.py:9
  242.7 3.8 %collective-permute-done.25 = f32[256,256]{1,0:T(8,128)S(1)} collective-permute-done((f32[256,256]{1,0:T(8,128)S(1)}, f32[256,256]{1,0:T(8,128)S(1)}, u32[]{:S(2)}, u32[]{:S(2)}) %collective-permute-start.25) | collective-permute-done | bytes 262176 | tf_op jit(solution)/shard_map/ppermute | solution.py:9
  246.5 27.7 %collective-permute-done.31 = f32[256,256]{1,0:T(8,128)S(1)} collective-permute-done((f32[256,256]{1,0:T(8,128)S(1)}, f32[256,256]{1,0:T(8,128)S(1)}, u32[]{:S(2)}, u32[]{:S(2)}) %collective-permute-start.31) | collective-permute-done | bytes 262176 | tf_op jit(solution)/shard_map/ppermute | solution.py:9
  (112 shorter events, 66.4 us)
Async XLA Ops:
  7.2 145.2 %all-gather.3.cloned.1.call-start = ((), (), s32[]{:S(2)}) async-start(), calls=%async_computation | async-start | bytes 4718592 | tf_op jit(solution)/shard_map/all_gather | solution.py:65
  7.9 91.6 %collective-permute-start = (f32[512,256]{1,0:T(8,128)}, f32[512,256]{1,0:T(8,128)}, u32[]{:S(2)}, u32[]{:S(2)}) collective-permute-start(f32[512,256]{1,0:T(8,128)} %bitcast.136), channel_id=1, source_target_pairs={{0,24},{8,0},{16,8},{24,16},{1,25},{9,1},{17,9},{25,17},{2,26},{10... | collective-permute-start | bytes 1572872 | tf_op jit(solution)/shard_map/ppermute | solution.py:9
  12.6 82.2 %collective-permute-start.3 = (f32[512,256]{1,0:T(8,128)}, f32[512,256]{1,0:T(8,128)}, u32[]{:S(2)}, u32[]{:S(2)}) collective-permute-start(f32[512,256]{1,0:T(8,128)} %bitcast.137), channel_id=1, source_target_pairs={{0,32},{32,0},{1,33},{33,1},{2,34},{34,2},{3,35},{35,3},{4,36},{36... | collective-permute-start | bytes 1572872 | tf_op jit(solution)/shard_map/ppermute | solution.py:9
  27.4 27.1 %collective-permute-start.21 = (f32[512,256]{1,0:T(8,128)}, f32[512,256]{1,0:T(8,128)}, u32[]{:S(2)}, u32[]{:S(2)}) collective-permute-start(f32[512,256]{1,0:T(8,128)} %bitcast.138), channel_id=1, source_target_pairs={{0,6},{2,0},{4,2},{6,4},{1,7},{3,1},{5,3},{7,5},{8,14},{10,8},{12,... | collective-permute-start | bytes 1572872 | tf_op jit(solution)/shard_map/ppermute | solution.py:9
  32.4 24.9 %collective-permute-start.22 = (f32[512,256]{1,0:T(8,128)}, f32[512,256]{1,0:T(8,128)S(1)}, u32[]{:S(2)}, u32[]{:S(2)}) collective-permute-start(f32[512,256]{1,0:T(8,128)} %bitcast.139), channel_id=1, source_target_pairs={{0,4},{2,6},{4,0},{6,2},{1,5},{3,7},{5,1},{7,3},{8,12},{10,14},{12... | collective-permute-start | bytes 1572872 | tf_op jit(solution)/shard_map/ppermute | solution.py:9
  34.9 25.1 %collective-permute-start.23 = (f32[512,256]{1,0:T(8,128)}, f32[512,256]{1,0:T(8,128)S(1)}, u32[]{:S(2)}, u32[]{:S(2)}) collective-permute-start(f32[512,256]{1,0:T(8,128)} %bitcast.140), channel_id=1, source_target_pairs={{0,2},{2,4},{4,6},{6,0},{1,3},{3,5},{5,7},{7,1},{8,10},{10,12},{12... | collective-permute-start | bytes 1572872 | tf_op jit(solution)/shard_map/ppermute | solution.py:9
  54.5 49.3 %collective-permute-start.1 = (f32[512,256]{1,0:T(8,128)S(1)}, f32[512,256]{1,0:T(8,128)S(1)}, u32[]{:S(2)}, u32[]{:S(2)}) collective-permute-start(f32[512,256]{1,0:T(8,128)S(1)} %bitcast.142), channel_id=1, source_target_pairs={{0,16},{8,24},{16,0},{24,8},{1,17},{9,25},{17,1},{25,9},{2,18},{10... | collective-permute-start | bytes 1572872 | tf_op jit(solution)/shard_map/ppermute | solution.py:9
  57.2 50.2 %collective-permute-start.2 = (f32[512,256]{1,0:T(8,128)S(1)}, f32[512,256]{1,0:T(8,128)S(1)}, u32[]{:S(2)}, u32[]{:S(2)}) collective-permute-start(f32[512,256]{1,0:T(8,128)S(1)} %bitcast.143), channel_id=1, source_target_pairs={{0,8},{8,16},{16,24},{24,0},{1,9},{9,17},{17,25},{25,1},{2,10},{10... | collective-permute-start | bytes 1572872 | tf_op jit(solution)/shard_map/ppermute | solution.py:9
  63.4 67.7 %collective-permute-start.24 = (f32[4,512,256]{2,1,0:T(8,128)}, f32[4,512,256]{2,1,0:T(8,128)S(1)}, u32[]{:S(2)}, u32[]{:S(2)}) collective-permute-start(f32[4,512,256]{2,1,0:T(8,128)} %pad_maximum_fusion), channel_id=1, source_target_pairs={{0,1},{1,0},{2,3},{3,2},{4,5},{5,4},{6,7},{7,6},{8,9},{9,8},{10,11... | collective-permute-start | bytes 6291464 | tf_op jit(solution)/shard_map/ppermute | solution.py:9
  94.8 17.0 %collective-permute-start.4 = (f32[512,256]{1,0:T(8,128)}, f32[512,256]{1,0:T(8,128)S(1)}, u32[]{:S(2)}, u32[]{:S(2)}) collective-permute-start(f32[512,256]{1,0:T(8,128)} %collective-permute-done.3), channel_id=1, source_target_pairs={{0,24},{8,0},{16,8},{24,16},{1,25},{9,1},{17,9},{25,17},{2,26},{10... | collective-permute-start | bytes 1572872 | tf_op jit(solution)/shard_map/ppermute | solution.py:9
  99.5 15.6 %collective-permute-start.5 = (f32[512,256]{1,0:T(8,128)}, f32[512,256]{1,0:T(8,128)S(1)}, u32[]{:S(2)}, u32[]{:S(2)}) collective-permute-start(f32[512,256]{1,0:T(8,128)} %collective-permute-done.3), channel_id=1, source_target_pairs={{0,16},{8,24},{16,0},{24,8},{1,17},{9,25},{17,1},{25,9},{2,18},{10... | collective-permute-start | bytes 1572872 | tf_op jit(solution)/shard_map/ppermute | solution.py:9
  103.8 16.8 %collective-permute-start.6 = (f32[512,256]{1,0:T(8,128)}, f32[512,256]{1,0:T(8,128)S(1)}, u32[]{:S(2)}, u32[]{:S(2)}) collective-permute-start(f32[512,256]{1,0:T(8,128)} %collective-permute-done.3), channel_id=1, source_target_pairs={{0,8},{8,16},{16,24},{24,0},{1,9},{9,17},{17,25},{25,1},{2,10},{10... | collective-permute-start | bytes 1572872 | tf_op jit(solution)/shard_map/ppermute | solution.py:9
  157.5 17.4 %collective-permute-start.7 = (f32[256,512]{1,0:T(8,128)S(1)}, f32[256,512]{1,0:T(8,128)S(1)}, u32[]{:S(2)}, u32[]{:S(2)}) collective-permute-start(f32[256,512]{1,0:T(8,128)S(1)} %bitcast.132), channel_id=1, source_target_pairs={{0,1},{1,0},{2,3},{3,2},{4,5},{5,4},{6,7},{7,6},{8,9},{9,8},{10,11... | collective-permute-start | bytes 1572872 | tf_op jit(solution)/shard_map/ppermute | solution.py:9
  159.4 17.4 %collective-permute-start.8 = (f32[256,512]{1,0:T(8,128)S(1)}, f32[256,512]{1,0:T(8,128)S(1)}, u32[]{:S(2)}, u32[]{:S(2)}) collective-permute-start(f32[256,512]{1,0:T(8,128)S(1)} %bitcast.133), channel_id=1, source_target_pairs={{0,6},{2,0},{4,2},{6,4},{1,7},{3,1},{5,3},{7,5},{8,14},{10,8},{12,... | collective-permute-start | bytes 1572872 | tf_op jit(solution)/shard_map/ppermute | solution.py:9
  164.9 18.0 %collective-permute-start.10 = (f32[256,512]{1,0:T(8,128)S(1)}, f32[256,512]{1,0:T(8,128)S(1)}, u32[]{:S(2)}, u32[]{:S(2)}) collective-permute-start(f32[256,512]{1,0:T(8,128)S(1)} %bitcast.134), channel_id=1, source_target_pairs={{0,2},{2,4},{4,6},{6,0},{1,3},{3,5},{5,7},{7,1},{8,10},{10,12},{12... | collective-permute-start | bytes 1572872 | tf_op jit(solution)/shard_map/ppermute | solution.py:9
  167.0 18.7 %collective-permute-start.14 = (f32[256,512]{1,0:T(8,128)S(1)}, f32[256,512]{1,0:T(8,128)S(1)}, u32[]{:S(2)}, u32[]{:S(2)}) collective-permute-start(f32[256,512]{1,0:T(8,128)S(1)} %bitcast.128), channel_id=1, source_target_pairs={{0,1},{1,0},{2,3},{3,2},{4,5},{5,4},{6,7},{7,6},{8,9},{9,8},{10,11... | collective-permute-start | bytes 1572872 | tf_op jit(solution)/shard_map/ppermute | solution.py:9
  169.1 18.8 %collective-permute-start.15 = (f32[256,512]{1,0:T(8,128)S(1)}, f32[256,512]{1,0:T(8,128)S(1)}, u32[]{:S(2)}, u32[]{:S(2)}) collective-permute-start(f32[256,512]{1,0:T(8,128)S(1)} %bitcast.129), channel_id=1, source_target_pairs={{0,6},{2,0},{4,2},{6,4},{1,7},{3,1},{5,3},{7,5},{8,14},{10,8},{12,... | collective-permute-start | bytes 1572872 | tf_op jit(solution)/shard_map/ppermute | solution.py:9
  174.9 18.5 %collective-permute-start.17 = (f32[256,512]{1,0:T(8,128)S(1)}, f32[256,512]{1,0:T(8,128)S(1)}, u32[]{:S(2)}, u32[]{:S(2)}) collective-permute-start(f32[256,512]{1,0:T(8,128)S(1)} %bitcast.131), channel_id=1, source_target_pairs={{0,2},{2,4},{4,6},{6,0},{1,3},{3,5},{5,7},{7,1},{8,10},{10,12},{12... | collective-permute-start | bytes 1572872 | tf_op jit(solution)/shard_map/ppermute | solution.py:9
  176.8 19.7 %collective-permute-start.9 = (f32[256,512]{1,0:T(8,128)S(1)}, f32[256,512]{1,0:T(8,128)S(1)}, u32[]{:S(2)}, u32[]{:S(2)}) collective-permute-start(f32[256,512]{1,0:T(8,128)S(1)} %collective-permute-done.8), channel_id=1, source_target_pairs={{0,1},{1,0},{2,3},{3,2},{4,5},{5,4},{6,7},{7,6},{8,9},{9,8},{10,11... | collective-permute-start | bytes 1572872 | tf_op jit(solution)/shard_map/ppermute | solution.py:9
  182.9 15.7 %collective-permute-start.12 = (f32[256,512]{1,0:T(8,128)S(1)}, f32[256,512]{1,0:T(8,128)S(1)}, u32[]{:S(2)}, u32[]{:S(2)}) collective-permute-start(f32[256,512]{1,0:T(8,128)S(1)} %collective-permute-done.8), channel_id=1, source_target_pairs={{0,6},{2,0},{4,2},{6,4},{1,7},{3,1},{5,3},{7,5},{8,14},{10,8},{12,... | collective-permute-start | bytes 1572872 | tf_op jit(solution)/shard_map/ppermute | solution.py:9
  185.6 26.9 %collective-permute-start.11 = (f32[256,512]{1,0:T(8,128)S(1)}, f32[256,512]{1,0:T(8,128)S(1)}, u32[]{:S(2)}, u32[]{:S(2)}) collective-permute-start(f32[256,512]{1,0:T(8,128)S(1)} %collective-permute-done.10), channel_id=1, source_target_pairs={{0,1},{1,0},{2,3},{3,2},{4,5},{5,4},{6,7},{7,6},{8,9},{9,8},{10,11... | collective-permute-start | bytes 1572872 | tf_op jit(solution)/shard_map/ppermute | solution.py:9
  187.8 25.2 %collective-permute-start.16 = (f32[256,512]{1,0:T(8,128)S(1)}, f32[256,512]{1,0:T(8,128)S(1)}, u32[]{:S(2)}, u32[]{:S(2)}) collective-permute-start(f32[256,512]{1,0:T(8,128)S(1)} %collective-permute-done.15), channel_id=1, source_target_pairs={{0,1},{1,0},{2,3},{3,2},{4,5},{5,4},{6,7},{7,6},{8,9},{9,8},{10,11... | collective-permute-start | bytes 1572872 | tf_op jit(solution)/shard_map/ppermute | solution.py:9
  193.4 16.3 %collective-permute-start.19 = (f32[256,512]{1,0:T(8,128)S(1)}, f32[256,512]{1,0:T(8,128)S(1)}, u32[]{:S(2)}, u32[]{:S(2)}) collective-permute-start(f32[256,512]{1,0:T(8,128)S(1)} %collective-permute-done.17), channel_id=1, source_target_pairs={{0,2},{2,4},{4,6},{6,0},{1,3},{3,5},{5,7},{7,1},{8,10},{10,12},{12... | collective-permute-start | bytes 1572872 | tf_op jit(solution)/shard_map/ppermute | solution.py:9
  196.5 17.3 %collective-permute-start.18 = (f32[256,512]{1,0:T(8,128)S(1)}, f32[256,512]{1,0:T(8,128)S(1)}, u32[]{:S(2)}, u32[]{:S(2)}) collective-permute-start(f32[256,512]{1,0:T(8,128)S(1)} %collective-permute-done.17), channel_id=1, source_target_pairs={{0,1},{1,0},{2,3},{3,2},{4,5},{5,4},{6,7},{7,6},{8,9},{9,8},{10,11... | collective-permute-start | bytes 1572872 | tf_op jit(solution)/shard_map/ppermute | solution.py:9
  198.6 15.6 %collective-permute-start.13 = (f32[256,512]{1,0:T(8,128)S(1)}, f32[256,512]{1,0:T(8,128)S(1)}, u32[]{:S(2)}, u32[]{:S(2)}) collective-permute-start(f32[256,512]{1,0:T(8,128)S(1)} %collective-permute-done.12), channel_id=1, source_target_pairs={{0,1},{1,0},{2,3},{3,2},{4,5},{5,4},{6,7},{7,6},{8,9},{9,8},{10,11... | collective-permute-start | bytes 1572872 | tf_op jit(solution)/shard_map/ppermute | solution.py:9
  217.5 16.4 %collective-permute-start.29 = (f32[256,256]{1,0:T(8,128)S(1)}, f32[256,256]{1,0:T(8,128)S(1)}, u32[]{:S(2)}, u32[]{:S(2)}) collective-permute-start(f32[256,256]{1,0:T(8,128)S(1)} %fusion.7), channel_id=1, source_target_pairs={{0,16},{8,24},{16,0},{24,8},{1,17},{9,25},{17,1},{25,9},{2,18},{10... | collective-permute-start | bytes 786440 | tf_op jit(solution)/shard_map/ppermute | solution.py:9
  220.2 18.8 %collective-permute-start.28 = (f32[256,256]{1,0:T(8,128)S(1)}, f32[256,256]{1,0:T(8,128)S(1)}, u32[]{:S(2)}, u32[]{:S(2)}) collective-permute-start(f32[256,256]{1,0:T(8,128)S(1)} %fusion.8), channel_id=1, source_target_pairs={{0,8},{8,16},{16,24},{24,0},{1,9},{9,17},{17,25},{25,1},{2,10},{10... | collective-permute-start | bytes 786440 | tf_op jit(solution)/shard_map/ppermute | solution.py:9
  223.0 16.0 %collective-permute-start.30 = (f32[256,256]{1,0:T(8,128)S(1)}, f32[256,256]{1,0:T(8,128)S(1)}, u32[]{:S(2)}, u32[]{:S(2)}) collective-permute-start(f32[256,256]{1,0:T(8,128)S(1)} %fusion.6), channel_id=1, source_target_pairs={{0,24},{8,0},{16,8},{24,16},{1,25},{9,1},{17,9},{25,17},{2,26},{10... | collective-permute-start | bytes 786440 | tf_op jit(solution)/shard_map/ppermute | solution.py:9
  227.9 14.8 %collective-permute-start.26 = (f32[256,256]{1,0:T(8,128)S(1)}, f32[256,256]{1,0:T(8,128)S(1)}, u32[]{:S(2)}, u32[]{:S(2)}) collective-permute-start(f32[256,256]{1,0:T(8,128)S(1)} %fusion.12), channel_id=1, source_target_pairs={{0,16},{8,24},{16,0},{24,8},{1,17},{9,25},{17,1},{25,9},{2,18},{10... | collective-permute-start | bytes 786440 | tf_op jit(solution)/shard_map/ppermute | solution.py:9
  231.3 15.2 %collective-permute-start.25 = (f32[256,256]{1,0:T(8,128)S(1)}, f32[256,256]{1,0:T(8,128)S(1)}, u32[]{:S(2)}, u32[]{:S(2)}) collective-permute-start(f32[256,256]{1,0:T(8,128)S(1)} %fusion.13), channel_id=1, source_target_pairs={{0,8},{8,16},{16,24},{24,0},{1,9},{9,17},{17,25},{25,1},{2,10},{10... | collective-permute-start | bytes 786440 | tf_op jit(solution)/shard_map/ppermute | solution.py:9
  233.8 12.6 %collective-permute-start.27 = (f32[256,256]{1,0:T(8,128)S(1)}, f32[256,256]{1,0:T(8,128)S(1)}, u32[]{:S(2)}, u32[]{:S(2)}) collective-permute-start(f32[256,256]{1,0:T(8,128)S(1)} %fusion.11), channel_id=1, source_target_pairs={{0,24},{8,0},{16,8},{24,16},{1,25},{9,1},{17,9},{25,17},{2,26},{10... | collective-permute-start | bytes 786440 | tf_op jit(solution)/shard_map/ppermute | solution.py:9
  239.6 34.6 %collective-permute-start.31 = (f32[256,256]{1,0:T(8,128)S(1)}, f32[256,256]{1,0:T(8,128)S(1)}, u32[]{:S(2)}, u32[]{:S(2)}) collective-permute-start(f32[256,256]{1,0:T(8,128)S(1)} %fusion.10), channel_id=1, source_target_pairs={{0,32},{32,0},{1,33},{33,1},{2,34},{34,2},{3,35},{35,3},{4,36},{36... | collective-permute-start | bytes 786440 | tf_op jit(solution)/shard_map/ppermute | solution.py:9
  (9 other events, 177.4 us)
Sparse Core Ops, SparseCore 0:
  10.1 142.2 all-gather.2

commit v2 on v1

v2 whole, which is shorter than its diff:
```python
import functools

import jax
import jax.numpy as jnp
from jax import lax
from jax.experimental import pallas as pl
from jax.experimental.pallas import tpu as pltpu
from jax.sharding import Mesh, PartitionSpec as P

def shift(value, axis, count, step):
    return lax.ppermute(value, axis, [(i, (i - step) % count) for i in range(count)])


def dot(left, right, contract):
    return lax.dot_general(
        left,
        right,
        (contract, ((), ())),
        precision=lax.Precision.HIGH,
        preferred_element_type=jnp.float32,
    )


def pick_kernel(info, row, out):
    slot = pl.program_id(0)
    for col in range(4):
        place = info[4 + slot * 4 + col]
        found = row[0, pl.ds(jnp.maximum(place, 0), 128, stride=8), :]
        out[col // 2, :, col % 2 * 128 : (col % 2 + 1) * 128] = jnp.where(
            place >= 0, found, 0.0
        )


def pick(rows, row_place, places):
    info = jnp.concatenate([row_place, places.reshape(-1)]).astype(jnp.int32)
    return pl.pallas_call(
        pick_kernel,
        out_shape=jax.ShapeDtypeStruct((2, 512, 256), jnp.float32),
        grid_spec=pltpu.PrefetchScalarGridSpec(
            num_scalar_prefetch=1,
            grid=(4,),
            in_specs=[pl.BlockSpec((1, 1024, 128), lambda i, info: (info[i], 0, 0))],
            out_specs=pl.BlockSpec((2, 128, 256), lambda i, info: (0, i, 0)),
        ),
        compiler_params=pltpu.CompilerParams(vmem_limit_bytes=56 << 20),
        cost_estimate=pl.CostEstimate(flops=0, bytes_accessed=3 << 20, transcendentals=0),
        name="pick",
    )(info, rows.reshape(8, 1024, 128))


def two_halves(value):
    high = value.astype(jnp.bfloat16)
    return high, (value - high.astype(jnp.float32)).astype(jnp.bfloat16)


def product_kernel(terms, count, has_base, classes, *refs):
    restricted, panels = refs[0], refs[1 : 1 + count]
    out, left, right, left_sems, right_sems = refs[1 + count + has_base :]

    def copies(n):
        index, panel, start, k = terms[n]
        yield pltpu.make_async_copy(
            restricted.at[classes[index], k], left.at[n], left_sems.at[n]
        )
        yield pltpu.make_async_copy(
            panels[panel].at[pl.ds(start, 256)], right.at[n], right_sems.at[n]
        )

    for n in range(len(terms)):
        for copy in copies(n):
            copy.start()
    for n in range(len(terms)):
        for copy in copies(n):
            copy.wait()
        if n > 0:
            total = out[...]
        elif has_base:
            total = refs[1 + count][...]
        else:
            total = jnp.zeros(out.shape, jnp.float32)
        lh, ll = two_halves(left[n])
        rh, rl = two_halves(right[n])
        for one, two in ((lh, rh), (lh, rl), (ll, rh)):
            total -= jnp.dot(one, two, preferred_element_type=jnp.float32)
        out[...] = total


def product(restricted, panels, classes, terms, base=None):
    has_base = base is not None
    whole = pl.BlockSpec(memory_space=pltpu.VMEM)
    return pl.pallas_call(
        functools.partial(product_kernel, terms, len(panels), has_base),
        out_shape=jax.ShapeDtypeStruct((512, 256), jnp.float32),
        grid_spec=pltpu.PrefetchScalarGridSpec(
            num_scalar_prefetch=1,
            grid=(),
            in_specs=[pl.BlockSpec(memory_space=pl.ANY)] * (1 + len(panels))
            + [whole] * has_base,
            out_specs=whole,
            scratch_shapes=[
                pltpu.VMEM((len(terms), 512, 256), jnp.float32),
                pltpu.VMEM((len(terms), 256, 256), jnp.float32),
                pltpu.SemaphoreType.DMA((len(terms),)),
                pltpu.SemaphoreType.DMA((len(terms),)),
            ],
        ),
        compiler_params=pltpu.CompilerParams(vmem_limit_bytes=28 << 20),
        cost_estimate=pl.CostEstimate(
            flops=len(terms) * (3 << 26),
            bytes_accessed=len(terms) * (3 << 18),
            transcendentals=0,
        ),
        name="product",
    )(classes, restricted, *panels, *([base] if has_base else []))


def on_device(parent_inverse, child_blocks, factor_rows, diag_inverse):
    child, half, x, y, core = (
        lax.axis_index(name) for name in ("zl", "zh", "x", "y", "core")
    )
    row_index, col_index = half * 4 + x, y * 2 + core
    own_list = lax.dynamic_index_in_dim(child_blocks, child, 0, keepdims=False).reshape(4, 8)
    row_names = lax.dynamic_index_in_dim(own_list, row_index, 1, keepdims=False)
    col_names = lax.dynamic_index_in_dim(own_list, col_index, 1, keepdims=False)
    row_alive, col_alive = row_names >= 0, col_names >= 0
    row_place = jnp.where(row_alive, row_names, 0) // 8
    col_place = col_names // 8
    places = jnp.where(row_alive[:, None] & col_alive[None], col_place[None], -1)

    factor = factor_rows.reshape(512, 256)
    parent = parent_inverse.reshape(128, 8, 128)
    gathered = lax.all_gather(parent, "zl", axis=0)

    lower = jnp.stack([factor] + [shift(factor, "y", 4, j) for j in (1, 2, 3)])
    near = [factor] + [shift(factor, "x", 4, j) for j in (1, 2, 3)]
    lower = jnp.concatenate([lower, shift(lower, "core", 2, 1)])
    to_x = jnp.stack([(x + j) % 4 for j in range(4)])
    block = jnp.concatenate([(1 - half) * 4 + to_x, half * 4 + jnp.arange(4)])
    block_place = jnp.where(block % 2 == core, 0, 4) + (block // 2 - y) % 4
    lower = jnp.take(lower, block_place, axis=0, mode="clip")
    gathered, top, bottom, lower, near = lax.optimization_barrier(
        (gathered, factor[:256], factor[256:], lower, near)
    )

    restricted = pick(gathered, row_place, places)
    restricted = lax.all_gather(restricted, ("y", "core"), axis=0)
    top, bottom = lax.optimization_barrier((shift(top, "zh", 2, 1), bottom))
    bottom = shift(bottom, "zh", 2, 1)
    far_top = [top] + [shift(top, "x", 4, j) for j in (1, 2, 3)]
    far_bottom = [bottom] + [shift(bottom, "x", 4, j) for j in (1, 2, 3)]

    classes = jnp.concatenate([half * 4 + to_x, (1 - half) * 4 + to_x]).astype(jnp.int32)
    terms = [(j, j, 256 * k, k) for j in range(4) for k in (0, 1)]
    terms += [(4 + j, 4 + j, 0, 0) for j in range(4)]
    inverse_local = product(restricted, near + far_top, classes, terms)
    terms = [(4 + j, j, 0, 1) for j in range(4)]
    inverse_local = product(restricted, far_bottom, classes, terms, inverse_local)

    share = [dot(lower[j], inverse_local, ((0,), (0,))) for j in range(4)]
    *share, own_lower = lax.optimization_barrier((*share, lower[4:]))
    other_half = share[0] + sum(shift(share[j], "x", 4, -j) for j in (1, 2, 3))
    other_half = shift(other_half, "zh", 2, 1)
    share = [dot(own_lower[j], inverse_local, ((0,), (0,))) for j in range(4)]
    own_half = lax.psum_scatter(jnp.stack(share), "x", scatter_dimension=0)
    reduced = own_half + other_half
    inverse_diag = diag_inverse - reduced[None]
    return inverse_local.reshape(1, 4, 1, 128, 256), inverse_diag


def solution(mesh):
    fine = Mesh(mesh.devices.reshape(8, 2, 4, 4, 2), ("zl", "zh", "x", "y", "core"))
    rows, cols = ("zh", "x"), ("y", "core")
    in_specs = (
        P("zl", rows, None, None, cols, None),
        P(),
        P("zl", None, rows, None, cols),
        P("zl", rows, cols),
    )
    out_specs = (P("zl", None, rows, None, cols), P("zl", rows, cols))
    return jax.shard_map(
        on_device, mesh=fine, in_specs=in_specs, out_specs=out_specs, check_vma=False
    )
```

time: 284 us -> 275 us (0.968)
  the two profiles are of different devices: /device:TPU:32 before, /device:TPU:14 now
where the time goes in v2:
time: 275 us; the launch traced here: 274 us
  waiting for transfers between devices  138 us (50%)
  starting transfers between devices  71.1 us (26%)
  local copies, waits for them, and re-layouts  20.2 us (7%)
  Pallas kernels  15.4 us (6%)
  between operations  14.2 us (5%)
  matrix products  8.11 us (3%)
  other arithmetic  6.81 us (2%)
    ppermute x19, waiting for transfers between devices, shift(): lax.ppermute(value, axis, [(i, (i - step) % count) for i in range(count)])  76.5 us
    ppermute x19, starting transfers between devices, shift(): lax.ppermute(value, axis, [(i, (i - step) % count) for i in range(count)])  71 us
    all_gather x1, waiting for transfers between devices, on_device(): gathered = lax.all_gather(parent, 'zl', axis=0)  61.1 us
    pallas_call x2, Pallas kernels, product(): pl.pallas_call(functools.partial(product_kernel, terms, len(panels), has_...  11 us
    dot_general x8, matrix products, dot(): lax.dot_general(left, right, (contract, ((), ())), precision=lax.Precisio...  8.11 us
    unnamed x18, local copies, waits for them, and re-layouts  7.83 us
  transfers between devices with their start and end apart: 22, of which 9 were waited for; matrix products, arithmetic and copies ran while one was open for 8% of the time, Pallas kernels for 3%

profile of v2, /device:TPU:14, one launch (start us, length us, event | category | flops | bytes accessed | tf_op | source)
XLA Modules:
  0.0 274.2 jit_solution(13344681936690866179)
XLA Ops:
  8.0 2.4 collective-permute-start
  10.3 4.5 %collective-permute-start.1 = (f32[512,256]{1,0:T(8,128)}, f32[512,256]{1,0:T(8,128)S(1)}, u32[]{:S(2)}, u32[]{:S(2)}) collective-permute-start(f32[512,256]{1,0:T(8,128)} %bitcast.76), channel_id=1, source_target_pairs={{0,4},{2,6},{4,0},{6,2},{1,5},{3,7},{5,1},{7,3},{8,12},{10,14},{12... | collective-permute-start | bytes 1572872 | tf_op jit(solution)/shard_map/ppermute | solution.py:11
  14.8 3.8 %collective-permute-start.2 = (f32[512,256]{1,0:T(8,128)}, f32[512,256]{1,0:T(8,128)}, u32[]{:S(2)}, u32[]{:S(2)}) collective-permute-start(f32[512,256]{1,0:T(8,128)} %bitcast.77), channel_id=1, source_target_pairs={{0,2},{2,4},{4,6},{6,0},{1,3},{3,5},{5,7},{7,1},{8,10},{10,12},{12... | collective-permute-start | bytes 1572872 | tf_op jit(solution)/shard_map/ppermute | solution.py:11
  18.7 2.7 collective-permute-start.4
  21.4 5.4 %collective-permute-start.5 = (f32[512,256]{1,0:T(8,128)}, f32[512,256]{1,0:T(8,128)S(1)}, u32[]{:S(2)}, u32[]{:S(2)}) collective-permute-start(f32[512,256]{1,0:T(8,128)} %bitcast.79), channel_id=1, source_target_pairs={{0,16},{8,24},{16,0},{24,8},{1,17},{9,25},{17,1},{25,9},{2,18},{10... | collective-permute-start | bytes 1572872 | tf_op jit(solution)/shard_map/ppermute | solution.py:11
  27.4 2.3 collective-permute-start.6
  29.7 6.3 %collective-permute-done.1 = f32[512,256]{1,0:T(8,128)S(1)} collective-permute-done((f32[512,256]{1,0:T(8,128)}, f32[512,256]{1,0:T(8,128)S(1)}, u32[]{:S(2)}, u32[]{:S(2)}) %collective-permute-start.1) | collective-permute-done | bytes 524320 | tf_op jit(solution)/shard_map/ppermute | solution.py:11
  36.0 2.8 %collective-permute-done.2 = f32[512,256]{1,0:T(8,128)} collective-permute-done((f32[512,256]{1,0:T(8,128)}, f32[512,256]{1,0:T(8,128)}, u32[]{:S(2)}, u32[]{:S(2)}) %collective-permute-start.2) | collective-permute-done | bytes 524320 | tf_op jit(solution)/shard_map/ppermute | solution.py:11
  38.8 2.8 %pad_maximum_fusion = f32[4,512,256]{2,1,0:T(8,128)} fusion(f32[1,512,256]{2,1,0:T(8,128)} %bitcast.12, f32[1,512,256]{2,1,0:T(8,128)S(1)} %bitcast.87, f32[1,512,256]{2,1,0:T(8,128)S(1)} %bitcast.86, f32[1,512,256]{2,1,0:T(8,128)} %bitcast.81), kind=kLoop, calls=%fused_computation.1 | loop fusion | flops 1572864 | bytes 4194304 | tf_op jit(solution)/shard_map/stack | solution.py:134
  49.7 3.1 %constant_dynamic-update-slice_fusion = f32[8,512,256]{2,1,0:T(8,128)} fusion(f32[8,512,256]{2,1,0:T(8,128)} %constant_dynamic-update-slice_fusion.1, f32[4,512,256]{2,1,0:T(8,128)} %collective-permute-done.3), kind=kLoop, calls=%fused_computation.30 | loop fusion | bytes 4194304 | tf_op jit(solution)/shard_map/concatenate | solution.py:136
  52.8 5.0 %gather_fusion = f32[8,512,256]{2,1,0:T(8,128)} fusion(f32[8,512,256]{2,1,0:T(8,128)} %constant_dynamic-update-slice_fusion, s32[1024]{0:T(1024)S(1)} %pad_clamp_fusion), kind=kCustom, calls=%fused_computation | custom fusion | bytes 8388640 | tf_op jit(solution)/shard_map/jit(_take)/gather | solution.py:140
  57.8 61.1 %all-gather.5.cloned.1.call-done = f32[8,1,128,8,1,128]{5,3,4,2,1,0:T(8,128)} async-done(((f32[1,1,128,8,1,128]{5,3,4,2,1,0:T(8,128)}), f32[8,1,128,8,1,128]{5,3,4,2,1,0:T(8,128)}) %all-gather.5.cloned.1.call-update) | async-done | bytes 4194320 | tf_op jit(solution)/shard_map/all_gather | solution.py:132
  119.0 4.4 %pick.1 = f32[2,512,256]{2,1,0:T(8,128)} custom-call(s32[20]{0:T(128)} %pad_add_fusion.2.info, f32[8,1024,128]{2,1,0:T(8,128)} %bitcast.85), custom_call_target="tpu_custom_call" | custom-call | bytes 3145728 | tf_op jit(solution)/shard_map/pick/pallas_call | solution.py:36
  123.4 4.9 %collective-permute-start.7 = (f32[256,256]{1,0:T(8,128)S(1)}, f32[256,256]{1,0:T(8,128)S(1)}, u32[]{:S(2)}, u32[]{:S(2)}) collective-permute-start(f32[256,256]{1,0:T(8,128)S(1)} %bitcast.89), channel_id=1, source_target_pairs={{0,32},{32,0},{1,33},{33,1},{2,34},{34,2},{3,35},{35,3},{4,36},{36... | collective-permute-start | bytes 786440 | tf_op jit(solution)/shard_map/ppermute | solution.py:11
  128.3 26.8 %collective-permute-done.7.refs_5_ = f32[256,256]{1,0:T(8,128)S(1)} collective-permute-done((f32[256,256]{1,0:T(8,128)S(1)}, f32[256,256]{1,0:T(8,128)S(1)}, u32[]{:S(2)}, u32[]{:S(2)}) %collective-permute-start.7) | collective-permute-done | bytes 262176 | tf_op jit(solution)/shard_map/ppermute | solution.py:11
  155.1 7.0 %collective-permute-start.8 = (f32[256,256]{1,0:T(8,128)}, f32[256,256]{1,0:T(8,128)S(1)}, u32[]{:S(2)}, u32[]{:S(2)}) collective-permute-start(f32[256,256]{1,0:T(8,128)} %bitcast.7), channel_id=1, source_target_pairs={{0,32},{32,0},{1,33},{33,1},{2,34},{34,2},{3,35},{35,3},{4,36},{36... | collective-permute-start | bytes 786440 | tf_op jit(solution)/shard_map/ppermute | solution.py:11
  162.2 2.4 collective-permute-start.12
  164.6 3.1 %collective-permute-start.13 = (f32[256,256]{1,0:T(8,128)S(1)}, f32[256,256]{1,0:T(8,128)S(1)}, u32[]{:S(2)}, u32[]{:S(2)}) collective-permute-start(f32[256,256]{1,0:T(8,128)S(1)} %collective-permute-done.7.refs_5_), channel_id=1, source_target_pairs={{0,16},{8,24},{16,0},{24,8},{1,17},{9,25},{17,1},{25,9},{2,18},{10... | collective-permute-start | bytes 786440 | tf_op jit(solution)/shard_map/ppermute | solution.py:11
  167.7 4.0 %collective-permute-start.14 = (f32[256,256]{1,0:T(8,128)S(1)}, f32[256,256]{1,0:T(8,128)S(1)}, u32[]{:S(2)}, u32[]{:S(2)}) collective-permute-start(f32[256,256]{1,0:T(8,128)S(1)} %collective-permute-done.7.refs_5_), channel_id=1, source_target_pairs={{0,8},{8,16},{16,24},{24,0},{1,9},{9,17},{17,25},{25,1},{2,10},{10... | collective-permute-start | bytes 786440 | tf_op jit(solution)/shard_map/ppermute | solution.py:11
  171.7 8.0 %collective-permute-done.8.refs_1_ = f32[256,256]{1,0:T(8,128)S(1)} collective-permute-done((f32[256,256]{1,0:T(8,128)}, f32[256,256]{1,0:T(8,128)S(1)}, u32[]{:S(2)}, u32[]{:S(2)}) %collective-permute-start.8) | collective-permute-done | bytes 262176 | tf_op jit(solution)/shard_map/ppermute | solution.py:11
  179.7 5.3 %collective-permute-start.10 = (f32[256,256]{1,0:T(8,128)S(1)}, f32[256,256]{1,0:T(8,128)}, u32[]{:S(2)}, u32[]{:S(2)}) collective-permute-start(f32[256,256]{1,0:T(8,128)S(1)} %collective-permute-done.8.refs_1_), channel_id=1, source_target_pairs={{0,16},{8,24},{16,0},{24,8},{1,17},{9,25},{17,1},{25,9},{2,18},{10... | collective-permute-start | bytes 786440 | tf_op jit(solution)/shard_map/ppermute | solution.py:11
  185.0 4.0 %collective-permute-start.11 = (f32[256,256]{1,0:T(8,128)S(1)}, f32[256,256]{1,0:T(8,128)}, u32[]{:S(2)}, u32[]{:S(2)}) collective-permute-start(f32[256,256]{1,0:T(8,128)S(1)} %collective-permute-done.8.refs_1_), channel_id=1, source_target_pairs={{0,8},{8,16},{16,24},{24,0},{1,9},{9,17},{17,25},{25,1},{2,10},{10... | collective-permute-start | bytes 786440 | tf_op jit(solution)/shard_map/ppermute | solution.py:11
  191.2 3.0 %slice.47 = f32[4,512,256]{2,1,0:T(8,128)} slice(f32[8,512,256]{2,1,0:T(8,128)} %gather_fusion), slice={[4:8], [0:512], [0:256]} | slice | bytes 4194304 | tf_op jit(solution)/shard_map/slice | solution.py:160
  194.3 3.4 %copy-done.1 = f32[16,512,256]{2,1,0:T(8,128)S(1)} copy-done((f32[16,512,256]{2,1,0:T(8,128)S(1)}, f32[16,512,256]{2,1,0:T(8,128)}, u32[]{:S(2)}) %copy-start.1) | copy-done | bytes 8388632
  197.7 6.9 %product.2.refs_5_ = f32[512,256]{1,0:T(8,128)S(1)} custom-call(s32[8]{0:T(128)S(1)} %pad_add_fusion.1.classes, f32[8,2,512,256]{3,2,1,0:T(8,128)S(1)} %bitcast.73, f32[512,256]{1,0:T(8,128)S(1)} %bitcast.83, f32[512,256]{1,0:T(8,128)S(1)} %collective-permute-done.4.refs_2_, f32[512,256]{1,0:T(8,128)S(1)} %collective-permute-done.5.refs_3_, ...), custom_call_target="tpu_custom_call" | custom-call | flops 2415919104 | bytes 9437184 | tf_op jit(solution)/shard_map/product/pallas_call | solution.py:91
  204.6 4.1 %product.3 = f32[512,256]{1,0:T(8,128)} custom-call(s32[8]{0:T(128)S(1)} %pad_add_fusion.1.classes, f32[8,2,512,256]{3,2,1,0:T(8,128)S(1)} %bitcast.74, f32[256,256]{1,0:T(8,128)S(1)} %collective-permute-done.8.refs_1_, f32[256,256]{1,0:T(8,128)} %collective-permute-done.9.refs_2_, f32[256,256]{1,0:T(8,128)} %collective-permute-done.10.refs_3_, ...), custom_call_target="tpu_custom_call" | custom-call | flops 805306368 | bytes 3145728 | tf_op jit(solution)/shard_map/product/pallas_call | solution.py:91
  218.0 5.1 %collective-permute-start.15 = (f32[256,256]{1,0:T(8,128)S(1)}, f32[256,256]{1,0:T(8,128)S(1)}, u32[]{:S(2)}, u32[]{:S(2)}) collective-permute-start(f32[256,256]{1,0:T(8,128)S(1)} %fusion.8), channel_id=1, source_target_pairs={{0,8},{8,16},{16,24},{24,0},{1,9},{9,17},{17,25},{25,1},{2,10},{10... | collective-permute-start | bytes 786440 | tf_op jit(solution)/shard_map/ppermute | solution.py:11
  225.1 2.8 %collective-permute-start.17 = (f32[256,256]{1,0:T(8,128)S(1)}, f32[256,256]{1,0:T(8,128)S(1)}, u32[]{:S(2)}, u32[]{:S(2)}) collective-permute-start(f32[256,256]{1,0:T(8,128)S(1)} %fusion.4), channel_id=1, source_target_pairs={{0,24},{8,0},{16,8},{24,16},{1,25},{9,1},{17,9},{25,17},{2,26},{10... | collective-permute-start | bytes 786440 | tf_op jit(solution)/shard_map/ppermute | solution.py:11
  227.9 8.4 %collective-permute-done.15 = f32[256,256]{1,0:T(8,128)S(1)} collective-permute-done((f32[256,256]{1,0:T(8,128)S(1)}, f32[256,256]{1,0:T(8,128)S(1)}, u32[]{:S(2)}, u32[]{:S(2)}) %collective-permute-start.15) | collective-permute-done | bytes 262176 | tf_op jit(solution)/shard_map/ppermute | solution.py:11
  238.1 6.4 %collective-permute-done.17 = f32[256,256]{1,0:T(8,128)S(1)} collective-permute-done((f32[256,256]{1,0:T(8,128)S(1)}, f32[256,256]{1,0:T(8,128)S(1)}, u32[]{:S(2)}, u32[]{:S(2)}) %collective-permute-start.17) | collective-permute-done | bytes 262176 | tf_op jit(solution)/shard_map/ppermute | solution.py:11
  244.5 5.4 %collective-permute-start.18 = (f32[256,256]{1,0:T(8,128)S(1)}, f32[256,256]{1,0:T(8,128)S(1)}, u32[]{:S(2)}, u32[]{:S(2)}) collective-permute-start(f32[256,256]{1,0:T(8,128)S(1)} %add_add_fusion), channel_id=1, source_target_pairs={{0,32},{32,0},{1,33},{33,1},{2,34},{34,2},{3,35},{35,3},{4,36},{36... | collective-permute-start | bytes 786440 | tf_op jit(solution)/shard_map/ppermute | solution.py:11
  250.0 15.9 %collective-permute-done.18 = f32[256,256]{1,0:T(8,128)S(1)} collective-permute-done((f32[256,256]{1,0:T(8,128)S(1)}, f32[256,256]{1,0:T(8,128)S(1)}, u32[]{:S(2)}, u32[]{:S(2)}) %collective-permute-start.18) | collective-permute-done | bytes 262176 | tf_op jit(solution)/shard_map/ppermute | solution.py:11
  (68 shorter events, 26.3 us)
Async XLA Ops:
  7.2 19.7 %copy-start = (s32[8,32]{1,0:T(8,128)S(1)}, s32[8,32]{1,0:T(8,128)}, u32[]{:S(2)}) copy-start(s32[8,32]{1,0:T(8,128)} %param.5) | copy-start | bytes 3076
  7.2 37.3 %copy-start.2 = (f32[1,4,1,128,256]{4,3,2,1,0:T(8,128)S(1)}, f32[1,4,1,128,256]{4,3,2,1,0:T(8,128)}, u32[]{:S(2)}) copy-start(f32[1,4,1,128,256]{4,3,2,1,0:T(8,128)} %param.6) | copy-start | bytes 1572868
  7.2 111.8 %all-gather.5.cloned.1.call-start = ((), (), s32[]{:S(2)}) async-start(), calls=%async_computation.2 | async-start | bytes 4718592 | tf_op jit(solution)/shard_map/all_gather | solution.py:132
  7.9 186.3 %all-gather.7.cloned.1.call-start = ((), (), s32[]{:S(2)}) async-start(), calls=%async_computation.3 | async-start | bytes 9437184 | tf_op jit(solution)/shard_map/all_gather | solution.py:146
  8.0 19.4 %collective-permute-start = (f32[512,256]{1,0:T(8,128)}, f32[512,256]{1,0:T(8,128)S(1)}, u32[]{:S(2)}, u32[]{:S(2)}) collective-permute-start(f32[512,256]{1,0:T(8,128)} %bitcast.75), channel_id=1, source_target_pairs={{0,6},{2,0},{4,2},{6,4},{1,7},{3,1},{5,3},{7,5},{8,14},{10,8},{12,... | collective-permute-start | bytes 1572872 | tf_op jit(solution)/shard_map/ppermute | solution.py:11
  10.3 25.6 %collective-permute-start.1 = (f32[512,256]{1,0:T(8,128)}, f32[512,256]{1,0:T(8,128)S(1)}, u32[]{:S(2)}, u32[]{:S(2)}) collective-permute-start(f32[512,256]{1,0:T(8,128)} %bitcast.76), channel_id=1, source_target_pairs={{0,4},{2,6},{4,0},{6,2},{1,5},{3,7},{5,1},{7,3},{8,12},{10,14},{12... | collective-permute-start | bytes 1572872 | tf_op jit(solution)/shard_map/ppermute | solution.py:11
  14.8 24.0 %collective-permute-start.2 = (f32[512,256]{1,0:T(8,128)}, f32[512,256]{1,0:T(8,128)}, u32[]{:S(2)}, u32[]{:S(2)}) collective-permute-start(f32[512,256]{1,0:T(8,128)} %bitcast.77), channel_id=1, source_target_pairs={{0,2},{2,4},{4,6},{6,0},{1,3},{3,5},{5,7},{7,1},{8,10},{10,12},{12... | collective-permute-start | bytes 1572872 | tf_op jit(solution)/shard_map/ppermute | solution.py:11
  18.7 39.2 %collective-permute-start.4 = (f32[512,256]{1,0:T(8,128)}, f32[512,256]{1,0:T(8,128)S(1)}, u32[]{:S(2)}, u32[]{:S(2)}) collective-permute-start(f32[512,256]{1,0:T(8,128)} %bitcast.78), channel_id=1, source_target_pairs={{0,24},{8,0},{16,8},{24,16},{1,25},{9,1},{17,9},{25,17},{2,26},{10... | collective-permute-start | bytes 1572872 | tf_op jit(solution)/shard_map/ppermute | solution.py:11
  21.4 36.4 %collective-permute-start.5 = (f32[512,256]{1,0:T(8,128)}, f32[512,256]{1,0:T(8,128)S(1)}, u32[]{:S(2)}, u32[]{:S(2)}) collective-permute-start(f32[512,256]{1,0:T(8,128)} %bitcast.79), channel_id=1, source_target_pairs={{0,16},{8,24},{16,0},{24,8},{1,17},{9,25},{17,1},{25,9},{2,18},{10... | collective-permute-start | bytes 1572872 | tf_op jit(solution)/shard_map/ppermute | solution.py:11
  27.4 30.4 %collective-permute-start.6 = (f32[512,256]{1,0:T(8,128)}, f32[512,256]{1,0:T(8,128)S(1)}, u32[]{:S(2)}, u32[]{:S(2)}) collective-permute-start(f32[512,256]{1,0:T(8,128)} %bitcast.80), channel_id=1, source_target_pairs={{0,8},{8,16},{16,24},{24,0},{1,9},{9,17},{17,25},{25,1},{2,10},{10... | collective-permute-start | bytes 1572872 | tf_op jit(solution)/shard_map/ppermute | solution.py:11
  41.7 8.0 %collective-permute-start.3 = (f32[4,512,256]{2,1,0:T(8,128)}, f32[4,512,256]{2,1,0:T(8,128)}, u32[]{:S(2)}, u32[]{:S(2)}) collective-permute-start(f32[4,512,256]{2,1,0:T(8,128)} %pad_maximum_fusion), channel_id=1, source_target_pairs={{0,1},{1,0},{2,3},{3,2},{4,5},{5,4},{6,7},{7,6},{8,9},{9,8},{10,11... | collective-permute-start | bytes 6291464 | tf_op jit(solution)/shard_map/ppermute | solution.py:11
  123.4 142.5 %reduce-scatter.2.cloned.1.call-start = ((), (), s32[]{:S(2)}) async-start(), calls=%async_computation.1 | async-start | bytes 1310720 | tf_op jit(solution)/shard_map/reduce_scatter | solution.py:164
  123.4 31.7 %collective-permute-start.7 = (f32[256,256]{1,0:T(8,128)S(1)}, f32[256,256]{1,0:T(8,128)S(1)}, u32[]{:S(2)}, u32[]{:S(2)}) collective-permute-start(f32[256,256]{1,0:T(8,128)S(1)} %bitcast.89), channel_id=1, source_target_pairs={{0,32},{32,0},{1,33},{33,1},{2,34},{34,2},{3,35},{35,3},{4,36},{36... | collective-permute-start | bytes 786440 | tf_op jit(solution)/shard_map/ppermute | solution.py:11
  155.1 24.6 %collective-permute-start.8 = (f32[256,256]{1,0:T(8,128)}, f32[256,256]{1,0:T(8,128)S(1)}, u32[]{:S(2)}, u32[]{:S(2)}) collective-permute-start(f32[256,256]{1,0:T(8,128)} %bitcast.7), channel_id=1, source_target_pairs={{0,32},{32,0},{1,33},{33,1},{2,34},{34,2},{3,35},{35,3},{4,36},{36... | collective-permute-start | bytes 786440 | tf_op jit(solution)/shard_map/ppermute | solution.py:11
  162.2 26.8 %collective-permute-start.12 = (f32[256,256]{1,0:T(8,128)S(1)}, f32[256,256]{1,0:T(8,128)S(1)}, u32[]{:S(2)}, u32[]{:S(2)}) collective-permute-start(f32[256,256]{1,0:T(8,128)S(1)} %collective-permute-done.7.refs_5_), channel_id=1, source_target_pairs={{0,24},{8,0},{16,8},{24,16},{1,25},{9,1},{17,9},{25,17},{2,26},{10... | collective-permute-start | bytes 786440 | tf_op jit(solution)/shard_map/ppermute | solution.py:11
  164.6 29.6 %collective-permute-start.13 = (f32[256,256]{1,0:T(8,128)S(1)}, f32[256,256]{1,0:T(8,128)S(1)}, u32[]{:S(2)}, u32[]{:S(2)}) collective-permute-start(f32[256,256]{1,0:T(8,128)S(1)} %collective-permute-done.7.refs_5_), channel_id=1, source_target_pairs={{0,16},{8,24},{16,0},{24,8},{1,17},{9,25},{17,1},{25,9},{2,18},{10... | collective-permute-start | bytes 786440 | tf_op jit(solution)/shard_map/ppermute | solution.py:11
  167.7 26.6 %collective-permute-start.14 = (f32[256,256]{1,0:T(8,128)S(1)}, f32[256,256]{1,0:T(8,128)S(1)}, u32[]{:S(2)}, u32[]{:S(2)}) collective-permute-start(f32[256,256]{1,0:T(8,128)S(1)} %collective-permute-done.7.refs_5_), channel_id=1, source_target_pairs={{0,8},{8,16},{16,24},{24,0},{1,9},{9,17},{17,25},{25,1},{2,10},{10... | collective-permute-start | bytes 786440 | tf_op jit(solution)/shard_map/ppermute | solution.py:11
  179.7 24.9 %collective-permute-start.10 = (f32[256,256]{1,0:T(8,128)S(1)}, f32[256,256]{1,0:T(8,128)}, u32[]{:S(2)}, u32[]{:S(2)}) collective-permute-start(f32[256,256]{1,0:T(8,128)S(1)} %collective-permute-done.8.refs_1_), channel_id=1, source_target_pairs={{0,16},{8,24},{16,0},{24,8},{1,17},{9,25},{17,1},{25,9},{2,18},{10... | collective-permute-start | bytes 786440 | tf_op jit(solution)/shard_map/ppermute | solution.py:11
  185.0 19.5 %collective-permute-start.11 = (f32[256,256]{1,0:T(8,128)S(1)}, f32[256,256]{1,0:T(8,128)}, u32[]{:S(2)}, u32[]{:S(2)}) collective-permute-start(f32[256,256]{1,0:T(8,128)S(1)} %collective-permute-done.8.refs_1_), channel_id=1, source_target_pairs={{0,8},{8,16},{16,24},{24,0},{1,9},{9,17},{17,25},{25,1},{2,10},{10... | collective-permute-start | bytes 786440 | tf_op jit(solution)/shard_map/ppermute | solution.py:11
  189.0 15.6 %collective-permute-start.9 = (f32[256,256]{1,0:T(8,128)S(1)}, f32[256,256]{1,0:T(8,128)}, u32[]{:S(2)}, u32[]{:S(2)}) collective-permute-start(f32[256,256]{1,0:T(8,128)S(1)} %collective-permute-done.8.refs_1_), channel_id=1, source_target_pairs={{0,24},{8,0},{16,8},{24,16},{1,25},{9,1},{17,9},{25,17},{2,26},{10... | collective-permute-start | bytes 786440 | tf_op jit(solution)/shard_map/ppermute | solution.py:11
  194.3 3.4 %copy-start.1 = (f32[16,512,256]{2,1,0:T(8,128)S(1)}, f32[16,512,256]{2,1,0:T(8,128)}, u32[]{:S(2)}) copy-start(f32[16,512,256]{2,1,0:T(8,128)} %all-gather.7.cloned.1.call-done) | copy-start | bytes 25165828
  204.5 4.2 %copy-start.4 = (f32[8,512,256]{2,1,0:T(8,128)S(1)}, f32[8,512,256]{2,1,0:T(8,128)}, u32[]{:S(2)}) copy-start(f32[8,512,256]{2,1,0:T(8,128)} %gather_fusion) | copy-start | bytes 12582916
  208.7 5.1 %copy-start.3 = (f32[512,256]{1,0:T(8,128)S(1)}, f32[512,256]{1,0:T(8,128)}, u32[]{:S(2)}) copy-start(f32[512,256]{1,0:T(8,128)} %product.3) | copy-start | bytes 1572868
  208.7 5.7 %copy-start.5 = (f32[4,512,256]{2,1,0:T(8,128)S(1)}, f32[4,512,256]{2,1,0:T(8,128)}, u32[]{:S(2)}) copy-start(f32[4,512,256]{2,1,0:T(8,128)} %slice.47) | copy-start | bytes 6291460
  215.1 50.8 %copy-start.6 = (f32[1,256,256]{2,1,0:T(8,128)S(1)}, f32[1,256,256]{2,1,0:T(8,128)}, u32[]{:S(2)}) copy-start(f32[1,256,256]{2,1,0:T(8,128)} %param.7) | copy-start | bytes 786436
  218.0 18.3 %collective-permute-start.15 = (f32[256,256]{1,0:T(8,128)S(1)}, f32[256,256]{1,0:T(8,128)S(1)}, u32[]{:S(2)}, u32[]{:S(2)}) collective-permute-start(f32[256,256]{1,0:T(8,128)S(1)} %fusion.8), channel_id=1, source_target_pairs={{0,8},{8,16},{16,24},{24,0},{1,9},{9,17},{17,25},{25,1},{2,10},{10... | collective-permute-start | bytes 786440 | tf_op jit(solution)/shard_map/ppermute | solution.py:11
  223.2 14.9 %collective-permute-start.16 = (f32[256,256]{1,0:T(8,128)S(1)}, f32[256,256]{1,0:T(8,128)S(1)}, u32[]{:S(2)}, u32[]{:S(2)}) collective-permute-start(f32[256,256]{1,0:T(8,128)S(1)} %fusion.6), channel_id=1, source_target_pairs={{0,16},{8,24},{16,0},{24,8},{1,17},{9,25},{17,1},{25,9},{2,18},{10... | collective-permute-start | bytes 786440 | tf_op jit(solution)/shard_map/ppermute | solution.py:11
  225.1 19.4 %collective-permute-start.17 = (f32[256,256]{1,0:T(8,128)S(1)}, f32[256,256]{1,0:T(8,128)S(1)}, u32[]{:S(2)}, u32[]{:S(2)}) collective-permute-start(f32[256,256]{1,0:T(8,128)S(1)} %fusion.4), channel_id=1, source_target_pairs={{0,24},{8,0},{16,8},{24,16},{1,25},{9,1},{17,9},{25,17},{2,26},{10... | collective-permute-start | bytes 786440 | tf_op jit(solution)/shard_map/ppermute | solution.py:11
  244.5 21.4 %collective-permute-start.18 = (f32[256,256]{1,0:T(8,128)S(1)}, f32[256,256]{1,0:T(8,128)S(1)}, u32[]{:S(2)}, u32[]{:S(2)}) collective-permute-start(f32[256,256]{1,0:T(8,128)S(1)} %add_add_fusion), channel_id=1, source_target_pairs={{0,32},{32,0},{1,33},{33,1},{2,34},{34,2},{3,35},{35,3},{4,36},{36... | collective-permute-start | bytes 786440 | tf_op jit(solution)/shard_map/ppermute | solution.py:11
Sparse Core Ops, SparseCore 0:
  10.1 108.8 all-gather.4
  123.5 50.9 all-gather.6
  218.1 30.4 reduce-scatter.1

commit v3 on v2

--- a/solution.py
+++ b/solution.py
@@ -21,31 +21,98 @@
     )
 
 
-def pick_kernel(info, row, out):
-    slot = pl.program_id(0)
-    for col in range(4):
-        place = info[4 + slot * 4 + col]
-        found = row[0, pl.ds(jnp.maximum(place, 0), 128, stride=8), :]
-        out[col // 2, :, col % 2 * 128 : (col % 2 + 1) * 128] = jnp.where(
-            place >= 0, found, 0.0
-        )
-
-
-def pick(rows, row_place, places):
-    info = jnp.concatenate([row_place, places.reshape(-1)]).astype(jnp.int32)
+def column_block(row, place):
+    found = row[pl.ds(jnp.maximum(place, 0), 128, stride=8), :]
+    return jnp.where(place >= 0, found, 0.0)
+
+
+def trim_kernel(info, up, down, *refs):
+    outs, held, sem = refs[:3], refs[3], refs[4]
+    for n, row in enumerate((up, down)):
+
+        @pl.when(info[0] == n)
+        def _():
+            pltpu.make_async_copy(row, held, sem).start()
+
+    pltpu.make_async_copy(up, held, sem).wait()
+    for n, out in enumerate(outs):
+        for col in range(4):
+            out[:, col * 128 : (col + 1) * 128] = column_block(held, info[1 + n * 4 + col])
+
+
+def trim(up, down, side, places):
+    info = jnp.concatenate([side[None], places.reshape(-1)]).astype(jnp.int32)
+    return pl.pallas_call(
+        trim_kernel,
+        out_shape=[jax.ShapeDtypeStruct((128, 512), jnp.float32)] * 3,
+        grid_spec=pltpu.PrefetchScalarGridSpec(
+            num_scalar_prefetch=1,
+            grid=(),
+            in_specs=[pl.BlockSpec(memory_space=pl.ANY)] * 2,
+            out_specs=[pl.BlockSpec(memory_space=pltpu.VMEM)] * 3,
+            scratch_shapes=[
+                pltpu.VMEM((1024, 128), jnp.float32),
+                pltpu.SemaphoreType.DMA,
+            ],
+        ),
+        compiler_params=pltpu.CompilerParams(vmem_limit_bytes=16 << 20),
+        cost_estimate=pl.CostEstimate(flops=0, bytes_accessed=5 << 18, transcendentals=0),
+        name="trim",
+    )(info, up, down)
+
+
+def pick_kernel(info, *refs):
+    rows, cut, out, held, held_cut, sems = refs[:9], refs[9:12], *refs[12:]
+    for slot in range(4):
+        for n in range(12):
+
+            @pl.when(info[slot] == n)
+            def _():
+                if n < 9:
+                    pltpu.make_async_copy(rows[n], held.at[slot], sems.at[slot]).start()
+                else:
+                    pltpu.make_async_copy(
+                        cut[n - 9], held_cut.at[slot], sems.at[slot]
+                    ).start()
+
+    for slot in range(4):
+        here = slice(slot * 128, (slot + 1) * 128)
+
+        @pl.when(info[slot] < 9)
+        def _():
+            pltpu.make_async_copy(rows[0], held.at[slot], sems.at[slot]).wait()
+            for col in range(4):
+                out[col // 2, here, col % 2 * 128 : (col % 2 + 1) * 128] = column_block(
+                    held.at[slot], info[4 + slot * 4 + col]
+                )
+
+        @pl.when(info[slot] >= 9)
+        def _():
+            pltpu.make_async_copy(cut[0], held_cut.at[slot], sems.at[slot]).wait()
+            for k in range(2):
+                out[k, here, :] = held_cut[slot, :, k * 256 : (k + 1) * 256]
+
+
+def pick(rows, cut, source, places):
+    info = jnp.concatenate([source, places.reshape(-1)]).astype(jnp.int32)
     return pl.pallas_call(
         pick_kernel,
         out_shape=jax.ShapeDtypeStruct((2, 512, 256), jnp.float32),
         grid_spec=pltpu.PrefetchScalarGridSpec(
             num_scalar_prefetch=1,
-            grid=(4,),
-            in_specs=[pl.BlockSpec((1, 1024, 128), lambda i, info: (info[i], 0, 0))],
-            out_specs=pl.BlockSpec((2, 128, 256), lambda i, info: (0, i, 0)),
+            grid=(),
+            in_specs=[pl.BlockSpec(memory_space=pl.ANY)] * 12,
+            out_specs=pl.BlockSpec(memory_space=pltpu.VMEM),
+            scratch_shapes=[
+                pltpu.VMEM((4, 1024, 128), jnp.float32),
+                pltpu.VMEM((4, 128, 512), jnp.float32),
+                pltpu.SemaphoreType.DMA((4,)),
+            ],
         ),
         compiler_params=pltpu.CompilerParams(vmem_limit_bytes=56 << 20),
         cost_estimate=pl.CostEstimate(flops=0, bytes_accessed=3 << 20, transcendentals=0),
         name="pick",
-    )(info, rows.reshape(8, 1024, 128))
+    )(info, *rows, *cut)
 
 
 def two_halves(value):
@@ -119,51 +186,79 @@
         lax.axis_index(name) for name in ("zl", "zh", "x", "y", "core")
     )
     row_index, col_index = half * 4 + x, y * 2 + core
-    own_list = lax.dynamic_index_in_dim(child_blocks, child, 0, keepdims=False).reshape(4, 8)
+    lists = child_blocks.reshape(8, 4, 8)
+    own_list = lax.dynamic_index_in_dim(lists, child, 0, keepdims=False)
     row_names = lax.dynamic_index_in_dim(own_list, row_index, 1, keepdims=False)
-    col_names = lax.dynamic_index_in_dim(own_list, col_index, 1, keepdims=False)
-    row_alive, col_alive = row_names >= 0, col_names >= 0
-    row_place = jnp.where(row_alive, row_names, 0) // 8
-    col_place = col_names // 8
-    places = jnp.where(row_alive[:, None] & col_alive[None], col_place[None], -1)
+    col_names = lax.dynamic_index_in_dim(lists, col_index, 2, keepdims=False)
+    row_alive = row_names >= 0
+    col_place = jnp.where(col_names >= 0, col_names // 8, -1)
+    offset = jnp.where(row_alive, row_names // 8 - child, 0)
+    away = jnp.abs(offset)
+    source = jnp.where(
+        away > 4, away + 4, jnp.where(offset < 0, 2 * away - 1, 2 * away)
+    )
+    places = jnp.where(
+        row_alive[:, None],
+        lax.dynamic_index_in_dim(col_place, child, 0, keepdims=True),
+        -1,
+    )
 
     factor = factor_rows.reshape(512, 256)
-    parent = parent_inverse.reshape(128, 8, 128)
-    gathered = lax.all_gather(parent, "zl", axis=0)
-
-    lower = jnp.stack([factor] + [shift(factor, "y", 4, j) for j in (1, 2, 3)])
-    near = [factor] + [shift(factor, "x", 4, j) for j in (1, 2, 3)]
-    lower = jnp.concatenate([lower, shift(lower, "core", 2, 1)])
+    lower = lax.all_gather(factor, ("y", "core"), axis=0)
+    near = lax.all_gather(factor, "x", axis=0).reshape(2048, 256)
+
+    up = down = parent_inverse.reshape(1024, 128)
+    rows = [up]
+    for _ in range(4):
+        up = lax.ppermute(up, "zl", [(i, i + 1) for i in range(7)])
+        down = lax.ppermute(down, "zl", [(i + 1, i) for i in range(7)])
+        up, down = lax.optimization_barrier((up, down))
+        rows += [up, down]
+    side = (child < 4).astype(jnp.int32)
+    further = child + (1 - 2 * side) * jnp.arange(1, 4, dtype=jnp.int32)
+    asked = jnp.take(col_place, jnp.clip(further, 0, 7), axis=0, mode="clip")
+    cut = [
+        lax.ppermute(
+            part,
+            "zl",
+            [(i, i + d) for i in range(4, 8 - d)] + [(i, i - d) for i in range(d, 4)],
+        )
+        for d, part in zip((1, 2, 3), trim(up, down, side, asked))
+    ]
+
     to_x = jnp.stack([(x + j) % 4 for j in range(4)])
-    block = jnp.concatenate([(1 - half) * 4 + to_x, half * 4 + jnp.arange(4)])
-    block_place = jnp.where(block % 2 == core, 0, 4) + (block // 2 - y) % 4
-    lower = jnp.take(lower, block_place, axis=0, mode="clip")
-    gathered, top, bottom, lower, near = lax.optimization_barrier(
-        (gathered, factor[:256], factor[256:], lower, near)
-    )
-
-    restricted = pick(gathered, row_place, places)
+    block = jnp.concatenate([(1 - half) * 4 + to_x, half * 4 + to_x])
+    *cut, top, bottom, lower, near = lax.optimization_barrier(
+        (*cut, factor[:256], factor[256:], lower, near)
+    )
+
+    restricted = pick(rows, cut, source, places)
+    restricted, lower = lax.optimization_barrier((restricted, lower))
+    lower = jnp.take(lower, block, axis=0, mode="clip")
+    lower, top = lax.optimization_barrier((lower, top))
     restricted = lax.all_gather(restricted, ("y", "core"), axis=0)
     top, bottom = lax.optimization_barrier((shift(top, "zh", 2, 1), bottom))
     bottom = shift(bottom, "zh", 2, 1)
     far_top = [top] + [shift(top, "x", 4, j) for j in (1, 2, 3)]
+
+    number = jnp.arange(4, dtype=jnp.int32)
+    classes = jnp.concatenate([half * 4 + number, (1 - half) * 4 + to_x]).astype(jnp.int32)
+    terms = [(j, 0, 512 * j + 256 * k, k) for j in range(4) for k in (0, 1)]
+    terms += [(4 + j, 1 + j, 0, 0) for j in range(4)]
+    inverse_local = product(restricted, [near] + far_top, classes, terms)
     far_bottom = [bottom] + [shift(bottom, "x", 4, j) for j in (1, 2, 3)]
-
-    classes = jnp.concatenate([half * 4 + to_x, (1 - half) * 4 + to_x]).astype(jnp.int32)
-    terms = [(j, j, 256 * k, k) for j in range(4) for k in (0, 1)]
-    terms += [(4 + j, 4 + j, 0, 0) for j in range(4)]
-    inverse_local = product(restricted, near + far_top, classes, terms)
     terms = [(4 + j, j, 0, 1) for j in range(4)]
     inverse_local = product(restricted, far_bottom, classes, terms, inverse_local)
 
     share = [dot(lower[j], inverse_local, ((0,), (0,))) for j in range(4)]
     *share, own_lower = lax.optimization_barrier((*share, lower[4:]))
     other_half = share[0] + sum(shift(share[j], "x", 4, -j) for j in (1, 2, 3))
+    share = [dot(own_lower[j], inverse_local, ((0,), (0,))) for j in range(4)]
+    other_half, *share = lax.optimization_barrier((other_half, *share))
     other_half = shift(other_half, "zh", 2, 1)
-    share = [dot(own_lower[j], inverse_local, ((0,), (0,))) for j in range(4)]
-    own_half = lax.psum_scatter(jnp.stack(share), "x", scatter_dimension=0)
-    reduced = own_half + other_half
-    inverse_diag = diag_inverse - reduced[None]
+    own_half = share[0] + sum(shift(share[j], "x", 4, -j) for j in (1, 2, 3))
+    rest, own_half = lax.optimization_barrier((diag_inverse[0] - other_half, own_half))
+    inverse_diag = (rest - own_half)[None]
     return inverse_local.reshape(1, 4, 1, 128, 256), inverse_diag
 
 

time: 275 us -> 258 us (0.938)
  the two profiles are of different devices: /device:TPU:14 before, /device:TPU:66 now
where the time goes in v3:
time: 258 us; the launch traced here: 257 us
  waiting for transfers between devices  106 us (41%)
  starting transfers between devices  95.7 us (37%)
  local copies, waits for them, and re-layouts  15.8 us (6%)
  Pallas kernels  14.9 us (6%)
  between operations  14.3 us (6%)
  matrix products  8.06 us (3%)
    ppermute x15, starting transfers between devices, shift(): lax.ppermute(value, axis, [(i, (i - step) % count) for i in range(count)])  65.9 us
    ppermute x15, waiting for transfers between devices, shift(): lax.ppermute(value, axis, [(i, (i - step) % count) for i in range(count)])  46 us
    ppermute x4, waiting for transfers between devices, on_device(): up = lax.ppermute(up, 'zl', [(i, i + 1) for i in range(7)])  29.5 us
    ppermute x4, waiting for transfers between devices, on_device(): down = lax.ppermute(down, 'zl', [(i + 1, i) for i in range(7)])  16.9 us
    ppermute x4, starting transfers between devices, on_device(): up = lax.ppermute(up, 'zl', [(i, i + 1) for i in range(7)])  16.8 us
    ppermute x3, waiting for transfers between devices, on_device(): lax.ppermute(part, 'zl', [(i, i + d) for i in range(4, 8 - d)] + [(i, i -...  12.7 us
    pallas_call x2, Pallas kernels, product(): pl.pallas_call(functools.partial(product_kernel, terms, len(panels), has_...  10.9 us
    dot_general x8, matrix products, dot(): lax.dot_general(left, right, (contract, ((), ())), precision=lax.Precisio...  8.06 us
  transfers between devices with their start and end apart: 29, of which 17 were waited for; matrix products, arithmetic and copies ran while one was open for 5% of the time, Pallas kernels for 3%

profile of v3, /device:TPU:66, one launch (start us, length us, event | category | flops | bytes accessed | tf_op | source)
XLA Modules:
  0.0 257.1 jit_solution(11610168520416350928)
XLA Ops:
  8.7 3.8 %collective-permute-start = (f32[1024,128]{1,0:T(8,128)}, f32[1024,128]{1,0:T(8,128)S(1)}, u32[]{:S(2)}, u32[]{:S(2)}) collective-permute-start(f32[1024,128]{1,0:T(8,128)} %bitcast.74), channel_id=1, source_target_pairs={{0,64},{64,128},{128,192},{192,256},{256,320},{320,384},{384,448},... | collective-permute-start | bytes 1572872 | tf_op jit(solution)/shard_map/ppermute | solution.py:213
  14.6 9.9 %collective-permute-done.refs_1_ = f32[1024,128]{1,0:T(8,128)S(1)} collective-permute-done((f32[1024,128]{1,0:T(8,128)}, f32[1024,128]{1,0:T(8,128)S(1)}, u32[]{:S(2)}, u32[]{:S(2)}) %collective-permute-start) | collective-permute-done | bytes 524320 | tf_op jit(solution)/shard_map/ppermute | solution.py:213
  24.5 4.9 %collective-permute-done.1.refs_2_ = f32[1024,128]{1,0:T(8,128)S(1)} collective-permute-done((f32[1024,128]{1,0:T(8,128)}, f32[1024,128]{1,0:T(8,128)S(1)}, u32[]{:S(2)}, u32[]{:S(2)}) %collective-permute-start.1) | collective-permute-done | bytes 524320 | tf_op jit(solution)/shard_map/ppermute | solution.py:214
  29.4 4.8 %collective-permute-start.2 = (f32[1024,128]{1,0:T(8,128)S(1)}, f32[1024,128]{1,0:T(8,128)S(1)}, u32[]{:S(2)}, u32[]{:S(2)}) collective-permute-start(f32[1024,128]{1,0:T(8,128)S(1)} %collective-permute-done.refs_1_), channel_id=1, source_target_pairs={{0,64},{64,128},{128,192},{192,256},{256,320},{320,384},{384,448},... | collective-permute-start | bytes 1572872 | tf_op jit(solution)/shard_map/ppermute | solution.py:213
  37.3 7.0 %collective-permute-done.2.refs_3_ = f32[1024,128]{1,0:T(8,128)S(1)} collective-permute-done((f32[1024,128]{1,0:T(8,128)S(1)}, f32[1024,128]{1,0:T(8,128)S(1)}, u32[]{:S(2)}, u32[]{:S(2)}) %collective-permute-start.2) | collective-permute-done | bytes 524320 | tf_op jit(solution)/shard_map/ppermute | solution.py:213
  44.2 4.1 %collective-permute-done.3.refs_4_ = f32[1024,128]{1,0:T(8,128)S(1)} collective-permute-done((f32[1024,128]{1,0:T(8,128)S(1)}, f32[1024,128]{1,0:T(8,128)S(1)}, u32[]{:S(2)}, u32[]{:S(2)}) %collective-permute-start.3) | collective-permute-done | bytes 524320 | tf_op jit(solution)/shard_map/ppermute | solution.py:214
  48.4 4.2 %collective-permute-start.4 = (f32[1024,128]{1,0:T(8,128)S(1)}, f32[1024,128]{1,0:T(8,128)}, u32[]{:S(2)}, u32[]{:S(2)}) collective-permute-start(f32[1024,128]{1,0:T(8,128)S(1)} %collective-permute-done.2.refs_3_), channel_id=1, source_target_pairs={{0,64},{64,128},{128,192},{192,256},{256,320},{320,384},{384,448},... | collective-permute-start | bytes 1572872 | tf_op jit(solution)/shard_map/ppermute | solution.py:213
  55.3 6.4 %collective-permute-done.4.refs_5_ = f32[1024,128]{1,0:T(8,128)} collective-permute-done((f32[1024,128]{1,0:T(8,128)S(1)}, f32[1024,128]{1,0:T(8,128)}, u32[]{:S(2)}, u32[]{:S(2)}) %collective-permute-start.4) | collective-permute-done | bytes 524320 | tf_op jit(solution)/shard_map/ppermute | solution.py:213
  61.7 4.0 %collective-permute-done.5.refs_6_ = f32[1024,128]{1,0:T(8,128)} collective-permute-done((f32[1024,128]{1,0:T(8,128)S(1)}, f32[1024,128]{1,0:T(8,128)}, u32[]{:S(2)}, u32[]{:S(2)}) %collective-permute-start.5) | collective-permute-done | bytes 524320 | tf_op jit(solution)/shard_map/ppermute | solution.py:214
  65.8 3.9 %collective-permute-start.6 = (f32[1024,128]{1,0:T(8,128)}, f32[1024,128]{1,0:T(8,128)S(1)}, u32[]{:S(2)}, u32[]{:S(2)}) collective-permute-start(f32[1024,128]{1,0:T(8,128)} %collective-permute-done.4.refs_5_), channel_id=1, source_target_pairs={{0,64},{64,128},{128,192},{192,256},{256,320},{320,384},{384,448},... | collective-permute-start | bytes 1572872 | tf_op jit(solution)/shard_map/ppermute | solution.py:213
  71.9 6.3 %collective-permute-done.6.up.refs_7_ = f32[1024,128]{1,0:T(8,128)S(1)} collective-permute-done((f32[1024,128]{1,0:T(8,128)}, f32[1024,128]{1,0:T(8,128)S(1)}, u32[]{:S(2)}, u32[]{:S(2)}) %collective-permute-start.6) | collective-permute-done | bytes 524320 | tf_op jit(solution)/shard_map/ppermute | solution.py:213
  78.1 3.8 %collective-permute-done.7.down.refs_8_ = f32[1024,128]{1,0:T(8,128)S(1)} collective-permute-done((f32[1024,128]{1,0:T(8,128)}, f32[1024,128]{1,0:T(8,128)S(1)}, u32[]{:S(2)}, u32[]{:S(2)}) %collective-permute-start.7) | collective-permute-done | bytes 524320 | tf_op jit(solution)/shard_map/ppermute | solution.py:214
  90.3 10.5 %collective-permute-done.8.refs_9_ = f32[128,512]{1,0:T(8,128)S(1)} collective-permute-done((f32[128,512]{1,0:T(8,128)S(1)}, f32[128,512]{1,0:T(8,128)S(1)}, u32[]{:S(2)}, u32[]{:S(2)}) %collective-permute-start.8) | collective-permute-done | bytes 262176 | tf_op jit(solution)/shard_map/ppermute | solution.py:221
  107.2 4.9 %gather_fusion.1 = f32[8,512,256]{2,1,0:T(8,128)} fusion(f32[8,512,256]{2,1,0:T(8,128)} %all-gather.5.cloned.1.call-done, s32[1024]{0:T(1024)S(1)} %pad_clamp_fusion), kind=kCustom, calls=%fused_computation.1 | custom fusion | bytes 8388640 | tf_op jit(solution)/shard_map/jit(_take)/gather | solution.py:237
  112.1 10.1 %collective-permute-start.11 = (f32[256,256]{1,0:T(8,128)S(1)}, f32[256,256]{1,0:T(8,128)S(1)}, u32[]{:S(2)}, u32[]{:S(2)}) collective-permute-start(f32[256,256]{1,0:T(8,128)S(1)} %bitcast.77), channel_id=1, source_target_pairs={{0,32},{32,0},{1,33},{33,1},{2,34},{34,2},{3,35},{35,3},{4,36},{36... | collective-permute-start | bytes 786440 | tf_op jit(solution)/shard_map/ppermute | solution.py:11
  122.3 21.0 %collective-permute-done.11.refs_2_ = f32[256,256]{1,0:T(8,128)S(1)} collective-permute-done((f32[256,256]{1,0:T(8,128)S(1)}, f32[256,256]{1,0:T(8,128)S(1)}, u32[]{:S(2)}, u32[]{:S(2)}) %collective-permute-start.11) | collective-permute-done | bytes 262176 | tf_op jit(solution)/shard_map/ppermute | solution.py:11
  143.3 8.2 %collective-permute-start.12 = (f32[256,256]{1,0:T(8,128)}, f32[256,256]{1,0:T(8,128)S(1)}, u32[]{:S(2)}, u32[]{:S(2)}) collective-permute-start(f32[256,256]{1,0:T(8,128)} %bitcast.11), channel_id=1, source_target_pairs={{0,32},{32,0},{1,33},{33,1},{2,34},{34,2},{3,35},{35,3},{4,36},{36... | collective-permute-start | bytes 786440 | tf_op jit(solution)/shard_map/ppermute | solution.py:11
  154.0 4.4 %collective-permute-start.17 = (f32[256,256]{1,0:T(8,128)S(1)}, f32[256,256]{1,0:T(8,128)S(1)}, u32[]{:S(2)}, u32[]{:S(2)}) collective-permute-start(f32[256,256]{1,0:T(8,128)S(1)} %collective-permute-done.11.refs_2_), channel_id=1, source_target_pairs={{0,16},{8,24},{16,0},{24,8},{1,17},{9,25},{17,1},{25,9},{2,18},{10... | collective-permute-start | bytes 786440 | tf_op jit(solution)/shard_map/ppermute | solution.py:11
  158.4 3.6 %collective-permute-start.18 = (f32[256,256]{1,0:T(8,128)S(1)}, f32[256,256]{1,0:T(8,128)S(1)}, u32[]{:S(2)}, u32[]{:S(2)}) collective-permute-start(f32[256,256]{1,0:T(8,128)S(1)} %collective-permute-done.11.refs_2_), channel_id=1, source_target_pairs={{0,8},{8,16},{16,24},{24,0},{1,9},{9,17},{17,25},{25,1},{2,10},{10... | collective-permute-start | bytes 786440 | tf_op jit(solution)/shard_map/ppermute | solution.py:11
  161.9 9.3 %collective-permute-done.12.refs_1_ = f32[256,256]{1,0:T(8,128)S(1)} collective-permute-done((f32[256,256]{1,0:T(8,128)}, f32[256,256]{1,0:T(8,128)S(1)}, u32[]{:S(2)}, u32[]{:S(2)}) %collective-permute-start.12) | collective-permute-done | bytes 262176 | tf_op jit(solution)/shard_map/ppermute | solution.py:11
  173.7 4.4 %collective-permute-start.14 = (f32[256,256]{1,0:T(8,128)S(1)}, f32[256,256]{1,0:T(8,128)}, u32[]{:S(2)}, u32[]{:S(2)}) collective-permute-start(f32[256,256]{1,0:T(8,128)S(1)} %collective-permute-done.12.refs_1_), channel_id=1, source_target_pairs={{0,16},{8,24},{16,0},{24,8},{1,17},{9,25},{17,1},{25,9},{2,18},{10... | collective-permute-start | bytes 786440 | tf_op jit(solution)/shard_map/ppermute | solution.py:11
  178.1 3.8 %collective-permute-start.15 = (f32[256,256]{1,0:T(8,128)S(1)}, f32[256,256]{1,0:T(8,128)}, u32[]{:S(2)}, u32[]{:S(2)}) collective-permute-start(f32[256,256]{1,0:T(8,128)S(1)} %collective-permute-done.12.refs_1_), channel_id=1, source_target_pairs={{0,8},{8,16},{16,24},{24,0},{1,9},{9,17},{17,25},{25,1},{2,10},{10... | collective-permute-start | bytes 786440 | tf_op jit(solution)/shard_map/ppermute | solution.py:11
  188.3 6.8 %product.2.refs_5_ = f32[512,256]{1,0:T(8,128)S(1)} custom-call(s32[8]{0:T(128)S(1)} %get-tuple-element.83.classes, f32[8,2,512,256]{3,2,1,0:T(8,128)S(1)} %bitcast.68, f32[2048,256]{1,0:T(8,128)S(1)} %bitcast.70, f32[256,256]{1,0:T(8,128)S(1)} %collective-permute-done.11.refs_2_, f32[256,256]{1,0:T(8,128)S(1)} %collective-permute-done.16.refs_3_, ...), custom_call_target="tpu_custom_call" | custom-call | flops 2415919104 | bytes 9437184 | tf_op jit(solution)/shard_map/product/pallas_call | solution.py:158
  195.2 4.1 %product.3 = f32[512,256]{1,0:T(8,128)} custom-call(s32[8]{0:T(128)S(1)} %get-tuple-element.83.classes, f32[8,2,512,256]{3,2,1,0:T(8,128)S(1)} %bitcast.69, f32[256,256]{1,0:T(8,128)S(1)} %collective-permute-done.12.refs_1_, f32[256,256]{1,0:T(8,128)} %collective-permute-done.13.refs_2_, f32[256,256]{1,0:T(8,128)} %collective-permute-done.14.refs_3_, ...), custom_call_target="tpu_custom_call" | custom-call | flops 805306368 | bytes 3145728 | tf_op jit(solution)/shard_map/product/pallas_call | solution.py:158
  208.2 4.3 %collective-permute-start.20 = (f32[256,256]{1,0:T(8,128)S(1)}, f32[256,256]{1,0:T(8,128)S(1)}, u32[]{:S(2)}, u32[]{:S(2)}) collective-permute-start(f32[256,256]{1,0:T(8,128)S(1)} %fusion.10), channel_id=1, source_target_pairs={{0,16},{8,24},{16,0},{24,8},{1,17},{9,25},{17,1},{25,9},{2,18},{10... | collective-permute-start | bytes 786440 | tf_op jit(solution)/shard_map/ppermute | solution.py:11
  212.5 3.6 %collective-permute-start.21 = (f32[256,256]{1,0:T(8,128)S(1)}, f32[256,256]{1,0:T(8,128)S(1)}, u32[]{:S(2)}, u32[]{:S(2)}) collective-permute-start(f32[256,256]{1,0:T(8,128)S(1)} %fusion.8), channel_id=1, source_target_pairs={{0,24},{8,0},{16,8},{24,16},{1,25},{9,1},{17,9},{25,17},{2,26},{10... | collective-permute-start | bytes 786440 | tf_op jit(solution)/shard_map/ppermute | solution.py:11
  217.4 3.4 %collective-permute-done.20 = f32[256,256]{1,0:T(8,128)S(1)} collective-permute-done((f32[256,256]{1,0:T(8,128)S(1)}, f32[256,256]{1,0:T(8,128)S(1)}, u32[]{:S(2)}, u32[]{:S(2)}) %collective-permute-start.20) | collective-permute-done | bytes 262176 | tf_op jit(solution)/shard_map/ppermute | solution.py:11
  220.9 3.8 %collective-permute-done.21 = f32[256,256]{1,0:T(8,128)S(1)} collective-permute-done((f32[256,256]{1,0:T(8,128)S(1)}, f32[256,256]{1,0:T(8,128)S(1)}, u32[]{:S(2)}, u32[]{:S(2)}) %collective-permute-start.21) | collective-permute-done | bytes 262176 | tf_op jit(solution)/shard_map/ppermute | solution.py:11
  224.7 6.4 %collective-permute-start.22 = (f32[256,256]{1,0:T(8,128)S(1)}, f32[256,256]{1,0:T(8,128)S(1)}, u32[]{:S(2)}, u32[]{:S(2)}) collective-permute-start(f32[256,256]{1,0:T(8,128)S(1)} %add_add_fusion.1), channel_id=1, source_target_pairs={{0,32},{32,0},{1,33},{33,1},{2,34},{34,2},{3,35},{35,3},{4,36},{36... | collective-permute-start | bytes 786440 | tf_op jit(solution)/shard_map/ppermute | solution.py:11
  233.6 3.8 %collective-permute-start.24 = (f32[256,256]{1,0:T(8,128)S(1)}, f32[256,256]{1,0:T(8,128)S(1)}, u32[]{:S(2)}, u32[]{:S(2)}) collective-permute-start(f32[256,256]{1,0:T(8,128)S(1)} %fusion.2), channel_id=1, source_target_pairs={{0,16},{8,24},{16,0},{24,8},{1,17},{9,25},{17,1},{25,9},{2,18},{10... | collective-permute-start | bytes 786440 | tf_op jit(solution)/shard_map/ppermute | solution.py:11
  237.4 4.0 %collective-permute-start.25 = (f32[256,256]{1,0:T(8,128)S(1)}, f32[256,256]{1,0:T(8,128)S(1)}, u32[]{:S(2)}, u32[]{:S(2)}) collective-permute-start(f32[256,256]{1,0:T(8,128)S(1)} %fusion), channel_id=1, source_target_pairs={{0,24},{8,0},{16,8},{24,16},{1,25},{9,1},{17,9},{25,17},{2,26},{10... | collective-permute-start | bytes 786440 | tf_op jit(solution)/shard_map/ppermute | solution.py:11
  241.4 7.5 %collective-permute-done.22 = f32[256,256]{1,0:T(8,128)S(1)} collective-permute-done((f32[256,256]{1,0:T(8,128)S(1)}, f32[256,256]{1,0:T(8,128)S(1)}, u32[]{:S(2)}, u32[]{:S(2)}) %collective-permute-start.22) | collective-permute-done | bytes 262176 | tf_op jit(solution)/shard_map/ppermute | solution.py:11
  (98 shorter events, 51.8 us)
Async XLA Ops:
  7.2 96.5 %all-gather.7.cloned.1.call-start = ((), (), s32[]{:S(2)}) async-start(), calls=%async_computation.1 | async-start | bytes 2621440 | tf_op jit(solution)/shard_map/all_gather | solution.py:208
  7.9 95.8 %all-gather.5.cloned.1.call-start = ((), (), s32[]{:S(2)}) async-start(), calls=%async_computation | async-start | bytes 4718592 | tf_op jit(solution)/shard_map/all_gather | solution.py:207
  8.6 176.3 %all-gather.9.cloned.1.call-start = ((), (), s32[]{:S(2)}) async-start(), calls=%async_computation.2 | async-start | bytes 9437184 | tf_op jit(solution)/shard_map/all_gather | solution.py:239
  8.7 15.8 %collective-permute-start = (f32[1024,128]{1,0:T(8,128)}, f32[1024,128]{1,0:T(8,128)S(1)}, u32[]{:S(2)}, u32[]{:S(2)}) collective-permute-start(f32[1024,128]{1,0:T(8,128)} %bitcast.74), channel_id=1, source_target_pairs={{0,64},{64,128},{128,192},{192,256},{256,320},{320,384},{384,448},... | collective-permute-start | bytes 1572872 | tf_op jit(solution)/shard_map/ppermute | solution.py:213
  12.5 16.9 %collective-permute-start.1 = (f32[1024,128]{1,0:T(8,128)}, f32[1024,128]{1,0:T(8,128)S(1)}, u32[]{:S(2)}, u32[]{:S(2)}) collective-permute-start(f32[1024,128]{1,0:T(8,128)} %bitcast.75), channel_id=1, source_target_pairs={{64,0},{128,64},{192,128},{256,192},{320,256},{384,320},{448,384},... | collective-permute-start | bytes 1572872 | tf_op jit(solution)/shard_map/ppermute | solution.py:214
  24.5 79.2 %copy-start.7 = (f32[1024,128]{1,0:T(8,128)}, f32[1024,128]{1,0:T(8,128)S(1)}, u32[]{:S(2)}) copy-start(f32[1024,128]{1,0:T(8,128)S(1)} %collective-permute-done.refs_1_) | copy-start | bytes 1572868
  29.4 74.3 %copy-start.8 = (f32[1024,128]{1,0:T(8,128)}, f32[1024,128]{1,0:T(8,128)S(1)}, u32[]{:S(2)}) copy-start(f32[1024,128]{1,0:T(8,128)S(1)} %collective-permute-done.1.refs_2_) | copy-start | bytes 1572868
  29.4 14.8 %collective-permute-start.2 = (f32[1024,128]{1,0:T(8,128)S(1)}, f32[1024,128]{1,0:T(8,128)S(1)}, u32[]{:S(2)}, u32[]{:S(2)}) collective-permute-start(f32[1024,128]{1,0:T(8,128)S(1)} %collective-permute-done.refs_1_), channel_id=1, source_target_pairs={{0,64},{64,128},{128,192},{192,256},{256,320},{320,384},{384,448},... | collective-permute-start | bytes 1572872 | tf_op jit(solution)/shard_map/ppermute | solution.py:213
  34.3 14.1 %collective-permute-start.3 = (f32[1024,128]{1,0:T(8,128)S(1)}, f32[1024,128]{1,0:T(8,128)S(1)}, u32[]{:S(2)}, u32[]{:S(2)}) collective-permute-start(f32[1024,128]{1,0:T(8,128)S(1)} %collective-permute-done.1.refs_2_), channel_id=1, source_target_pairs={{64,0},{128,64},{192,128},{256,192},{320,256},{384,320},{448,384},... | collective-permute-start | bytes 1572872 | tf_op jit(solution)/shard_map/ppermute | solution.py:214
  48.4 13.4 %collective-permute-start.4 = (f32[1024,128]{1,0:T(8,128)S(1)}, f32[1024,128]{1,0:T(8,128)}, u32[]{:S(2)}, u32[]{:S(2)}) collective-permute-start(f32[1024,128]{1,0:T(8,128)S(1)} %collective-permute-done.2.refs_3_), channel_id=1, source_target_pairs={{0,64},{64,128},{128,192},{192,256},{256,320},{320,384},{384,448},... | collective-permute-start | bytes 1572872 | tf_op jit(solution)/shard_map/ppermute | solution.py:213
  52.6 13.2 %collective-permute-start.5 = (f32[1024,128]{1,0:T(8,128)S(1)}, f32[1024,128]{1,0:T(8,128)}, u32[]{:S(2)}, u32[]{:S(2)}) collective-permute-start(f32[1024,128]{1,0:T(8,128)S(1)} %collective-permute-done.3.refs_4_), channel_id=1, source_target_pairs={{64,0},{128,64},{192,128},{256,192},{320,256},{384,320},{448,384},... | collective-permute-start | bytes 1572872 | tf_op jit(solution)/shard_map/ppermute | solution.py:214
  65.8 12.4 %collective-permute-start.6 = (f32[1024,128]{1,0:T(8,128)}, f32[1024,128]{1,0:T(8,128)S(1)}, u32[]{:S(2)}, u32[]{:S(2)}) collective-permute-start(f32[1024,128]{1,0:T(8,128)} %collective-permute-done.4.refs_5_), channel_id=1, source_target_pairs={{0,64},{64,128},{128,192},{192,256},{256,320},{320,384},{384,448},... | collective-permute-start | bytes 1572872 | tf_op jit(solution)/shard_map/ppermute | solution.py:213
  69.7 12.2 %collective-permute-start.7 = (f32[1024,128]{1,0:T(8,128)}, f32[1024,128]{1,0:T(8,128)S(1)}, u32[]{:S(2)}, u32[]{:S(2)}) collective-permute-start(f32[1024,128]{1,0:T(8,128)} %collective-permute-done.5.refs_6_), channel_id=1, source_target_pairs={{64,0},{128,64},{192,128},{256,192},{320,256},{384,320},{448,384},... | collective-permute-start | bytes 1572872 | tf_op jit(solution)/shard_map/ppermute | solution.py:214
  82.7 7.6 %collective-permute-start.10 = (f32[128,512]{1,0:T(8,128)S(1)}, f32[128,512]{1,0:T(8,128)S(1)}, u32[]{:S(2)}, u32[]{:S(2)}) collective-permute-start(f32[128,512]{1,0:T(8,128)S(1)} %get-tuple-element.48), channel_id=1, source_target_pairs={{256,448},{192,0},{257,449},{193,1},{258,450},{194,2},{259,451},{1... | collective-permute-start | bytes 786440 | tf_op jit(solution)/shard_map/ppermute | solution.py:221
  83.4 17.3 %collective-permute-start.8 = (f32[128,512]{1,0:T(8,128)S(1)}, f32[128,512]{1,0:T(8,128)S(1)}, u32[]{:S(2)}, u32[]{:S(2)}) collective-permute-start(f32[128,512]{1,0:T(8,128)S(1)} %get-tuple-element.46), channel_id=1, source_target_pairs={{256,320},{320,384},{384,448},{64,0},{128,64},{192,128},{257,321},... | collective-permute-start | bytes 786440 | tf_op jit(solution)/shard_map/ppermute | solution.py:221
  85.6 18.1 %collective-permute-start.9 = (f32[128,512]{1,0:T(8,128)S(1)}, f32[128,512]{1,0:T(8,128)}, u32[]{:S(2)}, u32[]{:S(2)}) collective-permute-start(f32[128,512]{1,0:T(8,128)S(1)} %get-tuple-element.47), channel_id=1, source_target_pairs={{256,384},{320,448},{128,0},{192,64},{257,385},{321,449},{129,1},{... | collective-permute-start | bytes 786440 | tf_op jit(solution)/shard_map/ppermute | solution.py:221
  112.1 72.9 %copy-start.1 = (f32[4,512,256]{2,1,0:T(8,128)S(1)}, f32[4,512,256]{2,1,0:T(8,128)}, u32[]{:S(2)}) copy-start(f32[4,512,256]{2,1,0:T(8,128)} %all-gather.7.cloned.1.call-done) | copy-start | bytes 6291460
  112.1 31.2 %collective-permute-start.11 = (f32[256,256]{1,0:T(8,128)S(1)}, f32[256,256]{1,0:T(8,128)S(1)}, u32[]{:S(2)}, u32[]{:S(2)}) collective-permute-start(f32[256,256]{1,0:T(8,128)S(1)} %bitcast.77), channel_id=1, source_target_pairs={{0,32},{32,0},{1,33},{33,1},{2,34},{34,2},{3,35},{35,3},{4,36},{36... | collective-permute-start | bytes 786440 | tf_op jit(solution)/shard_map/ppermute | solution.py:11
  143.3 28.0 %collective-permute-start.12 = (f32[256,256]{1,0:T(8,128)}, f32[256,256]{1,0:T(8,128)S(1)}, u32[]{:S(2)}, u32[]{:S(2)}) collective-permute-start(f32[256,256]{1,0:T(8,128)} %bitcast.11), channel_id=1, source_target_pairs={{0,32},{32,0},{1,33},{33,1},{2,34},{34,2},{3,35},{35,3},{4,36},{36... | collective-permute-start | bytes 786440 | tf_op jit(solution)/shard_map/ppermute | solution.py:11
  151.5 26.6 %collective-permute-start.16 = (f32[256,256]{1,0:T(8,128)S(1)}, f32[256,256]{1,0:T(8,128)S(1)}, u32[]{:S(2)}, u32[]{:S(2)}) collective-permute-start(f32[256,256]{1,0:T(8,128)S(1)} %collective-permute-done.11.refs_2_), channel_id=1, source_target_pairs={{0,24},{8,0},{16,8},{24,16},{1,25},{9,1},{17,9},{25,17},{2,26},{10... | collective-permute-start | bytes 786440 | tf_op jit(solution)/shard_map/ppermute | solution.py:11
  154.0 31.0 %collective-permute-start.17 = (f32[256,256]{1,0:T(8,128)S(1)}, f32[256,256]{1,0:T(8,128)S(1)}, u32[]{:S(2)}, u32[]{:S(2)}) collective-permute-start(f32[256,256]{1,0:T(8,128)S(1)} %collective-permute-done.11.refs_2_), channel_id=1, source_target_pairs={{0,16},{8,24},{16,0},{24,8},{1,17},{9,25},{17,1},{25,9},{2,18},{10... | collective-permute-start | bytes 786440 | tf_op jit(solution)/shard_map/ppermute | solution.py:11
  158.4 26.6 %collective-permute-start.18 = (f32[256,256]{1,0:T(8,128)S(1)}, f32[256,256]{1,0:T(8,128)S(1)}, u32[]{:S(2)}, u32[]{:S(2)}) collective-permute-start(f32[256,256]{1,0:T(8,128)S(1)} %collective-permute-done.11.refs_2_), channel_id=1, source_target_pairs={{0,8},{8,16},{16,24},{24,0},{1,9},{9,17},{17,25},{25,1},{2,10},{10... | collective-permute-start | bytes 786440 | tf_op jit(solution)/shard_map/ppermute | solution.py:11
  171.3 23.9 %collective-permute-start.13 = (f32[256,256]{1,0:T(8,128)S(1)}, f32[256,256]{1,0:T(8,128)}, u32[]{:S(2)}, u32[]{:S(2)}) collective-permute-start(f32[256,256]{1,0:T(8,128)S(1)} %collective-permute-done.12.refs_1_), channel_id=1, source_target_pairs={{0,24},{8,0},{16,8},{24,16},{1,25},{9,1},{17,9},{25,17},{2,26},{10... | collective-permute-start | bytes 786440 | tf_op jit(solution)/shard_map/ppermute | solution.py:11
  173.7 21.5 %collective-permute-start.14 = (f32[256,256]{1,0:T(8,128)S(1)}, f32[256,256]{1,0:T(8,128)}, u32[]{:S(2)}, u32[]{:S(2)}) collective-permute-start(f32[256,256]{1,0:T(8,128)S(1)} %collective-permute-done.12.refs_1_), channel_id=1, source_target_pairs={{0,16},{8,24},{16,0},{24,8},{1,17},{9,25},{17,1},{25,9},{2,18},{10... | collective-permute-start | bytes 786440 | tf_op jit(solution)/shard_map/ppermute | solution.py:11
  178.1 17.0 %collective-permute-start.15 = (f32[256,256]{1,0:T(8,128)S(1)}, f32[256,256]{1,0:T(8,128)}, u32[]{:S(2)}, u32[]{:S(2)}) collective-permute-start(f32[256,256]{1,0:T(8,128)S(1)} %collective-permute-done.12.refs_1_), channel_id=1, source_target_pairs={{0,8},{8,16},{16,24},{24,0},{1,9},{9,17},{17,25},{25,1},{2,10},{10... | collective-permute-start | bytes 786440 | tf_op jit(solution)/shard_map/ppermute | solution.py:11
  206.3 11.1 %collective-permute-start.19 = (f32[256,256]{1,0:T(8,128)S(1)}, f32[256,256]{1,0:T(8,128)S(1)}, u32[]{:S(2)}, u32[]{:S(2)}) collective-permute-start(f32[256,256]{1,0:T(8,128)S(1)} %fusion.12), channel_id=1, source_target_pairs={{0,8},{8,16},{16,24},{24,0},{1,9},{9,17},{17,25},{25,1},{2,10},{10... | collective-permute-start | bytes 786440 | tf_op jit(solution)/shard_map/ppermute | solution.py:11
  208.2 12.6 %collective-permute-start.20 = (f32[256,256]{1,0:T(8,128)S(1)}, f32[256,256]{1,0:T(8,128)S(1)}, u32[]{:S(2)}, u32[]{:S(2)}) collective-permute-start(f32[256,256]{1,0:T(8,128)S(1)} %fusion.10), channel_id=1, source_target_pairs={{0,16},{8,24},{16,0},{24,8},{1,17},{9,25},{17,1},{25,9},{2,18},{10... | collective-permute-start | bytes 786440 | tf_op jit(solution)/shard_map/ppermute | solution.py:11
  212.5 12.1 %collective-permute-start.21 = (f32[256,256]{1,0:T(8,128)S(1)}, f32[256,256]{1,0:T(8,128)S(1)}, u32[]{:S(2)}, u32[]{:S(2)}) collective-permute-start(f32[256,256]{1,0:T(8,128)S(1)} %fusion.8), channel_id=1, source_target_pairs={{0,24},{8,0},{16,8},{24,16},{1,25},{9,1},{17,9},{25,17},{2,26},{10... | collective-permute-start | bytes 786440 | tf_op jit(solution)/shard_map/ppermute | solution.py:11
  224.7 24.2 %collective-permute-start.22 = (f32[256,256]{1,0:T(8,128)S(1)}, f32[256,256]{1,0:T(8,128)S(1)}, u32[]{:S(2)}, u32[]{:S(2)}) collective-permute-start(f32[256,256]{1,0:T(8,128)S(1)} %add_add_fusion.1), channel_id=1, source_target_pairs={{0,32},{32,0},{1,33},{33,1},{2,34},{34,2},{3,35},{35,3},{4,36},{36... | collective-permute-start | bytes 786440 | tf_op jit(solution)/shard_map/ppermute | solution.py:11
  231.1 17.8 %collective-permute-start.23 = (f32[256,256]{1,0:T(8,128)S(1)}, f32[256,256]{1,0:T(8,128)S(1)}, u32[]{:S(2)}, u32[]{:S(2)}) collective-permute-start(f32[256,256]{1,0:T(8,128)S(1)} %fusion.4), channel_id=1, source_target_pairs={{0,8},{8,16},{16,24},{24,0},{1,9},{9,17},{17,25},{25,1},{2,10},{10... | collective-permute-start | bytes 786440 | tf_op jit(solution)/shard_map/ppermute | solution.py:11
  233.6 15.3 %collective-permute-start.24 = (f32[256,256]{1,0:T(8,128)S(1)}, f32[256,256]{1,0:T(8,128)S(1)}, u32[]{:S(2)}, u32[]{:S(2)}) collective-permute-start(f32[256,256]{1,0:T(8,128)S(1)} %fusion.2), channel_id=1, source_target_pairs={{0,16},{8,24},{16,0},{24,8},{1,17},{9,25},{17,1},{25,9},{2,18},{10... | collective-permute-start | bytes 786440 | tf_op jit(solution)/shard_map/ppermute | solution.py:11
  237.4 12.4 %collective-permute-start.25 = (f32[256,256]{1,0:T(8,128)S(1)}, f32[256,256]{1,0:T(8,128)S(1)}, u32[]{:S(2)}, u32[]{:S(2)}) collective-permute-start(f32[256,256]{1,0:T(8,128)S(1)} %fusion), channel_id=1, source_target_pairs={{0,24},{8,0},{16,8},{24,16},{1,25},{9,1},{17,9},{25,17},{2,26},{10... | collective-permute-start | bytes 786440 | tf_op jit(solution)/shard_map/ppermute | solution.py:11
  (11 other events, 236.2 us)
Sparse Core Ops, SparseCore 0:
  10.1 41.2 all-gather.6
  53.6 40.8 all-gather.4
  107.1 59.1 all-gather.8

commit v4 on v3

--- a/solution.py
+++ b/solution.py
@@ -120,9 +120,14 @@
     return high, (value - high.astype(jnp.float32)).astype(jnp.bfloat16)
 
 
-def product_kernel(terms, count, has_base, classes, *refs):
+def product_kernel(terms, count, last, classes, *refs):
     restricted, panels = refs[0], refs[1 : 1 + count]
-    out, left, right, left_sems, right_sems = refs[1 + count + has_base :]
+    if last:
+        base, lower, out, share, left, right, left_sems, right_sems, held, sem = refs[
+            1 + count :
+        ]
+    else:
+        out, left, right, left_sems, right_sems = refs[1 + count :]
 
     def copies(n):
         index, panel, start, k = terms[n]
@@ -136,13 +141,16 @@
     for n in range(len(terms)):
         for copy in copies(n):
             copy.start()
+    if last:
+        held_copy = pltpu.make_async_copy(lower, held, sem)
+        held_copy.start()
     for n in range(len(terms)):
         for copy in copies(n):
             copy.wait()
         if n > 0:
             total = out[...]
-        elif has_base:
-            total = refs[1 + count][...]
+        elif last:
+            total = base[...]
         else:
             total = jnp.zeros(out.shape, jnp.float32)
         lh, ll = two_halves(left[n])
@@ -150,35 +158,48 @@
         for one, two in ((lh, rh), (lh, rl), (ll, rh)):
             total -= jnp.dot(one, two, preferred_element_type=jnp.float32)
         out[...] = total
-
-
-def product(restricted, panels, classes, terms, base=None):
-    has_base = base is not None
-    whole = pl.BlockSpec(memory_space=pltpu.VMEM)
+    if last:
+        held_copy.wait()
+        rh, rl = two_halves(out[...])
+        for j in range(4):
+            lh, ll = two_halves(held[j])
+            total = jnp.zeros((256, 256), jnp.float32)
+            for one, two in ((lh, rh), (lh, rl), (ll, rh)):
+                total += jnp.dot(one, two, preferred_element_type=jnp.float32)
+            share[j] = total
+
+
+def product(restricted, panels, classes, terms, base=None, lower=None):
+    last = base is not None
+    whole, there = pl.BlockSpec(memory_space=pltpu.VMEM), pl.BlockSpec(memory_space=pl.ANY)
+    out_shape = [jax.ShapeDtypeStruct((512, 256), jnp.float32)]
+    scratch = [
+        pltpu.VMEM((len(terms), 512, 256), jnp.float32),
+        pltpu.VMEM((len(terms), 256, 256), jnp.float32),
+        pltpu.SemaphoreType.DMA((len(terms),)),
+        pltpu.SemaphoreType.DMA((len(terms),)),
+    ]
+    if last:
+        out_shape += [jax.ShapeDtypeStruct((4, 256, 256), jnp.float32)]
+        scratch += [pltpu.VMEM((4, 256, 512), jnp.float32), pltpu.SemaphoreType.DMA]
     return pl.pallas_call(
-        functools.partial(product_kernel, terms, len(panels), has_base),
-        out_shape=jax.ShapeDtypeStruct((512, 256), jnp.float32),
+        functools.partial(product_kernel, terms, len(panels), last),
+        out_shape=out_shape,
         grid_spec=pltpu.PrefetchScalarGridSpec(
             num_scalar_prefetch=1,
             grid=(),
-            in_specs=[pl.BlockSpec(memory_space=pl.ANY)] * (1 + len(panels))
-            + [whole] * has_base,
-            out_specs=whole,
-            scratch_shapes=[
-                pltpu.VMEM((len(terms), 512, 256), jnp.float32),
-                pltpu.VMEM((len(terms), 256, 256), jnp.float32),
-                pltpu.SemaphoreType.DMA((len(terms),)),
-                pltpu.SemaphoreType.DMA((len(terms),)),
-            ],
+            in_specs=[there] * (1 + len(panels)) + [whole, there] * last,
+            out_specs=[whole] * len(out_shape),
+            scratch_shapes=scratch,
         ),
-        compiler_params=pltpu.CompilerParams(vmem_limit_bytes=28 << 20),
+        compiler_params=pltpu.CompilerParams(vmem_limit_bytes=56 << 20),
         cost_estimate=pl.CostEstimate(
             flops=len(terms) * (3 << 26),
             bytes_accessed=len(terms) * (3 << 18),
             transcendentals=0,
         ),
         name="product",
-    )(classes, restricted, *panels, *([base] if has_base else []))
+    )(classes, restricted, *panels, *([base, lower] if last else []))
 
 
 def on_device(parent_inverse, child_blocks, factor_rows, diag_inverse):
@@ -227,15 +248,15 @@
     ]
 
     to_x = jnp.stack([(x + j) % 4 for j in range(4)])
-    block = jnp.concatenate([(1 - half) * 4 + to_x, half * 4 + to_x])
     *cut, top, bottom, lower, near = lax.optimization_barrier(
         (*cut, factor[:256], factor[256:], lower, near)
     )
 
     restricted = pick(rows, cut, source, places)
     restricted, lower = lax.optimization_barrier((restricted, lower))
-    lower = jnp.take(lower, block, axis=0, mode="clip")
-    lower, top = lax.optimization_barrier((lower, top))
+    far_lower = jnp.take(lower, (1 - half) * 4 + to_x, axis=0, mode="clip")
+    own_lower = jnp.take(lower, half * 4 + to_x, axis=0, mode="clip")
+    far_lower, top = lax.optimization_barrier((far_lower.transpose(0, 2, 1), top))
     restricted = lax.all_gather(restricted, ("y", "core"), axis=0)
     top, bottom = lax.optimization_barrier((shift(top, "zh", 2, 1), bottom))
     bottom = shift(bottom, "zh", 2, 1)
@@ -245,14 +266,16 @@
     classes = jnp.concatenate([half * 4 + number, (1 - half) * 4 + to_x]).astype(jnp.int32)
     terms = [(j, 0, 512 * j + 256 * k, k) for j in range(4) for k in (0, 1)]
     terms += [(4 + j, 1 + j, 0, 0) for j in range(4)]
-    inverse_local = product(restricted, [near] + far_top, classes, terms)
+    (inverse_local,) = product(restricted, [near] + far_top, classes, terms)
     far_bottom = [bottom] + [shift(bottom, "x", 4, j) for j in (1, 2, 3)]
     terms = [(4 + j, j, 0, 1) for j in range(4)]
-    inverse_local = product(restricted, far_bottom, classes, terms, inverse_local)
-
-    share = [dot(lower[j], inverse_local, ((0,), (0,))) for j in range(4)]
-    *share, own_lower = lax.optimization_barrier((*share, lower[4:]))
-    other_half = share[0] + sum(shift(share[j], "x", 4, -j) for j in (1, 2, 3))
+    inverse_local, share = product(
+        restricted, far_bottom, classes, terms, inverse_local, far_lower
+    )
+
+    others = [shift(share[j], "x", 4, -j) for j in (1, 2, 3)]
+    others[0], own_lower = lax.optimization_barrier((others[0], own_lower))
+    other_half = share[0] + sum(others)
     share = [dot(own_lower[j], inverse_local, ((0,), (0,))) for j in range(4)]
     other_half, *share = lax.optimization_barrier((other_half, *share))
     other_half = shift(other_half, "zh", 2, 1)

time: 258 us -> 259 us (level)
  the two profiles are of different devices: /device:TPU:66 before, /device:TPU:87 now
where the time goes in v4:
time: 259 us; the launch traced here: 258 us
  waiting for transfers between devices  116 us (45%)
  starting transfers between devices  86.5 us (33%)
  Pallas kernels  18.9 us (7%)
  local copies, waits for them, and re-layouts  16 us (6%)
  between operations  14.3 us (6%)
  other arithmetic  3.49 us (1%)
    ppermute x15, starting transfers between devices, shift(): lax.ppermute(value, axis, [(i, (i - step) % count) for i in range(count)])  57.9 us
    ppermute x15, waiting for transfers between devices, shift(): lax.ppermute(value, axis, [(i, (i - step) % count) for i in range(count)])  55.8 us
    ppermute x4, waiting for transfers between devices, on_device(): up = lax.ppermute(up, 'zl', [(i, i + 1) for i in range(7)])  27.6 us
    ppermute x4, waiting for transfers between devices, on_device(): down = lax.ppermute(down, 'zl', [(i + 1, i) for i in range(7)])  15.7 us
    ppermute x3, waiting for transfers between devices, on_device(): lax.ppermute(part, 'zl', [(i, i + d) for i in range(4, 8 - d)] + [(i, i -...  15.7 us
    ppermute x4, starting transfers between devices, on_device(): up = lax.ppermute(up, 'zl', [(i, i + 1) for i in range(7)])  15.5 us
    pallas_call x2, Pallas kernels, product(): pl.pallas_call(functools.partial(product_kernel, terms, len(panels), last...  14.8 us
    ppermute x4, starting transfers between devices, on_device(): down = lax.ppermute(down, 'zl', [(i + 1, i) for i in range(7)])  7.68 us
  transfers between devices with their start and end apart: 29, of which 16 were waited for; matrix products, arithmetic and copies ran while one was open for 6% of the time, Pallas kernels for 3%

profile of v4, /device:TPU:87, one launch (start us, length us, event | category | flops | bytes accessed | tf_op | source)
XLA Modules:
  0.0 257.8 jit_solution(17285105644111399349)
XLA Ops:
  8.7 3.5 %collective-permute-start = (f32[1024,128]{1,0:T(8,128)}, f32[1024,128]{1,0:T(8,128)S(1)}, u32[]{:S(2)}, u32[]{:S(2)}) collective-permute-start(f32[1024,128]{1,0:T(8,128)} %bitcast.76), channel_id=1, source_target_pairs={{0,64},{64,128},{128,192},{192,256},{256,320},{320,384},{384,448},... | collective-permute-start | bytes 1572872 | tf_op jit(solution)/shard_map/ppermute | solution.py:234
  14.2 9.4 %collective-permute-done.refs_1_ = f32[1024,128]{1,0:T(8,128)S(1)} collective-permute-done((f32[1024,128]{1,0:T(8,128)}, f32[1024,128]{1,0:T(8,128)S(1)}, u32[]{:S(2)}, u32[]{:S(2)}) %collective-permute-start) | collective-permute-done | bytes 524320 | tf_op jit(solution)/shard_map/ppermute | solution.py:234
  23.6 4.9 %collective-permute-done.1.refs_2_ = f32[1024,128]{1,0:T(8,128)S(1)} collective-permute-done((f32[1024,128]{1,0:T(8,128)}, f32[1024,128]{1,0:T(8,128)S(1)}, u32[]{:S(2)}, u32[]{:S(2)}) %collective-permute-start.1) | collective-permute-done | bytes 524320 | tf_op jit(solution)/shard_map/ppermute | solution.py:235
  28.6 4.2 %collective-permute-start.2 = (f32[1024,128]{1,0:T(8,128)S(1)}, f32[1024,128]{1,0:T(8,128)S(1)}, u32[]{:S(2)}, u32[]{:S(2)}) collective-permute-start(f32[1024,128]{1,0:T(8,128)S(1)} %collective-permute-done.refs_1_), channel_id=1, source_target_pairs={{0,64},{64,128},{128,192},{192,256},{256,320},{320,384},{384,448},... | collective-permute-start | bytes 1572872 | tf_op jit(solution)/shard_map/ppermute | solution.py:234
  35.8 6.6 %collective-permute-done.2.refs_3_ = f32[1024,128]{1,0:T(8,128)S(1)} collective-permute-done((f32[1024,128]{1,0:T(8,128)S(1)}, f32[1024,128]{1,0:T(8,128)S(1)}, u32[]{:S(2)}, u32[]{:S(2)}) %collective-permute-start.2) | collective-permute-done | bytes 524320 | tf_op jit(solution)/shard_map/ppermute | solution.py:234
  42.4 3.7 %collective-permute-done.3.refs_4_ = f32[1024,128]{1,0:T(8,128)S(1)} collective-permute-done((f32[1024,128]{1,0:T(8,128)S(1)}, f32[1024,128]{1,0:T(8,128)S(1)}, u32[]{:S(2)}, u32[]{:S(2)}) %collective-permute-start.3) | collective-permute-done | bytes 524320 | tf_op jit(solution)/shard_map/ppermute | solution.py:235
  46.1 4.1 %collective-permute-start.4 = (f32[1024,128]{1,0:T(8,128)S(1)}, f32[1024,128]{1,0:T(8,128)}, u32[]{:S(2)}, u32[]{:S(2)}) collective-permute-start(f32[1024,128]{1,0:T(8,128)S(1)} %collective-permute-done.2.refs_3_), channel_id=1, source_target_pairs={{0,64},{64,128},{128,192},{192,256},{256,320},{320,384},{384,448},... | collective-permute-start | bytes 1572872 | tf_op jit(solution)/shard_map/ppermute | solution.py:234
  53.0 5.7 %collective-permute-done.4.refs_5_ = f32[1024,128]{1,0:T(8,128)} collective-permute-done((f32[1024,128]{1,0:T(8,128)S(1)}, f32[1024,128]{1,0:T(8,128)}, u32[]{:S(2)}, u32[]{:S(2)}) %collective-permute-start.4) | collective-permute-done | bytes 524320 | tf_op jit(solution)/shard_map/ppermute | solution.py:234
  58.7 3.8 %collective-permute-done.5.refs_6_ = f32[1024,128]{1,0:T(8,128)S(1)} collective-permute-done((f32[1024,128]{1,0:T(8,128)S(1)}, f32[1024,128]{1,0:T(8,128)S(1)}, u32[]{:S(2)}, u32[]{:S(2)}) %collective-permute-start.5) | collective-permute-done | bytes 524320 | tf_op jit(solution)/shard_map/ppermute | solution.py:235
  63.3 3.5 %collective-permute-start.6 = (f32[1024,128]{1,0:T(8,128)}, f32[1024,128]{1,0:T(8,128)S(1)}, u32[]{:S(2)}, u32[]{:S(2)}) collective-permute-start(f32[1024,128]{1,0:T(8,128)} %collective-permute-done.4.refs_5_), channel_id=1, source_target_pairs={{0,64},{64,128},{128,192},{192,256},{256,320},{320,384},{384,448},... | collective-permute-start | bytes 1572872 | tf_op jit(solution)/shard_map/ppermute | solution.py:234
  69.0 5.9 %collective-permute-done.6.up.refs_7_ = f32[1024,128]{1,0:T(8,128)S(1)} collective-permute-done((f32[1024,128]{1,0:T(8,128)}, f32[1024,128]{1,0:T(8,128)S(1)}, u32[]{:S(2)}, u32[]{:S(2)}) %collective-permute-start.6) | collective-permute-done | bytes 524320 | tf_op jit(solution)/shard_map/ppermute | solution.py:234
  75.0 3.3 %collective-permute-done.7.down.refs_8_ = f32[1024,128]{1,0:T(8,128)S(1)} collective-permute-done((f32[1024,128]{1,0:T(8,128)}, f32[1024,128]{1,0:T(8,128)S(1)}, u32[]{:S(2)}, u32[]{:S(2)}) %collective-permute-start.7) | collective-permute-done | bytes 524320 | tf_op jit(solution)/shard_map/ppermute | solution.py:235
  85.9 3.8 %collective-permute-done.8.refs_9_ = f32[128,512]{1,0:T(8,128)S(1)} collective-permute-done((f32[128,512]{1,0:T(8,128)S(1)}, f32[128,512]{1,0:T(8,128)S(1)}, u32[]{:S(2)}, u32[]{:S(2)}) %collective-permute-start.8) | collective-permute-done | bytes 262176 | tf_op jit(solution)/shard_map/ppermute | solution.py:242
  90.4 11.9 %collective-permute-done.9.refs_10_ = f32[128,512]{1,0:T(8,128)} collective-permute-done((f32[128,512]{1,0:T(8,128)S(1)}, f32[128,512]{1,0:T(8,128)}, u32[]{:S(2)}, u32[]{:S(2)}) %collective-permute-start.9) | collective-permute-done | bytes 262176 | tf_op jit(solution)/shard_map/ppermute | solution.py:242
  102.3 3.3 %pick.1 = f32[2,512,256]{2,1,0:T(8,128)} custom-call(s32[20]{0:T(128)} %pad_add_fusion.1.info, f32[1024,128]{1,0:T(8,128)} %bitcast.78, f32[1024,128]{1,0:T(8,128)} %copy-done.4, f32[1024,128]{1,0:T(8,128)} %copy-done.5, f32[1024,128]{1,0:T(8,128)} %copy-done.6, f32[1024,128]{1,0:T(8,128)} %copy-done.7, f32[1024,128]{1,0:T(8,128)} %collective-permute-done.4.refs_5_, ...), custom_call_target="tpu_custom_call" | custom-call | bytes 3145728 | tf_op jit(solution)/shard_map/pick/pallas_call | solution.py:98
  105.7 2.9 %gather_fusion.1 = f32[4,512,256]{2,1,0:T(8,128)S(1)} fusion(f32[8,512,256]{2,1,0:T(8,128)} %all-gather.5.cloned.1.call-done, s32[1024]{0:T(1024)S(1)} %pad_clamp_fusion.1), kind=kCustom, calls=%fused_computation.1 | custom fusion | bytes 4194320 | tf_op jit(solution)/shard_map/jit(_take)/gather | solution.py:257
  110.4 9.9 %collective-permute-start.11 = (f32[256,256]{1,0:T(8,128)S(1)}, f32[256,256]{1,0:T(8,128)S(1)}, u32[]{:S(2)}, u32[]{:S(2)}) collective-permute-start(f32[256,256]{1,0:T(8,128)S(1)} %bitcast.80), channel_id=1, source_target_pairs={{0,32},{32,0},{1,33},{33,1},{2,34},{34,2},{3,35},{35,3},{4,36},{36... | collective-permute-start | bytes 786440 | tf_op jit(solution)/shard_map/ppermute | solution.py:11
  120.4 22.6 %collective-permute-done.11.refs_2_ = f32[256,256]{1,0:T(8,128)S(1)} collective-permute-done((f32[256,256]{1,0:T(8,128)S(1)}, f32[256,256]{1,0:T(8,128)S(1)}, u32[]{:S(2)}, u32[]{:S(2)}) %collective-permute-start.11) | collective-permute-done | bytes 262176 | tf_op jit(solution)/shard_map/ppermute | solution.py:11
  143.0 6.3 %collective-permute-start.12 = (f32[256,256]{1,0:T(8,128)S(1)}, f32[256,256]{1,0:T(8,128)S(1)}, u32[]{:S(2)}, u32[]{:S(2)}) collective-permute-start(f32[256,256]{1,0:T(8,128)S(1)} %bitcast.79), channel_id=1, source_target_pairs={{0,32},{32,0},{1,33},{33,1},{2,34},{34,2},{3,35},{35,3},{4,36},{36... | collective-permute-start | bytes 786440 | tf_op jit(solution)/shard_map/ppermute | solution.py:11
  149.3 2.7 %collective-permute-start.16 = (f32[256,256]{1,0:T(8,128)S(1)}, f32[256,256]{1,0:T(8,128)S(1)}, u32[]{:S(2)}, u32[]{:S(2)}) collective-permute-start(f32[256,256]{1,0:T(8,128)S(1)} %collective-permute-done.11.refs_2_), channel_id=1, source_target_pairs={{0,24},{8,0},{16,8},{24,16},{1,25},{9,1},{17,9},{25,17},{2,26},{10... | collective-permute-start | bytes 786440 | tf_op jit(solution)/shard_map/ppermute | solution.py:11
  154.6 3.7 %collective-permute-start.18 = (f32[256,256]{1,0:T(8,128)S(1)}, f32[256,256]{1,0:T(8,128)S(1)}, u32[]{:S(2)}, u32[]{:S(2)}) collective-permute-start(f32[256,256]{1,0:T(8,128)S(1)} %collective-permute-done.11.refs_2_), channel_id=1, source_target_pairs={{0,8},{8,16},{16,24},{24,0},{1,9},{9,17},{17,25},{25,1},{2,10},{10... | collective-permute-start | bytes 786440 | tf_op jit(solution)/shard_map/ppermute | solution.py:11
  158.4 11.1 %collective-permute-done.12.refs_1_ = f32[256,256]{1,0:T(8,128)S(1)} collective-permute-done((f32[256,256]{1,0:T(8,128)S(1)}, f32[256,256]{1,0:T(8,128)S(1)}, u32[]{:S(2)}, u32[]{:S(2)}) %collective-permute-start.12) | collective-permute-done | bytes 262176 | tf_op jit(solution)/shard_map/ppermute | solution.py:11
  174.8 3.7 %collective-permute-start.15 = (f32[256,256]{1,0:T(8,128)S(1)}, f32[256,256]{1,0:T(8,128)S(1)}, u32[]{:S(2)}, u32[]{:S(2)}) collective-permute-start(f32[256,256]{1,0:T(8,128)S(1)} %collective-permute-done.12.refs_1_), channel_id=1, source_target_pairs={{0,8},{8,16},{16,24},{24,0},{1,9},{9,17},{17,25},{25,1},{2,10},{10... | collective-permute-start | bytes 786440 | tf_op jit(solution)/shard_map/ppermute | solution.py:11
  179.9 8.1 %product.2.refs_5_ = f32[512,256]{1,0:T(8,128)} custom-call(s32[8]{0:T(128)} %pad_add_fusion.classes, f32[8,2,512,256]{3,2,1,0:T(8,128)} %bitcast.69, f32[2048,256]{1,0:T(8,128)} %bitcast.75, f32[256,256]{1,0:T(8,128)} %copy-done.11, f32[256,256]{1,0:T(8,128)} %copy-done.12, f32[256,256]{1,0:T(8,128)} %copy-done.13, f32[256,256]{1,0:T(8,128)} %copy-done.14), custom_call_target="tpu_custom_call" | custom-call | flops 2415919104 | bytes 9437184 | tf_op jit(solution)/shard_map/product/pallas_call | solution.py:185
  189.6 6.6 %product.3 = (f32[512,256]{1,0:T(8,128)}, f32[4,256,256]{2,1,0:T(8,128)}) custom-call(s32[8]{0:T(128)} %pad_add_fusion.classes, f32[8,2,512,256]{3,2,1,0:T(8,128)} %bitcast.70, f32[256,256]{1,0:T(8,128)} %copy-done.10, f32[256,256]{1,0:T(8,128)} %copy-done.15, f32[256,256]{1,0:T(8,128)} %copy-done.16, f32[256,256]{1,0:T(8,128)} %copy-done.17, ...), custom_call_target="tpu_custom_call" | custom-call | flops 805306368 | bytes 3145728 | tf_op jit(solution)/shard_map/product/pallas_call | solution.py:185
  198.1 4.3 %collective-permute-start.19 = (f32[256,256]{1,0:T(8,128)}, f32[256,256]{1,0:T(8,128)S(1)}, u32[]{:S(2)}, u32[]{:S(2)}) collective-permute-start(f32[256,256]{1,0:T(8,128)} %get-tuple-element.82), channel_id=1, source_target_pairs={{0,8},{8,16},{16,24},{24,0},{1,9},{9,17},{17,25},{25,1},{2,10},{10... | collective-permute-start | bytes 786440 | tf_op jit(solution)/shard_map/ppermute | solution.py:11
  202.5 2.9 %gather_fusion.2 = f32[4,512,256]{2,1,0:T(8,128)S(1)} fusion(f32[8,512,256]{2,1,0:T(8,128)} %all-gather.5.cloned.1.call-done, s32[1024]{0:T(1024)S(1)} %pad_clamp_fusion), kind=kCustom, calls=%fused_computation.2 | custom fusion | bytes 4194320 | tf_op jit(solution)/shard_map/jit(_take)/gather | solution.py:258
  212.5 3.5 %collective-permute-done.20 = f32[256,256]{1,0:T(8,128)S(1)} collective-permute-done((f32[256,256]{1,0:T(8,128)S(1)}, f32[256,256]{1,0:T(8,128)S(1)}, u32[]{:S(2)}, u32[]{:S(2)}) %collective-permute-start.20) | collective-permute-done | bytes 262176 | tf_op jit(solution)/shard_map/ppermute | solution.py:11
  215.9 6.7 %collective-permute-done.21 = f32[256,256]{1,0:T(8,128)S(1)} collective-permute-done((f32[256,256]{1,0:T(8,128)S(1)}, f32[256,256]{1,0:T(8,128)S(1)}, u32[]{:S(2)}, u32[]{:S(2)}) %collective-permute-start.21) | collective-permute-done | bytes 262176 | tf_op jit(solution)/shard_map/ppermute | solution.py:11
  223.7 7.6 %collective-permute-start.22 = (f32[256,256]{1,0:T(8,128)S(1)}, f32[256,256]{1,0:T(8,128)S(1)}, u32[]{:S(2)}, u32[]{:S(2)}) collective-permute-start(f32[256,256]{1,0:T(8,128)S(1)} %bitcast_add_fusion), channel_id=1, source_target_pairs={{0,32},{32,0},{1,33},{33,1},{2,34},{34,2},{3,35},{35,3},{4,36},{36... | collective-permute-start | bytes 786440 | tf_op jit(solution)/shard_map/ppermute | solution.py:11
  235.1 3.4 %collective-permute-start.25 = (f32[256,256]{1,0:T(8,128)S(1)}, f32[256,256]{1,0:T(8,128)S(1)}, u32[]{:S(2)}, u32[]{:S(2)}) collective-permute-start(f32[256,256]{1,0:T(8,128)S(1)} %fusion), channel_id=1, source_target_pairs={{0,24},{8,0},{16,8},{24,16},{1,25},{9,1},{17,9},{25,17},{2,26},{10... | collective-permute-start | bytes 786440 | tf_op jit(solution)/shard_map/ppermute | solution.py:11
  238.5 9.7 %collective-permute-done.22 = f32[256,256]{1,0:T(8,128)S(1)} collective-permute-done((f32[256,256]{1,0:T(8,128)S(1)}, f32[256,256]{1,0:T(8,128)S(1)}, u32[]{:S(2)}, u32[]{:S(2)}) %collective-permute-start.22) | collective-permute-done | bytes 262176 | tf_op jit(solution)/shard_map/ppermute | solution.py:11
  (112 shorter events, 49.7 us)
Async XLA Ops:
  7.2 77.9 %copy-start.3 = (f32[1,4,1,128,256]{4,3,2,1,0:T(8,128)S(1)}, f32[1,4,1,128,256]{4,3,2,1,0:T(8,128)}, u32[]{:S(2)}) copy-start(f32[1,4,1,128,256]{4,3,2,1,0:T(8,128)} %param.6) | copy-start | bytes 1572868
  7.2 95.1 %all-gather.7.cloned.1.call-start = ((), (), s32[]{:S(2)}) async-start(), calls=%async_computation.1 | async-start | bytes 2621440 | tf_op jit(solution)/shard_map/all_gather | solution.py:229
  7.9 94.3 %all-gather.5.cloned.1.call-start = ((), (), s32[]{:S(2)}) async-start(), calls=%async_computation | async-start | bytes 4718592 | tf_op jit(solution)/shard_map/all_gather | solution.py:228
  8.7 170.5 %all-gather.9.cloned.1.call-start = ((), (), s32[]{:S(2)}) async-start(), calls=%async_computation.2 | async-start | bytes 9437184 | tf_op jit(solution)/shard_map/all_gather | solution.py:260
  8.7 14.9 %collective-permute-start = (f32[1024,128]{1,0:T(8,128)}, f32[1024,128]{1,0:T(8,128)S(1)}, u32[]{:S(2)}, u32[]{:S(2)}) collective-permute-start(f32[1024,128]{1,0:T(8,128)} %bitcast.76), channel_id=1, source_target_pairs={{0,64},{64,128},{128,192},{192,256},{256,320},{320,384},{384,448},... | collective-permute-start | bytes 1572872 | tf_op jit(solution)/shard_map/ppermute | solution.py:234
  12.3 16.3 %collective-permute-start.1 = (f32[1024,128]{1,0:T(8,128)}, f32[1024,128]{1,0:T(8,128)S(1)}, u32[]{:S(2)}, u32[]{:S(2)}) collective-permute-start(f32[1024,128]{1,0:T(8,128)} %bitcast.77), channel_id=1, source_target_pairs={{64,0},{128,64},{192,128},{256,192},{320,256},{384,320},{448,384},... | collective-permute-start | bytes 1572872 | tf_op jit(solution)/shard_map/ppermute | solution.py:235
  23.6 78.6 %copy-start.4 = (f32[1024,128]{1,0:T(8,128)}, f32[1024,128]{1,0:T(8,128)S(1)}, u32[]{:S(2)}) copy-start(f32[1024,128]{1,0:T(8,128)S(1)} %collective-permute-done.refs_1_) | copy-start | bytes 1572868
  28.6 73.7 %copy-start.5 = (f32[1024,128]{1,0:T(8,128)}, f32[1024,128]{1,0:T(8,128)S(1)}, u32[]{:S(2)}) copy-start(f32[1024,128]{1,0:T(8,128)S(1)} %collective-permute-done.1.refs_2_) | copy-start | bytes 1572868
  28.6 13.9 %collective-permute-start.2 = (f32[1024,128]{1,0:T(8,128)S(1)}, f32[1024,128]{1,0:T(8,128)S(1)}, u32[]{:S(2)}, u32[]{:S(2)}) collective-permute-start(f32[1024,128]{1,0:T(8,128)S(1)} %collective-permute-done.refs_1_), channel_id=1, source_target_pairs={{0,64},{64,128},{128,192},{192,256},{256,320},{320,384},{384,448},... | collective-permute-start | bytes 1572872 | tf_op jit(solution)/shard_map/ppermute | solution.py:234
  32.8 13.3 %collective-permute-start.3 = (f32[1024,128]{1,0:T(8,128)S(1)}, f32[1024,128]{1,0:T(8,128)S(1)}, u32[]{:S(2)}, u32[]{:S(2)}) collective-permute-start(f32[1024,128]{1,0:T(8,128)S(1)} %collective-permute-done.1.refs_2_), channel_id=1, source_target_pairs={{64,0},{128,64},{192,128},{256,192},{320,256},{384,320},{448,384},... | collective-permute-start | bytes 1572872 | tf_op jit(solution)/shard_map/ppermute | solution.py:235
  46.1 12.6 %collective-permute-start.4 = (f32[1024,128]{1,0:T(8,128)S(1)}, f32[1024,128]{1,0:T(8,128)}, u32[]{:S(2)}, u32[]{:S(2)}) collective-permute-start(f32[1024,128]{1,0:T(8,128)S(1)} %collective-permute-done.2.refs_3_), channel_id=1, source_target_pairs={{0,64},{64,128},{128,192},{192,256},{256,320},{320,384},{384,448},... | collective-permute-start | bytes 1572872 | tf_op jit(solution)/shard_map/ppermute | solution.py:234
  50.2 12.3 %collective-permute-start.5 = (f32[1024,128]{1,0:T(8,128)S(1)}, f32[1024,128]{1,0:T(8,128)S(1)}, u32[]{:S(2)}, u32[]{:S(2)}) collective-permute-start(f32[1024,128]{1,0:T(8,128)S(1)} %collective-permute-done.3.refs_4_), channel_id=1, source_target_pairs={{64,0},{128,64},{192,128},{256,192},{320,256},{384,320},{448,384},... | collective-permute-start | bytes 1572872 | tf_op jit(solution)/shard_map/ppermute | solution.py:235
  63.3 11.7 %collective-permute-start.6 = (f32[1024,128]{1,0:T(8,128)}, f32[1024,128]{1,0:T(8,128)S(1)}, u32[]{:S(2)}, u32[]{:S(2)}) collective-permute-start(f32[1024,128]{1,0:T(8,128)} %collective-permute-done.4.refs_5_), channel_id=1, source_target_pairs={{0,64},{64,128},{128,192},{192,256},{256,320},{320,384},{384,448},... | collective-permute-start | bytes 1572872 | tf_op jit(solution)/shard_map/ppermute | solution.py:234
  66.9 11.4 %collective-permute-start.7 = (f32[1024,128]{1,0:T(8,128)}, f32[1024,128]{1,0:T(8,128)S(1)}, u32[]{:S(2)}, u32[]{:S(2)}) collective-permute-start(f32[1024,128]{1,0:T(8,128)} %copy-done.8), channel_id=1, source_target_pairs={{64,0},{128,64},{192,128},{256,192},{320,256},{384,320},{448,384},... | collective-permute-start | bytes 1572872 | tf_op jit(solution)/shard_map/ppermute | solution.py:235
  79.1 6.8 %collective-permute-start.10 = (f32[128,512]{1,0:T(8,128)S(1)}, f32[128,512]{1,0:T(8,128)S(1)}, u32[]{:S(2)}, u32[]{:S(2)}) collective-permute-start(f32[128,512]{1,0:T(8,128)S(1)} %get-tuple-element.47), channel_id=1, source_target_pairs={{256,448},{192,0},{257,449},{193,1},{258,450},{194,2},{259,451},{1... | collective-permute-start | bytes 786440 | tf_op jit(solution)/shard_map/ppermute | solution.py:242
  79.8 9.9 %collective-permute-start.8 = (f32[128,512]{1,0:T(8,128)S(1)}, f32[128,512]{1,0:T(8,128)S(1)}, u32[]{:S(2)}, u32[]{:S(2)}) collective-permute-start(f32[128,512]{1,0:T(8,128)S(1)} %get-tuple-element.45), channel_id=1, source_target_pairs={{256,320},{320,384},{384,448},{64,0},{128,64},{192,128},{257,321},... | collective-permute-start | bytes 786440 | tf_op jit(solution)/shard_map/ppermute | solution.py:242
  81.9 20.4 %collective-permute-start.9 = (f32[128,512]{1,0:T(8,128)S(1)}, f32[128,512]{1,0:T(8,128)}, u32[]{:S(2)}, u32[]{:S(2)}) collective-permute-start(f32[128,512]{1,0:T(8,128)S(1)} %get-tuple-element.46), channel_id=1, source_target_pairs={{256,384},{320,448},{128,0},{192,64},{257,385},{321,449},{129,1},{... | collective-permute-start | bytes 786440 | tf_op jit(solution)/shard_map/ppermute | solution.py:242
  110.4 32.6 %collective-permute-start.11 = (f32[256,256]{1,0:T(8,128)S(1)}, f32[256,256]{1,0:T(8,128)S(1)}, u32[]{:S(2)}, u32[]{:S(2)}) collective-permute-start(f32[256,256]{1,0:T(8,128)S(1)} %bitcast.80), channel_id=1, source_target_pairs={{0,32},{32,0},{1,33},{33,1},{2,34},{34,2},{3,35},{35,3},{4,36},{36... | collective-permute-start | bytes 786440 | tf_op jit(solution)/shard_map/ppermute | solution.py:11
  143.0 26.5 %collective-permute-start.12 = (f32[256,256]{1,0:T(8,128)S(1)}, f32[256,256]{1,0:T(8,128)S(1)}, u32[]{:S(2)}, u32[]{:S(2)}) collective-permute-start(f32[256,256]{1,0:T(8,128)S(1)} %bitcast.79), channel_id=1, source_target_pairs={{0,32},{32,0},{1,33},{33,1},{2,34},{34,2},{3,35},{35,3},{4,36},{36... | collective-permute-start | bytes 786440 | tf_op jit(solution)/shard_map/ppermute | solution.py:11
  149.3 25.5 %collective-permute-start.16 = (f32[256,256]{1,0:T(8,128)S(1)}, f32[256,256]{1,0:T(8,128)S(1)}, u32[]{:S(2)}, u32[]{:S(2)}) collective-permute-start(f32[256,256]{1,0:T(8,128)S(1)} %collective-permute-done.11.refs_2_), channel_id=1, source_target_pairs={{0,24},{8,0},{16,8},{24,16},{1,25},{9,1},{17,9},{25,17},{2,26},{10... | collective-permute-start | bytes 786440 | tf_op jit(solution)/shard_map/ppermute | solution.py:11
  152.1 27.0 %collective-permute-start.17 = (f32[256,256]{1,0:T(8,128)S(1)}, f32[256,256]{1,0:T(8,128)S(1)}, u32[]{:S(2)}, u32[]{:S(2)}) collective-permute-start(f32[256,256]{1,0:T(8,128)S(1)} %collective-permute-done.11.refs_2_), channel_id=1, source_target_pairs={{0,16},{8,24},{16,0},{24,8},{1,17},{9,25},{17,1},{25,9},{2,18},{10... | collective-permute-start | bytes 786440 | tf_op jit(solution)/shard_map/ppermute | solution.py:11
  154.6 24.5 %collective-permute-start.18 = (f32[256,256]{1,0:T(8,128)S(1)}, f32[256,256]{1,0:T(8,128)S(1)}, u32[]{:S(2)}, u32[]{:S(2)}) collective-permute-start(f32[256,256]{1,0:T(8,128)S(1)} %collective-permute-done.11.refs_2_), channel_id=1, source_target_pairs={{0,8},{8,16},{16,24},{24,0},{1,9},{9,17},{17,25},{25,1},{2,10},{10... | collective-permute-start | bytes 786440 | tf_op jit(solution)/shard_map/ppermute | solution.py:11
  169.5 18.6 %collective-permute-start.13 = (f32[256,256]{1,0:T(8,128)S(1)}, f32[256,256]{1,0:T(8,128)S(1)}, u32[]{:S(2)}, u32[]{:S(2)}) collective-permute-start(f32[256,256]{1,0:T(8,128)S(1)} %collective-permute-done.12.refs_1_), channel_id=1, source_target_pairs={{0,24},{8,0},{16,8},{24,16},{1,25},{9,1},{17,9},{25,17},{2,26},{10... | collective-permute-start | bytes 786440 | tf_op jit(solution)/shard_map/ppermute | solution.py:11
  172.2 15.8 %collective-permute-start.14 = (f32[256,256]{1,0:T(8,128)S(1)}, f32[256,256]{1,0:T(8,128)S(1)}, u32[]{:S(2)}, u32[]{:S(2)}) collective-permute-start(f32[256,256]{1,0:T(8,128)S(1)} %collective-permute-done.12.refs_1_), channel_id=1, source_target_pairs={{0,16},{8,24},{16,0},{24,8},{1,17},{9,25},{17,1},{25,9},{2,18},{10... | collective-permute-start | bytes 786440 | tf_op jit(solution)/shard_map/ppermute | solution.py:11
  174.8 13.3 %collective-permute-start.15 = (f32[256,256]{1,0:T(8,128)S(1)}, f32[256,256]{1,0:T(8,128)S(1)}, u32[]{:S(2)}, u32[]{:S(2)}) collective-permute-start(f32[256,256]{1,0:T(8,128)S(1)} %collective-permute-done.12.refs_1_), channel_id=1, source_target_pairs={{0,8},{8,16},{16,24},{24,0},{1,9},{9,17},{17,25},{25,1},{2,10},{10... | collective-permute-start | bytes 786440 | tf_op jit(solution)/shard_map/ppermute | solution.py:11
  198.1 11.9 %collective-permute-start.19 = (f32[256,256]{1,0:T(8,128)}, f32[256,256]{1,0:T(8,128)S(1)}, u32[]{:S(2)}, u32[]{:S(2)}) collective-permute-start(f32[256,256]{1,0:T(8,128)} %get-tuple-element.82), channel_id=1, source_target_pairs={{0,8},{8,16},{16,24},{24,0},{1,9},{9,17},{17,25},{25,1},{2,10},{10... | collective-permute-start | bytes 786440 | tf_op jit(solution)/shard_map/ppermute | solution.py:11
  205.4 10.5 %collective-permute-start.20 = (f32[256,256]{1,0:T(8,128)S(1)}, f32[256,256]{1,0:T(8,128)S(1)}, u32[]{:S(2)}, u32[]{:S(2)}) collective-permute-start(f32[256,256]{1,0:T(8,128)S(1)} %get-tuple-element.80), channel_id=1, source_target_pairs={{0,16},{8,24},{16,0},{24,8},{1,17},{9,25},{17,1},{25,9},{2,18},{10... | collective-permute-start | bytes 786440 | tf_op jit(solution)/shard_map/ppermute | solution.py:11
  207.4 15.3 %collective-permute-start.21 = (f32[256,256]{1,0:T(8,128)S(1)}, f32[256,256]{1,0:T(8,128)S(1)}, u32[]{:S(2)}, u32[]{:S(2)}) collective-permute-start(f32[256,256]{1,0:T(8,128)S(1)} %get-tuple-element.81), channel_id=1, source_target_pairs={{0,24},{8,0},{16,8},{24,16},{1,25},{9,1},{17,9},{25,17},{2,26},{10... | collective-permute-start | bytes 786440 | tf_op jit(solution)/shard_map/ppermute | solution.py:11
  223.7 24.6 %collective-permute-start.22 = (f32[256,256]{1,0:T(8,128)S(1)}, f32[256,256]{1,0:T(8,128)S(1)}, u32[]{:S(2)}, u32[]{:S(2)}) collective-permute-start(f32[256,256]{1,0:T(8,128)S(1)} %bitcast_add_fusion), channel_id=1, source_target_pairs={{0,32},{32,0},{1,33},{33,1},{2,34},{34,2},{3,35},{35,3},{4,36},{36... | collective-permute-start | bytes 786440 | tf_op jit(solution)/shard_map/ppermute | solution.py:11
  231.3 17.0 %collective-permute-start.23 = (f32[256,256]{1,0:T(8,128)S(1)}, f32[256,256]{1,0:T(8,128)S(1)}, u32[]{:S(2)}, u32[]{:S(2)}) collective-permute-start(f32[256,256]{1,0:T(8,128)S(1)} %fusion.4), channel_id=1, source_target_pairs={{0,8},{8,16},{16,24},{24,0},{1,9},{9,17},{17,25},{25,1},{2,10},{10... | collective-permute-start | bytes 786440 | tf_op jit(solution)/shard_map/ppermute | solution.py:11
  233.2 15.1 %collective-permute-start.24 = (f32[256,256]{1,0:T(8,128)S(1)}, f32[256,256]{1,0:T(8,128)S(1)}, u32[]{:S(2)}, u32[]{:S(2)}) collective-permute-start(f32[256,256]{1,0:T(8,128)S(1)} %fusion.2), channel_id=1, source_target_pairs={{0,16},{8,24},{16,0},{24,8},{1,17},{9,25},{17,1},{25,9},{2,18},{10... | collective-permute-start | bytes 786440 | tf_op jit(solution)/shard_map/ppermute | solution.py:11
  235.1 15.3 %collective-permute-start.25 = (f32[256,256]{1,0:T(8,128)S(1)}, f32[256,256]{1,0:T(8,128)S(1)}, u32[]{:S(2)}, u32[]{:S(2)}) collective-permute-start(f32[256,256]{1,0:T(8,128)S(1)} %fusion), channel_id=1, source_target_pairs={{0,24},{8,0},{16,8},{24,16},{1,25},{9,1},{17,9},{25,17},{2,26},{10... | collective-permute-start | bytes 786440 | tf_op jit(solution)/shard_map/ppermute | solution.py:11
  (18 other events, 238.2 us)
Sparse Core Ops, SparseCore 0:
  10.1 40.1 all-gather.6
  52.4 40.8 all-gather.4
  105.7 60.4 all-gather.8

commit v5 on v3

--- a/solution.py
+++ b/solution.py
@@ -120,65 +120,143 @@
     return high, (value - high.astype(jnp.float32)).astype(jnp.bfloat16)
 
 
-def product_kernel(terms, count, has_base, classes, *refs):
-    restricted, panels = refs[0], refs[1 : 1 + count]
-    out, left, right, left_sems, right_sems = refs[1 + count + has_base :]
+def halve_kernel(lower, near, lower_high, lower_low, near_high, near_low):
+    lower_high[...], lower_low[...] = two_halves(lower[...])
+    near_high[...], near_low[...] = two_halves(-near[...])
+
+
+def halve(*values):
+    whole = pl.BlockSpec(memory_space=pltpu.VMEM)
+    return pl.pallas_call(
+        halve_kernel,
+        out_shape=[
+            jax.ShapeDtypeStruct(value.shape, jnp.bfloat16) for value in values for _ in (0, 1)
+        ],
+        in_specs=[whole] * len(values),
+        out_specs=[whole] * (2 * len(values)),
+        compiler_params=pltpu.CompilerParams(vmem_limit_bytes=32 << 20),
+        cost_estimate=pl.CostEstimate(flops=0, bytes_accessed=8 << 20, transcendentals=0),
+        name="halve",
+    )(*values)
+
+
+def add_product(total, left, right):
+    for one, two in ((left[0], right[0]), (left[0], right[1]), (left[1], right[0])):
+        total += jnp.dot(one, two, preferred_element_type=jnp.float32)
+    return total
+
+
+def near_kernel(classes, *refs):
+    restricted, high, low, panels = refs[0], refs[1], refs[2], refs[3:7]
+    out, left, right_high, right_low, right, left_sems, sems, low_sems = refs[7:]
 
     def copies(n):
-        index, panel, start, k = terms[n]
-        yield pltpu.make_async_copy(
-            restricted.at[classes[index], k], left.at[n], left_sems.at[n]
-        )
-        yield pltpu.make_async_copy(
-            panels[panel].at[pl.ds(start, 256)], right.at[n], right_sems.at[n]
-        )
-
-    for n in range(len(terms)):
+        piece = restricted.at[classes[n // 2 if n < 8 else n - 4], n % 2 if n < 8 else 0]
+        yield pltpu.make_async_copy(piece, left.at[n], left_sems.at[n])
+        if n < 8:
+            rows = pl.ds(256 * n, 256)
+            yield pltpu.make_async_copy(high.at[rows], right_high.at[n], sems.at[n])
+            yield pltpu.make_async_copy(low.at[rows], right_low.at[n], low_sems.at[n])
+        else:
+            yield pltpu.make_async_copy(panels[n - 8], right.at[n - 8], sems.at[n])
+
+    for n in range(12):
         for copy in copies(n):
             copy.start()
-    for n in range(len(terms)):
+    for n in range(12):
         for copy in copies(n):
             copy.wait()
-        if n > 0:
-            total = out[...]
-        elif has_base:
-            total = refs[1 + count][...]
-        else:
-            total = jnp.zeros(out.shape, jnp.float32)
-        lh, ll = two_halves(left[n])
-        rh, rl = two_halves(right[n])
-        for one, two in ((lh, rh), (lh, rl), (ll, rh)):
-            total -= jnp.dot(one, two, preferred_element_type=jnp.float32)
-        out[...] = total
-
-
-def product(restricted, panels, classes, terms, base=None):
-    has_base = base is not None
-    whole = pl.BlockSpec(memory_space=pltpu.VMEM)
-    return pl.pallas_call(
-        functools.partial(product_kernel, terms, len(panels), has_base),
+        panel = (right_high[n], right_low[n]) if n < 8 else two_halves(-right[n - 8])
+        total = jnp.zeros(out.shape, jnp.float32) if n == 0 else out[...]
+        out[...] = add_product(total, two_halves(left[n]), panel)
+
+
+def near_product(restricted, halves, panels, classes):
+    there = pl.BlockSpec(memory_space=pl.ANY)
+    return pl.pallas_call(
+        near_kernel,
         out_shape=jax.ShapeDtypeStruct((512, 256), jnp.float32),
         grid_spec=pltpu.PrefetchScalarGridSpec(
             num_scalar_prefetch=1,
             grid=(),
-            in_specs=[pl.BlockSpec(memory_space=pl.ANY)] * (1 + len(panels))
-            + [whole] * has_base,
-            out_specs=whole,
+            in_specs=[there] * 7,
+            out_specs=pl.BlockSpec(memory_space=pltpu.VMEM),
             scratch_shapes=[
-                pltpu.VMEM((len(terms), 512, 256), jnp.float32),
-                pltpu.VMEM((len(terms), 256, 256), jnp.float32),
-                pltpu.SemaphoreType.DMA((len(terms),)),
-                pltpu.SemaphoreType.DMA((len(terms),)),
+                pltpu.VMEM((12, 512, 256), jnp.float32),
+                pltpu.VMEM((8, 256, 256), jnp.bfloat16),
+                pltpu.VMEM((8, 256, 256), jnp.bfloat16),
+                pltpu.VMEM((4, 256, 256), jnp.float32),
+                pltpu.SemaphoreType.DMA((12,)),
+                pltpu.SemaphoreType.DMA((12,)),
+                pltpu.SemaphoreType.DMA((8,)),
             ],
         ),
-        compiler_params=pltpu.CompilerParams(vmem_limit_bytes=28 << 20),
+        compiler_params=pltpu.CompilerParams(vmem_limit_bytes=56 << 20),
         cost_estimate=pl.CostEstimate(
-            flops=len(terms) * (3 << 26),
-            bytes_accessed=len(terms) * (3 << 18),
-            transcendentals=0,
-        ),
-        name="product",
-    )(classes, restricted, *panels, *([base] if has_base else []))
+            flops=9 << 28, bytes_accessed=9 << 20, transcendentals=0
+        ),
+        name="near_product",
+    )(classes, restricted, *halves, *panels)
+
+
+def far_kernel(classes, *refs):
+    restricted, panels, base, lower, out, share = (
+        refs[0], refs[1:5], refs[5], refs[6:8], refs[8], refs[9:13]
+    )
+    left, right, held_high, held_low, left_sems, right_sems, sems = refs[13:]
+    held = (held_high, held_low)
+
+    def copies(n):
+        piece = restricted.at[classes[4 + n], 1]
+        yield pltpu.make_async_copy(piece, left.at[n], left_sems.at[n])
+        yield pltpu.make_async_copy(panels[n], right.at[n], right_sems.at[n])
+
+    for n in range(4):
+        for copy in copies(n):
+            copy.start()
+    for k in range(2):
+        pltpu.make_async_copy(lower[k], held[k], sems.at[k]).start()
+    out[...] = base[...]
+    for n in range(4):
+        for copy in copies(n):
+            copy.wait()
+        out[...] = add_product(out[...], two_halves(left[n]), two_halves(-right[n]))
+    for k in range(2):
+        pltpu.make_async_copy(lower[k], held[k], sems.at[k]).wait()
+    whole = two_halves(out[...])
+    for j in range(4):
+        share[j][...] = add_product(
+            jnp.zeros((256, 256), jnp.float32), (held_high[j], held_low[j]), whole
+        )
+
+
+def far_product(restricted, panels, classes, base, lower):
+    whole, there = pl.BlockSpec(memory_space=pltpu.VMEM), pl.BlockSpec(memory_space=pl.ANY)
+    block = jax.ShapeDtypeStruct((256, 256), jnp.float32)
+    return pl.pallas_call(
+        far_kernel,
+        out_shape=[jax.ShapeDtypeStruct((512, 256), jnp.float32)] + [block] * 4,
+        grid_spec=pltpu.PrefetchScalarGridSpec(
+            num_scalar_prefetch=1,
+            grid=(),
+            in_specs=[there] * 5 + [whole] + [there] * 2,
+            out_specs=[whole] * 5,
+            scratch_shapes=[
+                pltpu.VMEM((4, 512, 256), jnp.float32),
+                pltpu.VMEM((4, 256, 256), jnp.float32),
+                pltpu.VMEM((4, 256, 512), jnp.bfloat16),
+                pltpu.VMEM((4, 256, 512), jnp.bfloat16),
+                pltpu.SemaphoreType.DMA((4,)),
+                pltpu.SemaphoreType.DMA((4,)),
+                pltpu.SemaphoreType.DMA((2,)),
+            ],
+        ),
+        compiler_params=pltpu.CompilerParams(vmem_limit_bytes=56 << 20),
+        cost_estimate=pl.CostEstimate(
+            flops=3 << 29, bytes_accessed=6 << 20, transcendentals=0
+        ),
+        name="far_product",
+    )(classes, restricted, *panels, base, *lower)
 
 
 def on_device(parent_inverse, child_blocks, factor_rows, diag_inverse):
@@ -227,32 +305,36 @@
     ]
 
     to_x = jnp.stack([(x + j) % 4 for j in range(4)])
-    block = jnp.concatenate([(1 - half) * 4 + to_x, half * 4 + to_x])
     *cut, top, bottom, lower, near = lax.optimization_barrier(
         (*cut, factor[:256], factor[256:], lower, near)
     )
 
     restricted = pick(rows, cut, source, places)
     restricted, lower = lax.optimization_barrier((restricted, lower))
-    lower = jnp.take(lower, block, axis=0, mode="clip")
-    lower, top = lax.optimization_barrier((lower, top))
+    far_lower = jnp.take(lower, (1 - half) * 4 + to_x, axis=0, mode="clip")
+    far_lower, lower, near, top = lax.optimization_barrier(
+        (far_lower.transpose(0, 2, 1), lower, near, top)
+    )
     restricted = lax.all_gather(restricted, ("y", "core"), axis=0)
-    top, bottom = lax.optimization_barrier((shift(top, "zh", 2, 1), bottom))
+    own_lower = jnp.take(lower, half * 4 + to_x, axis=0, mode="clip")
+    halves = halve(far_lower, near)
+    top, bottom, own_lower, *halves = lax.optimization_barrier(
+        (shift(top, "zh", 2, 1), bottom, own_lower, *halves)
+    )
     bottom = shift(bottom, "zh", 2, 1)
     far_top = [top] + [shift(top, "x", 4, j) for j in (1, 2, 3)]
 
     number = jnp.arange(4, dtype=jnp.int32)
     classes = jnp.concatenate([half * 4 + number, (1 - half) * 4 + to_x]).astype(jnp.int32)
-    terms = [(j, 0, 512 * j + 256 * k, k) for j in range(4) for k in (0, 1)]
-    terms += [(4 + j, 1 + j, 0, 0) for j in range(4)]
-    inverse_local = product(restricted, [near] + far_top, classes, terms)
+    inverse_local = near_product(restricted, halves[2:], far_top, classes)
     far_bottom = [bottom] + [shift(bottom, "x", 4, j) for j in (1, 2, 3)]
-    terms = [(4 + j, j, 0, 1) for j in range(4)]
-    inverse_local = product(restricted, far_bottom, classes, terms, inverse_local)
-
-    share = [dot(lower[j], inverse_local, ((0,), (0,))) for j in range(4)]
-    *share, own_lower = lax.optimization_barrier((*share, lower[4:]))
-    other_half = share[0] + sum(shift(share[j], "x", 4, -j) for j in (1, 2, 3))
+    inverse_local, *share = far_product(
+        restricted, far_bottom, classes, inverse_local, halves[:2]
+    )
+
+    others = [shift(share[j], "x", 4, -j) for j in (1, 2, 3)]
+    others[0], own_lower = lax.optimization_barrier((others[0], own_lower))
+    other_half = share[0] + sum(others)
     share = [dot(own_lower[j], inverse_local, ((0,), (0,))) for j in range(4)]
     other_half, *share = lax.optimization_barrier((other_half, *share))
     other_half = shift(other_half, "zh", 2, 1)

time: 258 us -> 256 us (level)
  the two profiles are of different devices: /device:TPU:66 before, /device:TPU:72 now
where the time goes in v5:
time: 256 us; the launch traced here: 255 us
  waiting for transfers between devices  99.2 us (39%)
  starting transfers between devices  93.8 us (37%)
  Pallas kernels  21.1 us (8%)
  local copies, waits for them, and re-layouts  19.5 us (8%)
  between operations  14.4 us (6%)
  matrix products  4.52 us (2%)
    ppermute x15, starting transfers between devices, shift(): lax.ppermute(value, axis, [(i, (i - step) % count) for i in range(count)])  63.8 us
    ppermute x15, waiting for transfers between devices, shift(): lax.ppermute(value, axis, [(i, (i - step) % count) for i in range(count)])  37.9 us
    ppermute x4, waiting for transfers between devices, on_device(): up = lax.ppermute(up, 'zl', [(i, i + 1) for i in range(7)])  29.6 us
    ppermute x4, starting transfers between devices, on_device(): up = lax.ppermute(up, 'zl', [(i, i + 1) for i in range(7)])  16.7 us
    ppermute x4, waiting for transfers between devices, on_device(): down = lax.ppermute(down, 'zl', [(i + 1, i) for i in range(7)])  16.7 us
    ppermute x3, waiting for transfers between devices, on_device(): lax.ppermute(part, 'zl', [(i, i + d) for i in range(4, 8 - d)] + [(i, i -...  13.6 us
    pallas_call x1, Pallas kernels, near_product(): pl.pallas_call(near_kernel, out_shape=jax.ShapeDtypeStruct((512, 256), jn...  9.01 us
    unnamed x50, local copies, waits for them, and re-layouts  7.96 us
  transfers between devices with their start and end apart: 29, of which 17 were waited for; matrix products, arithmetic and copies ran while one was open for 7% of the time, Pallas kernels for 4%

profile of v5, /device:TPU:72, one launch (start us, length us, event | category | flops | bytes accessed | tf_op | source)
XLA Modules:
  0.0 255.0 jit_solution(15925825977562091621)
XLA Ops:
  8.7 3.8 %collective-permute-start = (f32[1024,128]{1,0:T(8,128)}, f32[1024,128]{1,0:T(8,128)S(1)}, u32[]{:S(2)}, u32[]{:S(2)}) collective-permute-start(f32[1024,128]{1,0:T(8,128)} %bitcast.68), channel_id=1, source_target_pairs={{0,64},{64,128},{128,192},{192,256},{256,320},{320,384},{384,448},... | collective-permute-start | bytes 1572872 | tf_op jit(solution)/shard_map/ppermute | solution.py:291
  14.6 9.9 %collective-permute-done.refs_1_ = f32[1024,128]{1,0:T(8,128)S(1)} collective-permute-done((f32[1024,128]{1,0:T(8,128)}, f32[1024,128]{1,0:T(8,128)S(1)}, u32[]{:S(2)}, u32[]{:S(2)}) %collective-permute-start) | collective-permute-done | bytes 524320 | tf_op jit(solution)/shard_map/ppermute | solution.py:291
  24.5 4.9 %collective-permute-done.1.refs_2_ = f32[1024,128]{1,0:T(8,128)S(1)} collective-permute-done((f32[1024,128]{1,0:T(8,128)}, f32[1024,128]{1,0:T(8,128)S(1)}, u32[]{:S(2)}, u32[]{:S(2)}) %collective-permute-start.1) | collective-permute-done | bytes 524320 | tf_op jit(solution)/shard_map/ppermute | solution.py:292
  29.4 4.8 %collective-permute-start.2 = (f32[1024,128]{1,0:T(8,128)S(1)}, f32[1024,128]{1,0:T(8,128)S(1)}, u32[]{:S(2)}, u32[]{:S(2)}) collective-permute-start(f32[1024,128]{1,0:T(8,128)S(1)} %collective-permute-done.refs_1_), channel_id=1, source_target_pairs={{0,64},{64,128},{128,192},{192,256},{256,320},{320,384},{384,448},... | collective-permute-start | bytes 1572872 | tf_op jit(solution)/shard_map/ppermute | solution.py:291
  37.3 7.0 %collective-permute-done.2.refs_3_ = f32[1024,128]{1,0:T(8,128)S(1)} collective-permute-done((f32[1024,128]{1,0:T(8,128)S(1)}, f32[1024,128]{1,0:T(8,128)S(1)}, u32[]{:S(2)}, u32[]{:S(2)}) %collective-permute-start.2) | collective-permute-done | bytes 524320 | tf_op jit(solution)/shard_map/ppermute | solution.py:291
  44.2 4.1 %collective-permute-done.3.refs_4_ = f32[1024,128]{1,0:T(8,128)S(1)} collective-permute-done((f32[1024,128]{1,0:T(8,128)S(1)}, f32[1024,128]{1,0:T(8,128)S(1)}, u32[]{:S(2)}, u32[]{:S(2)}) %collective-permute-start.3) | collective-permute-done | bytes 524320 | tf_op jit(solution)/shard_map/ppermute | solution.py:292
  48.4 4.2 %collective-permute-start.4 = (f32[1024,128]{1,0:T(8,128)S(1)}, f32[1024,128]{1,0:T(8,128)}, u32[]{:S(2)}, u32[]{:S(2)}) collective-permute-start(f32[1024,128]{1,0:T(8,128)S(1)} %collective-permute-done.2.refs_3_), channel_id=1, source_target_pairs={{0,64},{64,128},{128,192},{192,256},{256,320},{320,384},{384,448},... | collective-permute-start | bytes 1572872 | tf_op jit(solution)/shard_map/ppermute | solution.py:291
  55.4 6.4 %collective-permute-done.4.refs_5_ = f32[1024,128]{1,0:T(8,128)} collective-permute-done((f32[1024,128]{1,0:T(8,128)S(1)}, f32[1024,128]{1,0:T(8,128)}, u32[]{:S(2)}, u32[]{:S(2)}) %collective-permute-start.4) | collective-permute-done | bytes 524320 | tf_op jit(solution)/shard_map/ppermute | solution.py:291
  61.7 4.0 %collective-permute-done.5.refs_6_ = f32[1024,128]{1,0:T(8,128)S(1)} collective-permute-done((f32[1024,128]{1,0:T(8,128)S(1)}, f32[1024,128]{1,0:T(8,128)S(1)}, u32[]{:S(2)}, u32[]{:S(2)}) %collective-permute-start.5) | collective-permute-done | bytes 524320 | tf_op jit(solution)/shard_map/ppermute | solution.py:292
  66.6 3.8 %collective-permute-start.6 = (f32[1024,128]{1,0:T(8,128)}, f32[1024,128]{1,0:T(8,128)S(1)}, u32[]{:S(2)}, u32[]{:S(2)}) collective-permute-start(f32[1024,128]{1,0:T(8,128)} %collective-permute-done.4.refs_5_), channel_id=1, source_target_pairs={{0,64},{64,128},{128,192},{192,256},{256,320},{320,384},{384,448},... | collective-permute-start | bytes 1572872 | tf_op jit(solution)/shard_map/ppermute | solution.py:291
  72.7 6.4 %collective-permute-done.6.up.refs_7_ = f32[1024,128]{1,0:T(8,128)S(1)} collective-permute-done((f32[1024,128]{1,0:T(8,128)}, f32[1024,128]{1,0:T(8,128)S(1)}, u32[]{:S(2)}, u32[]{:S(2)}) %collective-permute-start.6) | collective-permute-done | bytes 524320 | tf_op jit(solution)/shard_map/ppermute | solution.py:291
  79.1 3.6 %collective-permute-done.7.down.refs_8_ = f32[1024,128]{1,0:T(8,128)S(1)} collective-permute-done((f32[1024,128]{1,0:T(8,128)}, f32[1024,128]{1,0:T(8,128)S(1)}, u32[]{:S(2)}, u32[]{:S(2)}) %collective-permute-start.7) | collective-permute-done | bytes 524320 | tf_op jit(solution)/shard_map/ppermute | solution.py:292
  90.2 11.3 %collective-permute-done.8.refs_9_ = f32[128,512]{1,0:T(8,128)S(1)} collective-permute-done((f32[128,512]{1,0:T(8,128)S(1)}, f32[128,512]{1,0:T(8,128)S(1)}, u32[]{:S(2)}, u32[]{:S(2)}) %collective-permute-start.8) | collective-permute-done | bytes 262176 | tf_op jit(solution)/shard_map/ppermute | solution.py:299
  104.6 3.3 %pick.1 = f32[2,512,256]{2,1,0:T(8,128)} custom-call(s32[20]{0:T(128)} %pad_add_fusion.1.info, f32[1024,128]{1,0:T(8,128)} %bitcast.70, f32[1024,128]{1,0:T(8,128)} %copy-done.9, f32[1024,128]{1,0:T(8,128)} %copy-done.10, f32[1024,128]{1,0:T(8,128)} %copy-done.11, f32[1024,128]{1,0:T(8,128)} %copy-done.12, f32[1024,128]{1,0:T(8,128)} %collective-permute-done.4.refs_5_, ...), custom_call_target="tpu_custom_call" | custom-call | bytes 3145728 | tf_op jit(solution)/shard_map/pick/pallas_call | solution.py:98
  108.1 4.2 %gather_fusion.1 = f32[4,512,256]{2,1,0:T(8,128)} fusion(f32[8,512,256]{2,1,0:T(8,128)} %all-gather.5.cloned.1.call-done, s32[1024]{0:T(1024)S(1)} %pad_clamp_fusion.1), kind=kCustom, calls=%fused_computation.1 | custom fusion | bytes 4194320 | tf_op jit(solution)/shard_map/jit(_take)/gather | solution.py:314
  114.2 10.0 %collective-permute-start.11 = (f32[256,256]{1,0:T(8,128)S(1)}, f32[256,256]{1,0:T(8,128)S(1)}, u32[]{:S(2)}, u32[]{:S(2)}) collective-permute-start(f32[256,256]{1,0:T(8,128)S(1)} %bitcast.72), channel_id=1, source_target_pairs={{0,32},{32,0},{1,33},{33,1},{2,34},{34,2},{3,35},{35,3},{4,36},{36... | collective-permute-start | bytes 786440 | tf_op jit(solution)/shard_map/ppermute | solution.py:11
  130.5 2.9 %gather_fusion.2 = f32[4,512,256]{2,1,0:T(8,128)S(1)} fusion(f32[8,512,256]{2,1,0:T(8,128)} %all-gather.5.cloned.1.call-done, s32[1024]{0:T(1024)S(1)} %pad_clamp_fusion), kind=kCustom, calls=%fused_computation.2 | custom fusion | bytes 4194320 | tf_op jit(solution)/shard_map/jit(_take)/gather | solution.py:319
  133.4 11.2 %collective-permute-done.11.refs_3_ = f32[256,256]{1,0:T(8,128)S(1)} collective-permute-done((f32[256,256]{1,0:T(8,128)S(1)}, f32[256,256]{1,0:T(8,128)S(1)}, u32[]{:S(2)}, u32[]{:S(2)}) %collective-permute-start.11) | collective-permute-done | bytes 262176 | tf_op jit(solution)/shard_map/ppermute | solution.py:11
  144.6 6.9 %collective-permute-start.12 = (f32[256,256]{1,0:T(8,128)S(1)}, f32[256,256]{1,0:T(8,128)S(1)}, u32[]{:S(2)}, u32[]{:S(2)}) collective-permute-start(f32[256,256]{1,0:T(8,128)S(1)} %bitcast.71), channel_id=1, source_target_pairs={{0,32},{32,0},{1,33},{33,1},{2,34},{34,2},{3,35},{35,3},{4,36},{36... | collective-permute-start | bytes 786440 | tf_op jit(solution)/shard_map/ppermute | solution.py:11
  151.5 4.6 %collective-permute-start.16 = (f32[256,256]{1,0:T(8,128)S(1)}, f32[256,256]{1,0:T(8,128)S(1)}, u32[]{:S(2)}, u32[]{:S(2)}) collective-permute-start(f32[256,256]{1,0:T(8,128)S(1)} %collective-permute-done.11.refs_3_), channel_id=1, source_target_pairs={{0,24},{8,0},{16,8},{24,16},{1,25},{9,1},{17,9},{25,17},{2,26},{10... | collective-permute-start | bytes 786440 | tf_op jit(solution)/shard_map/ppermute | solution.py:11
  161.7 9.5 %collective-permute-done.12.refs_1_ = f32[256,256]{1,0:T(8,128)S(1)} collective-permute-done((f32[256,256]{1,0:T(8,128)S(1)}, f32[256,256]{1,0:T(8,128)S(1)}, u32[]{:S(2)}, u32[]{:S(2)}) %collective-permute-start.12) | collective-permute-done | bytes 262176 | tf_op jit(solution)/shard_map/ppermute | solution.py:11
  171.2 4.6 %collective-permute-start.13 = (f32[256,256]{1,0:T(8,128)S(1)}, f32[256,256]{1,0:T(8,128)S(1)}, u32[]{:S(2)}, u32[]{:S(2)}) collective-permute-start(f32[256,256]{1,0:T(8,128)S(1)} %collective-permute-done.12.refs_1_), channel_id=1, source_target_pairs={{0,24},{8,0},{16,8},{24,16},{1,25},{9,1},{17,9},{25,17},{2,26},{10... | collective-permute-start | bytes 786440 | tf_op jit(solution)/shard_map/ppermute | solution.py:11
  175.8 2.8 %collective-permute-start.14 = (f32[256,256]{1,0:T(8,128)S(1)}, f32[256,256]{1,0:T(8,128)}, u32[]{:S(2)}, u32[]{:S(2)}) collective-permute-start(f32[256,256]{1,0:T(8,128)S(1)} %collective-permute-done.12.refs_1_), channel_id=1, source_target_pairs={{0,16},{8,24},{16,0},{24,8},{1,17},{9,25},{17,1},{25,9},{2,18},{10... | collective-permute-start | bytes 786440 | tf_op jit(solution)/shard_map/ppermute | solution.py:11
  182.7 9.0 %near_product.1.refs_5_ = f32[512,256]{1,0:T(8,128)} custom-call(s32[8]{0:T(128)} %pad_add_fusion.classes, f32[8,2,512,256]{3,2,1,0:T(8,128)} %bitcast.63, bf16[2048,256]{1,0:T(8,128)(2,1)} %copy-done.5, bf16[2048,256]{1,0:T(8,128)(2,1)} %copy-done.6, f32[256,256]{1,0:T(8,128)} %copy-done.16, f32[256,256]{1,0:T(8,128)} %copy-done.17, f32[256,256]{1,0:T(8,128)} %copy-done.18, ...), custom_call_target="tpu_custom_call" | custom-call | flops 2415919104 | bytes 9437184 | tf_op jit(solution)/shard_map/near_product/pallas_call | solution.py:176
  192.9 7.3 %far_product.1 = (f32[512,256]{1,0:T(8,128)}, f32[256,256]{1,0:T(8,128)}, f32[256,256]{1,0:T(8,128)}, f32[256,256]{1,0:T(8,128)}, f32[256,256]{1,0:T(8,128)}) custom-call(s32[8]{0:T(128)} %pad_add_fusion.classes, f32[8,2,512,256]{3,2,1,0:T(8,128)} %bitcast.64, f32[256,256]{1,0:T(8,128)} %copy-done.15, f32[256,256]{1,0:T(8,128)} %copy-done.19, ...), custom_call_target="tpu_custom_call" | custom-call | flops 1610612736 | bytes 6291456 | tf_op jit(solution)/shard_map/far_product/pallas_call | solution.py:236
  200.2 3.4 %collective-permute-start.19 = (f32[256,256]{1,0:T(8,128)}, f32[256,256]{1,0:T(8,128)S(1)}, u32[]{:S(2)}, u32[]{:S(2)}) collective-permute-start(f32[256,256]{1,0:T(8,128)} %get-tuple-element.87), channel_id=1, source_target_pairs={{0,8},{8,16},{16,24},{24,0},{1,9},{9,17},{17,25},{25,1},{2,10},{10... | collective-permute-start | bytes 786440 | tf_op jit(solution)/shard_map/ppermute | solution.py:11
  203.6 4.0 %collective-permute-start.20 = (f32[256,256]{1,0:T(8,128)}, f32[256,256]{1,0:T(8,128)S(1)}, u32[]{:S(2)}, u32[]{:S(2)}) collective-permute-start(f32[256,256]{1,0:T(8,128)} %get-tuple-element.90), channel_id=1, source_target_pairs={{0,16},{8,24},{16,0},{24,8},{1,17},{9,25},{17,1},{25,9},{2,18},{10... | collective-permute-start | bytes 786440 | tf_op jit(solution)/shard_map/ppermute | solution.py:11
  210.3 7.2 %collective-permute-done.19 = f32[256,256]{1,0:T(8,128)S(1)} collective-permute-done((f32[256,256]{1,0:T(8,128)}, f32[256,256]{1,0:T(8,128)S(1)}, u32[]{:S(2)}, u32[]{:S(2)}) %collective-permute-start.19) | collective-permute-done | bytes 262176 | tf_op jit(solution)/shard_map/ppermute | solution.py:11
  222.2 7.6 %collective-permute-start.22 = (f32[256,256]{1,0:T(8,128)S(1)}, f32[256,256]{1,0:T(8,128)S(1)}, u32[]{:S(2)}, u32[]{:S(2)}) collective-permute-start(f32[256,256]{1,0:T(8,128)S(1)} %add_add_fusion.1), channel_id=1, source_target_pairs={{0,32},{32,0},{1,33},{33,1},{2,34},{34,2},{3,35},{35,3},{4,36},{36... | collective-permute-start | bytes 786440 | tf_op jit(solution)/shard_map/ppermute | solution.py:11
  231.8 3.9 %collective-permute-start.24 = (f32[256,256]{1,0:T(8,128)S(1)}, f32[256,256]{1,0:T(8,128)S(1)}, u32[]{:S(2)}, u32[]{:S(2)}) collective-permute-start(f32[256,256]{1,0:T(8,128)S(1)} %fusion.2), channel_id=1, source_target_pairs={{0,16},{8,24},{16,0},{24,8},{1,17},{9,25},{17,1},{25,9},{2,18},{10... | collective-permute-start | bytes 786440 | tf_op jit(solution)/shard_map/ppermute | solution.py:11
  235.7 3.1 %collective-permute-start.25 = (f32[256,256]{1,0:T(8,128)S(1)}, f32[256,256]{1,0:T(8,128)S(1)}, u32[]{:S(2)}, u32[]{:S(2)}) collective-permute-start(f32[256,256]{1,0:T(8,128)S(1)} %fusion), channel_id=1, source_target_pairs={{0,24},{8,0},{16,8},{24,16},{1,25},{9,1},{17,9},{25,17},{2,26},{10... | collective-permute-start | bytes 786440 | tf_op jit(solution)/shard_map/ppermute | solution.py:11
  238.8 4.9 %collective-permute-done.22 = f32[256,256]{1,0:T(8,128)S(1)} collective-permute-done((f32[256,256]{1,0:T(8,128)S(1)}, f32[256,256]{1,0:T(8,128)S(1)}, u32[]{:S(2)}, u32[]{:S(2)}) %collective-permute-start.22) | collective-permute-done | bytes 262176 | tf_op jit(solution)/shard_map/ppermute | solution.py:11
  (118 shorter events, 55.9 us)
Async XLA Ops:
  7.2 82.2 %copy-start.8 = (f32[1,4,1,128,256]{4,3,2,1,0:T(8,128)S(1)}, f32[1,4,1,128,256]{4,3,2,1,0:T(8,128)}, u32[]{:S(2)}) copy-start(f32[1,4,1,128,256]{4,3,2,1,0:T(8,128)} %param.6) | copy-start | bytes 1572868
  7.2 97.4 %all-gather.7.cloned.1.call-start = ((), (), s32[]{:S(2)}) async-start(), calls=%async_computation.1 | async-start | bytes 2621440 | tf_op jit(solution)/shard_map/all_gather | solution.py:286
  7.9 96.6 %all-gather.5.cloned.1.call-start = ((), (), s32[]{:S(2)}) async-start(), calls=%async_computation | async-start | bytes 4718592 | tf_op jit(solution)/shard_map/all_gather | solution.py:285
  8.7 173.4 %all-gather.9.cloned.1.call-start = ((), (), s32[]{:S(2)}) async-start(), calls=%async_computation.2 | async-start | bytes 9437184 | tf_op jit(solution)/shard_map/all_gather | solution.py:318
  8.7 15.8 %collective-permute-start = (f32[1024,128]{1,0:T(8,128)}, f32[1024,128]{1,0:T(8,128)S(1)}, u32[]{:S(2)}, u32[]{:S(2)}) collective-permute-start(f32[1024,128]{1,0:T(8,128)} %bitcast.68), channel_id=1, source_target_pairs={{0,64},{64,128},{128,192},{192,256},{256,320},{320,384},{384,448},... | collective-permute-start | bytes 1572872 | tf_op jit(solution)/shard_map/ppermute | solution.py:291
  12.5 16.9 %collective-permute-start.1 = (f32[1024,128]{1,0:T(8,128)}, f32[1024,128]{1,0:T(8,128)S(1)}, u32[]{:S(2)}, u32[]{:S(2)}) collective-permute-start(f32[1024,128]{1,0:T(8,128)} %bitcast.69), channel_id=1, source_target_pairs={{64,0},{128,64},{192,128},{256,192},{320,256},{384,320},{448,384},... | collective-permute-start | bytes 1572872 | tf_op jit(solution)/shard_map/ppermute | solution.py:292
  24.5 80.1 %copy-start.9 = (f32[1024,128]{1,0:T(8,128)}, f32[1024,128]{1,0:T(8,128)S(1)}, u32[]{:S(2)}) copy-start(f32[1024,128]{1,0:T(8,128)S(1)} %collective-permute-done.refs_1_) | copy-start | bytes 1572868
  29.4 75.1 %copy-start.10 = (f32[1024,128]{1,0:T(8,128)}, f32[1024,128]{1,0:T(8,128)S(1)}, u32[]{:S(2)}) copy-start(f32[1024,128]{1,0:T(8,128)S(1)} %collective-permute-done.1.refs_2_) | copy-start | bytes 1572868
  29.4 14.8 %collective-permute-start.2 = (f32[1024,128]{1,0:T(8,128)S(1)}, f32[1024,128]{1,0:T(8,128)S(1)}, u32[]{:S(2)}, u32[]{:S(2)}) collective-permute-start(f32[1024,128]{1,0:T(8,128)S(1)} %collective-permute-done.refs_1_), channel_id=1, source_target_pairs={{0,64},{64,128},{128,192},{192,256},{256,320},{320,384},{384,448},... | collective-permute-start | bytes 1572872 | tf_op jit(solution)/shard_map/ppermute | solution.py:291
  34.3 14.1 %collective-permute-start.3 = (f32[1024,128]{1,0:T(8,128)S(1)}, f32[1024,128]{1,0:T(8,128)S(1)}, u32[]{:S(2)}, u32[]{:S(2)}) collective-permute-start(f32[1024,128]{1,0:T(8,128)S(1)} %collective-permute-done.1.refs_2_), channel_id=1, source_target_pairs={{64,0},{128,64},{192,128},{256,192},{320,256},{384,320},{448,384},... | collective-permute-start | bytes 1572872 | tf_op jit(solution)/shard_map/ppermute | solution.py:292
  48.4 13.4 %collective-permute-start.4 = (f32[1024,128]{1,0:T(8,128)S(1)}, f32[1024,128]{1,0:T(8,128)}, u32[]{:S(2)}, u32[]{:S(2)}) collective-permute-start(f32[1024,128]{1,0:T(8,128)S(1)} %collective-permute-done.2.refs_3_), channel_id=1, source_target_pairs={{0,64},{64,128},{128,192},{192,256},{256,320},{320,384},{384,448},... | collective-permute-start | bytes 1572872 | tf_op jit(solution)/shard_map/ppermute | solution.py:291
  52.6 13.2 %collective-permute-start.5 = (f32[1024,128]{1,0:T(8,128)S(1)}, f32[1024,128]{1,0:T(8,128)S(1)}, u32[]{:S(2)}, u32[]{:S(2)}) collective-permute-start(f32[1024,128]{1,0:T(8,128)S(1)} %collective-permute-done.3.refs_4_), channel_id=1, source_target_pairs={{64,0},{128,64},{192,128},{256,192},{320,256},{384,320},{448,384},... | collective-permute-start | bytes 1572872 | tf_op jit(solution)/shard_map/ppermute | solution.py:292
  66.6 12.5 %collective-permute-start.6 = (f32[1024,128]{1,0:T(8,128)}, f32[1024,128]{1,0:T(8,128)S(1)}, u32[]{:S(2)}, u32[]{:S(2)}) collective-permute-start(f32[1024,128]{1,0:T(8,128)} %collective-permute-done.4.refs_5_), channel_id=1, source_target_pairs={{0,64},{64,128},{128,192},{192,256},{256,320},{320,384},{384,448},... | collective-permute-start | bytes 1572872 | tf_op jit(solution)/shard_map/ppermute | solution.py:291
  70.4 12.2 %collective-permute-start.7 = (f32[1024,128]{1,0:T(8,128)}, f32[1024,128]{1,0:T(8,128)S(1)}, u32[]{:S(2)}, u32[]{:S(2)}) collective-permute-start(f32[1024,128]{1,0:T(8,128)} %copy-done.13), channel_id=1, source_target_pairs={{64,0},{128,64},{192,128},{256,192},{320,256},{384,320},{448,384},... | collective-permute-start | bytes 1572872 | tf_op jit(solution)/shard_map/ppermute | solution.py:292
  83.4 6.8 %collective-permute-start.10 = (f32[128,512]{1,0:T(8,128)S(1)}, f32[128,512]{1,0:T(8,128)S(1)}, u32[]{:S(2)}, u32[]{:S(2)}) collective-permute-start(f32[128,512]{1,0:T(8,128)S(1)} %get-tuple-element.61), channel_id=1, source_target_pairs={{256,448},{192,0},{257,449},{193,1},{258,450},{194,2},{259,451},{1... | collective-permute-start | bytes 786440 | tf_op jit(solution)/shard_map/ppermute | solution.py:299
  84.1 17.4 %collective-permute-start.8 = (f32[128,512]{1,0:T(8,128)S(1)}, f32[128,512]{1,0:T(8,128)S(1)}, u32[]{:S(2)}, u32[]{:S(2)}) collective-permute-start(f32[128,512]{1,0:T(8,128)S(1)} %get-tuple-element.59), channel_id=1, source_target_pairs={{256,320},{320,384},{384,448},{64,0},{128,64},{192,128},{257,321},... | collective-permute-start | bytes 786440 | tf_op jit(solution)/shard_map/ppermute | solution.py:299
  86.3 18.2 %collective-permute-start.9 = (f32[128,512]{1,0:T(8,128)S(1)}, f32[128,512]{1,0:T(8,128)}, u32[]{:S(2)}, u32[]{:S(2)}) collective-permute-start(f32[128,512]{1,0:T(8,128)S(1)} %get-tuple-element.60), channel_id=1, source_target_pairs={{256,384},{320,448},{128,0},{192,64},{257,385},{321,449},{129,1},{... | collective-permute-start | bytes 786440 | tf_op jit(solution)/shard_map/ppermute | solution.py:299
  114.2 30.3 %collective-permute-start.11 = (f32[256,256]{1,0:T(8,128)S(1)}, f32[256,256]{1,0:T(8,128)S(1)}, u32[]{:S(2)}, u32[]{:S(2)}) collective-permute-start(f32[256,256]{1,0:T(8,128)S(1)} %bitcast.72), channel_id=1, source_target_pairs={{0,32},{32,0},{1,33},{33,1},{2,34},{34,2},{3,35},{35,3},{4,36},{36... | collective-permute-start | bytes 786440 | tf_op jit(solution)/shard_map/ppermute | solution.py:11
  144.6 26.6 %collective-permute-start.12 = (f32[256,256]{1,0:T(8,128)S(1)}, f32[256,256]{1,0:T(8,128)S(1)}, u32[]{:S(2)}, u32[]{:S(2)}) collective-permute-start(f32[256,256]{1,0:T(8,128)S(1)} %bitcast.71), channel_id=1, source_target_pairs={{0,32},{32,0},{1,33},{33,1},{2,34},{34,2},{3,35},{35,3},{4,36},{36... | collective-permute-start | bytes 786440 | tf_op jit(solution)/shard_map/ppermute | solution.py:11
  151.5 27.1 %collective-permute-start.16 = (f32[256,256]{1,0:T(8,128)S(1)}, f32[256,256]{1,0:T(8,128)S(1)}, u32[]{:S(2)}, u32[]{:S(2)}) collective-permute-start(f32[256,256]{1,0:T(8,128)S(1)} %collective-permute-done.11.refs_3_), channel_id=1, source_target_pairs={{0,24},{8,0},{16,8},{24,16},{1,25},{9,1},{17,9},{25,17},{2,26},{10... | collective-permute-start | bytes 786440 | tf_op jit(solution)/shard_map/ppermute | solution.py:11
  156.1 25.9 %collective-permute-start.17 = (f32[256,256]{1,0:T(8,128)S(1)}, f32[256,256]{1,0:T(8,128)S(1)}, u32[]{:S(2)}, u32[]{:S(2)}) collective-permute-start(f32[256,256]{1,0:T(8,128)S(1)} %collective-permute-done.11.refs_3_), channel_id=1, source_target_pairs={{0,16},{8,24},{16,0},{24,8},{1,17},{9,25},{17,1},{25,9},{2,18},{10... | collective-permute-start | bytes 786440 | tf_op jit(solution)/shard_map/ppermute | solution.py:11
  158.9 23.1 %collective-permute-start.18 = (f32[256,256]{1,0:T(8,128)S(1)}, f32[256,256]{1,0:T(8,128)}, u32[]{:S(2)}, u32[]{:S(2)}) collective-permute-start(f32[256,256]{1,0:T(8,128)S(1)} %collective-permute-done.11.refs_3_), channel_id=1, source_target_pairs={{0,8},{8,16},{16,24},{24,0},{1,9},{9,17},{17,25},{25,1},{2,10},{10... | collective-permute-start | bytes 786440 | tf_op jit(solution)/shard_map/ppermute | solution.py:11
  171.2 20.5 %collective-permute-start.13 = (f32[256,256]{1,0:T(8,128)S(1)}, f32[256,256]{1,0:T(8,128)S(1)}, u32[]{:S(2)}, u32[]{:S(2)}) collective-permute-start(f32[256,256]{1,0:T(8,128)S(1)} %collective-permute-done.12.refs_1_), channel_id=1, source_target_pairs={{0,24},{8,0},{16,8},{24,16},{1,25},{9,1},{17,9},{25,17},{2,26},{10... | collective-permute-start | bytes 786440 | tf_op jit(solution)/shard_map/ppermute | solution.py:11
  175.8 15.9 %collective-permute-start.14 = (f32[256,256]{1,0:T(8,128)S(1)}, f32[256,256]{1,0:T(8,128)}, u32[]{:S(2)}, u32[]{:S(2)}) collective-permute-start(f32[256,256]{1,0:T(8,128)S(1)} %collective-permute-done.12.refs_1_), channel_id=1, source_target_pairs={{0,16},{8,24},{16,0},{24,8},{1,17},{9,25},{17,1},{25,9},{2,18},{10... | collective-permute-start | bytes 786440 | tf_op jit(solution)/shard_map/ppermute | solution.py:11
  178.6 14.3 %collective-permute-start.15 = (f32[256,256]{1,0:T(8,128)S(1)}, f32[256,256]{1,0:T(8,128)}, u32[]{:S(2)}, u32[]{:S(2)}) collective-permute-start(f32[256,256]{1,0:T(8,128)S(1)} %collective-permute-done.12.refs_1_), channel_id=1, source_target_pairs={{0,8},{8,16},{16,24},{24,0},{1,9},{9,17},{17,25},{25,1},{2,10},{10... | collective-permute-start | bytes 786440 | tf_op jit(solution)/shard_map/ppermute | solution.py:11
  200.2 17.3 %collective-permute-start.19 = (f32[256,256]{1,0:T(8,128)}, f32[256,256]{1,0:T(8,128)S(1)}, u32[]{:S(2)}, u32[]{:S(2)}) collective-permute-start(f32[256,256]{1,0:T(8,128)} %get-tuple-element.87), channel_id=1, source_target_pairs={{0,8},{8,16},{16,24},{24,0},{1,9},{9,17},{17,25},{25,1},{2,10},{10... | collective-permute-start | bytes 786440 | tf_op jit(solution)/shard_map/ppermute | solution.py:11
  203.6 18.5 %collective-permute-start.20 = (f32[256,256]{1,0:T(8,128)}, f32[256,256]{1,0:T(8,128)S(1)}, u32[]{:S(2)}, u32[]{:S(2)}) collective-permute-start(f32[256,256]{1,0:T(8,128)} %get-tuple-element.90), channel_id=1, source_target_pairs={{0,16},{8,24},{16,0},{24,8},{1,17},{9,25},{17,1},{25,9},{2,18},{10... | collective-permute-start | bytes 786440 | tf_op jit(solution)/shard_map/ppermute | solution.py:11
  207.6 14.5 %collective-permute-start.21 = (f32[256,256]{1,0:T(8,128)}, f32[256,256]{1,0:T(8,128)S(1)}, u32[]{:S(2)}, u32[]{:S(2)}) collective-permute-start(f32[256,256]{1,0:T(8,128)} %get-tuple-element.91), channel_id=1, source_target_pairs={{0,24},{8,0},{16,8},{24,16},{1,25},{9,1},{17,9},{25,17},{2,26},{10... | collective-permute-start | bytes 786440 | tf_op jit(solution)/shard_map/ppermute | solution.py:11
  222.2 21.5 %collective-permute-start.22 = (f32[256,256]{1,0:T(8,128)S(1)}, f32[256,256]{1,0:T(8,128)S(1)}, u32[]{:S(2)}, u32[]{:S(2)}) collective-permute-start(f32[256,256]{1,0:T(8,128)S(1)} %add_add_fusion.1), channel_id=1, source_target_pairs={{0,32},{32,0},{1,33},{33,1},{2,34},{34,2},{3,35},{35,3},{4,36},{36... | collective-permute-start | bytes 786440 | tf_op jit(solution)/shard_map/ppermute | solution.py:11
  229.8 13.9 %collective-permute-start.23 = (f32[256,256]{1,0:T(8,128)S(1)}, f32[256,256]{1,0:T(8,128)S(1)}, u32[]{:S(2)}, u32[]{:S(2)}) collective-permute-start(f32[256,256]{1,0:T(8,128)S(1)} %fusion.4), channel_id=1, source_target_pairs={{0,8},{8,16},{16,24},{24,0},{1,9},{9,17},{17,25},{25,1},{2,10},{10... | collective-permute-start | bytes 786440 | tf_op jit(solution)/shard_map/ppermute | solution.py:11
  231.8 13.5 %collective-permute-start.24 = (f32[256,256]{1,0:T(8,128)S(1)}, f32[256,256]{1,0:T(8,128)S(1)}, u32[]{:S(2)}, u32[]{:S(2)}) collective-permute-start(f32[256,256]{1,0:T(8,128)S(1)} %fusion.2), channel_id=1, source_target_pairs={{0,16},{8,24},{16,0},{24,8},{1,17},{9,25},{17,1},{25,9},{2,18},{10... | collective-permute-start | bytes 786440 | tf_op jit(solution)/shard_map/ppermute | solution.py:11
  235.7 12.0 %collective-permute-start.25 = (f32[256,256]{1,0:T(8,128)S(1)}, f32[256,256]{1,0:T(8,128)S(1)}, u32[]{:S(2)}, u32[]{:S(2)}) collective-permute-start(f32[256,256]{1,0:T(8,128)S(1)} %fusion), channel_id=1, source_target_pairs={{0,24},{8,0},{16,8},{24,16},{1,25},{9,1},{17,9},{25,17},{2,26},{10... | collective-permute-start | bytes 786440 | tf_op jit(solution)/shard_map/ppermute | solution.py:11
  (21 other events, 251.2 us)
Sparse Core Ops, SparseCore 0:
  10.1 42.1 all-gather.6
  54.4 38.8 all-gather.4
  108.1 58.0 all-gather.8

commit v6 on v4

--- a/solution.py
+++ b/solution.py
@@ -123,9 +123,8 @@
 def product_kernel(terms, count, last, classes, *refs):
     restricted, panels = refs[0], refs[1 : 1 + count]
     if last:
-        base, lower, out, share, left, right, left_sems, right_sems, held, sem = refs[
-            1 + count :
-        ]
+        base, lower, out, *share = refs[1 + count : 8 + count]
+        left, right, left_sems, right_sems, held, sem = refs[8 + count :]
     else:
         out, left, right, left_sems, right_sems = refs[1 + count :]
 
@@ -166,7 +165,7 @@
             total = jnp.zeros((256, 256), jnp.float32)
             for one, two in ((lh, rh), (lh, rl), (ll, rh)):
                 total += jnp.dot(one, two, preferred_element_type=jnp.float32)
-            share[j] = total
+            share[j][...] = total
 
 
 def product(restricted, panels, classes, terms, base=None, lower=None):
@@ -180,7 +179,7 @@
         pltpu.SemaphoreType.DMA((len(terms),)),
     ]
     if last:
-        out_shape += [jax.ShapeDtypeStruct((4, 256, 256), jnp.float32)]
+        out_shape += [jax.ShapeDtypeStruct((256, 256), jnp.float32)] * 4
         scratch += [pltpu.VMEM((4, 256, 512), jnp.float32), pltpu.SemaphoreType.DMA]
     return pl.pallas_call(
         functools.partial(product_kernel, terms, len(panels), last),
@@ -255,10 +254,13 @@
     restricted = pick(rows, cut, source, places)
     restricted, lower = lax.optimization_barrier((restricted, lower))
     far_lower = jnp.take(lower, (1 - half) * 4 + to_x, axis=0, mode="clip")
+    far_lower, lower, top = lax.optimization_barrier((far_lower, lower, top))
+    far_lower = far_lower.transpose(0, 2, 1)
     own_lower = jnp.take(lower, half * 4 + to_x, axis=0, mode="clip")
-    far_lower, top = lax.optimization_barrier((far_lower.transpose(0, 2, 1), top))
     restricted = lax.all_gather(restricted, ("y", "core"), axis=0)
-    top, bottom = lax.optimization_barrier((shift(top, "zh", 2, 1), bottom))
+    top, bottom, far_lower, own_lower = lax.optimization_barrier(
+        (shift(top, "zh", 2, 1), bottom, far_lower, own_lower)
+    )
     bottom = shift(bottom, "zh", 2, 1)
     far_top = [top] + [shift(top, "x", 4, j) for j in (1, 2, 3)]
 
@@ -269,7 +271,7 @@
     (inverse_local,) = product(restricted, [near] + far_top, classes, terms)
     far_bottom = [bottom] + [shift(bottom, "x", 4, j) for j in (1, 2, 3)]
     terms = [(4 + j, j, 0, 1) for j in range(4)]
-    inverse_local, share = product(
+    inverse_local, *share = product(
         restricted, far_bottom, classes, terms, inverse_local, far_lower
     )
 

time: 259 us -> 252 us (0.973)
  the two profiles are of different devices: /device:TPU:87 before, /device:TPU:72 now
where the time goes in v6:
time: 252 us; the launch traced here: 251 us
  waiting for transfers between devices  105 us (42%)
  starting transfers between devices  93.3 us (37%)
  Pallas kernels  18.7 us (7%)
  between operations  14.3 us (6%)
  local copies, waits for them, and re-layouts  12.5 us (5%)
  matrix products  4.52 us (2%)
    ppermute x15, starting transfers between devices, shift(): lax.ppermute(value, axis, [(i, (i - step) % count) for i in range(count)])  63.3 us
    ppermute x15, waiting for transfers between devices, shift(): lax.ppermute(value, axis, [(i, (i - step) % count) for i in range(count)])  44 us
    ppermute x4, waiting for transfers between devices, on_device(): up = lax.ppermute(up, 'zl', [(i, i + 1) for i in range(7)])  29.6 us
    ppermute x4, starting transfers between devices, on_device(): up = lax.ppermute(up, 'zl', [(i, i + 1) for i in range(7)])  16.7 us
    ppermute x4, waiting for transfers between devices, on_device(): down = lax.ppermute(down, 'zl', [(i + 1, i) for i in range(7)])  16.7 us
    pallas_call x2, Pallas kernels, product(): pl.pallas_call(functools.partial(product_kernel, terms, len(panels), last...  14.6 us
    ppermute x3, waiting for transfers between devices, on_device(): lax.ppermute(part, 'zl', [(i, i + d) for i in range(4, 8 - d)] + [(i, i -...  13.7 us
    ppermute x4, starting transfers between devices, on_device(): down = lax.ppermute(down, 'zl', [(i + 1, i) for i in range(7)])  7.88 us
  transfers between devices with their start and end apart: 29, of which 17 were waited for; matrix products, arithmetic and copies ran while one was open for 7% of the time, Pallas kernels for 4%

profile of v6, /device:TPU:72, one launch (start us, length us, event | category | flops | bytes accessed | tf_op | source)
XLA Modules:
  0.0 251.3 jit_solution(5311061841809463004)
XLA Ops:
  8.7 3.8 %collective-permute-start = (f32[1024,128]{1,0:T(8,128)}, f32[1024,128]{1,0:T(8,128)S(1)}, u32[]{:S(2)}, u32[]{:S(2)}) collective-permute-start(f32[1024,128]{1,0:T(8,128)} %bitcast.68), channel_id=1, source_target_pairs={{0,64},{64,128},{128,192},{192,256},{256,320},{320,384},{384,448},... | collective-permute-start | bytes 1572872 | tf_op jit(solution)/shard_map/ppermute | solution.py:233
  14.6 9.9 %collective-permute-done.refs_1_ = f32[1024,128]{1,0:T(8,128)S(1)} collective-permute-done((f32[1024,128]{1,0:T(8,128)}, f32[1024,128]{1,0:T(8,128)S(1)}, u32[]{:S(2)}, u32[]{:S(2)}) %collective-permute-start) | collective-permute-done | bytes 524320 | tf_op jit(solution)/shard_map/ppermute | solution.py:233
  24.5 4.9 %collective-permute-done.1.refs_2_ = f32[1024,128]{1,0:T(8,128)S(1)} collective-permute-done((f32[1024,128]{1,0:T(8,128)}, f32[1024,128]{1,0:T(8,128)S(1)}, u32[]{:S(2)}, u32[]{:S(2)}) %collective-permute-start.1) | collective-permute-done | bytes 524320 | tf_op jit(solution)/shard_map/ppermute | solution.py:234
  29.4 4.8 %collective-permute-start.2 = (f32[1024,128]{1,0:T(8,128)S(1)}, f32[1024,128]{1,0:T(8,128)S(1)}, u32[]{:S(2)}, u32[]{:S(2)}) collective-permute-start(f32[1024,128]{1,0:T(8,128)S(1)} %collective-permute-done.refs_1_), channel_id=1, source_target_pairs={{0,64},{64,128},{128,192},{192,256},{256,320},{320,384},{384,448},... | collective-permute-start | bytes 1572872 | tf_op jit(solution)/shard_map/ppermute | solution.py:233
  37.3 7.0 %collective-permute-done.2.refs_3_ = f32[1024,128]{1,0:T(8,128)S(1)} collective-permute-done((f32[1024,128]{1,0:T(8,128)S(1)}, f32[1024,128]{1,0:T(8,128)S(1)}, u32[]{:S(2)}, u32[]{:S(2)}) %collective-permute-start.2) | collective-permute-done | bytes 524320 | tf_op jit(solution)/shard_map/ppermute | solution.py:233
  44.2 4.1 %collective-permute-done.3.refs_4_ = f32[1024,128]{1,0:T(8,128)S(1)} collective-permute-done((f32[1024,128]{1,0:T(8,128)S(1)}, f32[1024,128]{1,0:T(8,128)S(1)}, u32[]{:S(2)}, u32[]{:S(2)}) %collective-permute-start.3) | collective-permute-done | bytes 524320 | tf_op jit(solution)/shard_map/ppermute | solution.py:234
  48.4 4.2 %collective-permute-start.4 = (f32[1024,128]{1,0:T(8,128)S(1)}, f32[1024,128]{1,0:T(8,128)}, u32[]{:S(2)}, u32[]{:S(2)}) collective-permute-start(f32[1024,128]{1,0:T(8,128)S(1)} %collective-permute-done.2.refs_3_), channel_id=1, source_target_pairs={{0,64},{64,128},{128,192},{192,256},{256,320},{320,384},{384,448},... | collective-permute-start | bytes 1572872 | tf_op jit(solution)/shard_map/ppermute | solution.py:233
  55.4 6.4 %collective-permute-done.4.refs_5_ = f32[1024,128]{1,0:T(8,128)} collective-permute-done((f32[1024,128]{1,0:T(8,128)S(1)}, f32[1024,128]{1,0:T(8,128)}, u32[]{:S(2)}, u32[]{:S(2)}) %collective-permute-start.4) | collective-permute-done | bytes 524320 | tf_op jit(solution)/shard_map/ppermute | solution.py:233
  61.7 4.0 %collective-permute-done.5.refs_6_ = f32[1024,128]{1,0:T(8,128)S(1)} collective-permute-done((f32[1024,128]{1,0:T(8,128)S(1)}, f32[1024,128]{1,0:T(8,128)S(1)}, u32[]{:S(2)}, u32[]{:S(2)}) %collective-permute-start.5) | collective-permute-done | bytes 524320 | tf_op jit(solution)/shard_map/ppermute | solution.py:234
  66.6 3.8 %collective-permute-start.6 = (f32[1024,128]{1,0:T(8,128)}, f32[1024,128]{1,0:T(8,128)S(1)}, u32[]{:S(2)}, u32[]{:S(2)}) collective-permute-start(f32[1024,128]{1,0:T(8,128)} %collective-permute-done.4.refs_5_), channel_id=1, source_target_pairs={{0,64},{64,128},{128,192},{192,256},{256,320},{320,384},{384,448},... | collective-permute-start | bytes 1572872 | tf_op jit(solution)/shard_map/ppermute | solution.py:233
  72.7 6.4 %collective-permute-done.6.up.refs_7_ = f32[1024,128]{1,0:T(8,128)S(1)} collective-permute-done((f32[1024,128]{1,0:T(8,128)}, f32[1024,128]{1,0:T(8,128)S(1)}, u32[]{:S(2)}, u32[]{:S(2)}) %collective-permute-start.6) | collective-permute-done | bytes 524320 | tf_op jit(solution)/shard_map/ppermute | solution.py:233
  79.1 3.6 %collective-permute-done.7.down.refs_8_ = f32[1024,128]{1,0:T(8,128)S(1)} collective-permute-done((f32[1024,128]{1,0:T(8,128)}, f32[1024,128]{1,0:T(8,128)S(1)}, u32[]{:S(2)}, u32[]{:S(2)}) %collective-permute-start.7) | collective-permute-done | bytes 524320 | tf_op jit(solution)/shard_map/ppermute | solution.py:234
  90.2 11.3 %collective-permute-done.8.refs_9_ = f32[128,512]{1,0:T(8,128)S(1)} collective-permute-done((f32[128,512]{1,0:T(8,128)S(1)}, f32[128,512]{1,0:T(8,128)S(1)}, u32[]{:S(2)}, u32[]{:S(2)}) %collective-permute-start.8) | collective-permute-done | bytes 262176 | tf_op jit(solution)/shard_map/ppermute | solution.py:241
  104.6 3.3 %pick.1 = f32[2,512,256]{2,1,0:T(8,128)} custom-call(s32[20]{0:T(128)} %pad_add_fusion.1.info, f32[1024,128]{1,0:T(8,128)} %bitcast.70, f32[1024,128]{1,0:T(8,128)} %copy-done.4, f32[1024,128]{1,0:T(8,128)} %copy-done.5, f32[1024,128]{1,0:T(8,128)} %copy-done.6, f32[1024,128]{1,0:T(8,128)} %copy-done.7, f32[1024,128]{1,0:T(8,128)} %collective-permute-done.4.refs_5_, ...), custom_call_target="tpu_custom_call" | custom-call | bytes 3145728 | tf_op jit(solution)/shard_map/pick/pallas_call | solution.py:98
  108.1 2.9 %gather_fusion.1 = f32[4,512,256]{2,1,0:T(8,128)S(1)} fusion(f32[8,512,256]{2,1,0:T(8,128)} %all-gather.5.cloned.1.call-done, s32[1024]{0:T(1024)S(1)} %pad_clamp_fusion.1), kind=kCustom, calls=%fused_computation.1 | custom fusion | bytes 4194320 | tf_op jit(solution)/shard_map/jit(_take)/gather | solution.py:256
  111.0 10.2 %collective-permute-start.11 = (f32[256,256]{1,0:T(8,128)S(1)}, f32[256,256]{1,0:T(8,128)S(1)}, u32[]{:S(2)}, u32[]{:S(2)}) collective-permute-start(f32[256,256]{1,0:T(8,128)S(1)} %bitcast.72), channel_id=1, source_target_pairs={{0,32},{32,0},{1,33},{33,1},{2,34},{34,2},{3,35},{35,3},{4,36},{36... | collective-permute-start | bytes 786440 | tf_op jit(solution)/shard_map/ppermute | solution.py:11
  123.1 2.9 %gather_fusion.2 = f32[4,512,256]{2,1,0:T(8,128)S(1)} fusion(f32[8,512,256]{2,1,0:T(8,128)} %all-gather.5.cloned.1.call-done, s32[1024]{0:T(1024)S(1)} %pad_clamp_fusion), kind=kCustom, calls=%fused_computation.2 | custom fusion | bytes 4194320 | tf_op jit(solution)/shard_map/jit(_take)/gather | solution.py:259
  126.0 15.4 %collective-permute-done.11.refs_2_ = f32[256,256]{1,0:T(8,128)S(1)} collective-permute-done((f32[256,256]{1,0:T(8,128)S(1)}, f32[256,256]{1,0:T(8,128)S(1)}, u32[]{:S(2)}, u32[]{:S(2)}) %collective-permute-start.11) | collective-permute-done | bytes 262176 | tf_op jit(solution)/shard_map/ppermute | solution.py:11
  141.4 6.9 %collective-permute-start.12 = (f32[256,256]{1,0:T(8,128)S(1)}, f32[256,256]{1,0:T(8,128)S(1)}, u32[]{:S(2)}, u32[]{:S(2)}) collective-permute-start(f32[256,256]{1,0:T(8,128)S(1)} %bitcast.71), channel_id=1, source_target_pairs={{0,32},{32,0},{1,33},{33,1},{2,34},{34,2},{3,35},{35,3},{4,36},{36... | collective-permute-start | bytes 786440 | tf_op jit(solution)/shard_map/ppermute | solution.py:11
  148.3 4.6 %collective-permute-start.16 = (f32[256,256]{1,0:T(8,128)S(1)}, f32[256,256]{1,0:T(8,128)S(1)}, u32[]{:S(2)}, u32[]{:S(2)}) collective-permute-start(f32[256,256]{1,0:T(8,128)S(1)} %collective-permute-done.11.refs_2_), channel_id=1, source_target_pairs={{0,24},{8,0},{16,8},{24,16},{1,25},{9,1},{17,9},{25,17},{2,26},{10... | collective-permute-start | bytes 786440 | tf_op jit(solution)/shard_map/ppermute | solution.py:11
  158.5 9.5 %collective-permute-done.12.refs_1_ = f32[256,256]{1,0:T(8,128)S(1)} collective-permute-done((f32[256,256]{1,0:T(8,128)S(1)}, f32[256,256]{1,0:T(8,128)S(1)}, u32[]{:S(2)}, u32[]{:S(2)}) %collective-permute-start.12) | collective-permute-done | bytes 262176 | tf_op jit(solution)/shard_map/ppermute | solution.py:11
  168.0 4.6 %collective-permute-start.13 = (f32[256,256]{1,0:T(8,128)S(1)}, f32[256,256]{1,0:T(8,128)S(1)}, u32[]{:S(2)}, u32[]{:S(2)}) collective-permute-start(f32[256,256]{1,0:T(8,128)S(1)} %collective-permute-done.12.refs_1_), channel_id=1, source_target_pairs={{0,24},{8,0},{16,8},{24,16},{1,25},{9,1},{17,9},{25,17},{2,26},{10... | collective-permute-start | bytes 786440 | tf_op jit(solution)/shard_map/ppermute | solution.py:11
  175.3 2.8 %collective-permute-start.15 = (f32[256,256]{1,0:T(8,128)S(1)}, f32[256,256]{1,0:T(8,128)}, u32[]{:S(2)}, u32[]{:S(2)}) collective-permute-start(f32[256,256]{1,0:T(8,128)S(1)} %collective-permute-done.12.refs_1_), channel_id=1, source_target_pairs={{0,8},{8,16},{16,24},{24,0},{1,9},{9,17},{17,25},{25,1},{2,10},{10... | collective-permute-start | bytes 786440 | tf_op jit(solution)/shard_map/ppermute | solution.py:11
  179.4 8.1 %product.2.refs_5_ = f32[512,256]{1,0:T(8,128)} custom-call(s32[8]{0:T(128)} %pad_add_fusion.classes, f32[8,2,512,256]{3,2,1,0:T(8,128)} %bitcast.61, f32[2048,256]{1,0:T(8,128)} %bitcast.67, f32[256,256]{1,0:T(8,128)} %copy-done.11, f32[256,256]{1,0:T(8,128)} %copy-done.12, f32[256,256]{1,0:T(8,128)} %copy-done.13, f32[256,256]{1,0:T(8,128)} %collective-permute-done.18.refs_5_), custom_call_target="tpu_custom_call" | custom-call | flops 2415919104 | bytes 9437184 | tf_op jit(solution)/shard_map/product/pallas_call | solution.py:184
  189.7 6.5 %product.3 = (f32[512,256]{1,0:T(8,128)}, f32[256,256]{1,0:T(8,128)}, f32[256,256]{1,0:T(8,128)}, f32[256,256]{1,0:T(8,128)}, f32[256,256]{1,0:T(8,128)}) custom-call(s32[8]{0:T(128)} %pad_add_fusion.classes, f32[8,2,512,256]{3,2,1,0:T(8,128)} %bitcast.62, f32[256,256]{1,0:T(8,128)} %copy-done.10, f32[256,256]{1,0:T(8,128)} %copy-done.14, ...), custom_call_target="tpu_custom_call" | custom-call | flops 805306368 | bytes 3145728 | tf_op jit(solution)/shard_map/product/pallas_call | solution.py:184
  198.6 3.9 %collective-permute-start.20 = (f32[256,256]{1,0:T(8,128)}, f32[256,256]{1,0:T(8,128)S(1)}, u32[]{:S(2)}, u32[]{:S(2)}) collective-permute-start(f32[256,256]{1,0:T(8,128)} %get-tuple-element.74), channel_id=1, source_target_pairs={{0,16},{8,24},{16,0},{24,8},{1,17},{9,25},{17,1},{25,9},{2,18},{10... | collective-permute-start | bytes 786440 | tf_op jit(solution)/shard_map/ppermute | solution.py:11
  202.6 3.1 %collective-permute-start.21 = (f32[256,256]{1,0:T(8,128)}, f32[256,256]{1,0:T(8,128)S(1)}, u32[]{:S(2)}, u32[]{:S(2)}) collective-permute-start(f32[256,256]{1,0:T(8,128)} %get-tuple-element.75), channel_id=1, source_target_pairs={{0,24},{8,0},{16,8},{24,16},{1,25},{9,1},{17,9},{25,17},{2,26},{10... | collective-permute-start | bytes 786440 | tf_op jit(solution)/shard_map/ppermute | solution.py:11
  205.6 7.8 %collective-permute-done.19 = f32[256,256]{1,0:T(8,128)S(1)} collective-permute-done((f32[256,256]{1,0:T(8,128)}, f32[256,256]{1,0:T(8,128)S(1)}, u32[]{:S(2)}, u32[]{:S(2)}) %collective-permute-start.19) | collective-permute-done | bytes 262176 | tf_op jit(solution)/shard_map/ppermute | solution.py:11
  218.1 7.6 %collective-permute-start.22 = (f32[256,256]{1,0:T(8,128)S(1)}, f32[256,256]{1,0:T(8,128)S(1)}, u32[]{:S(2)}, u32[]{:S(2)}) collective-permute-start(f32[256,256]{1,0:T(8,128)S(1)} %add_add_fusion.1), channel_id=1, source_target_pairs={{0,32},{32,0},{1,33},{33,1},{2,34},{34,2},{3,35},{35,3},{4,36},{36... | collective-permute-start | bytes 786440 | tf_op jit(solution)/shard_map/ppermute | solution.py:11
  227.6 3.9 %collective-permute-start.24 = (f32[256,256]{1,0:T(8,128)S(1)}, f32[256,256]{1,0:T(8,128)S(1)}, u32[]{:S(2)}, u32[]{:S(2)}) collective-permute-start(f32[256,256]{1,0:T(8,128)S(1)} %fusion.2), channel_id=1, source_target_pairs={{0,16},{8,24},{16,0},{24,8},{1,17},{9,25},{17,1},{25,9},{2,18},{10... | collective-permute-start | bytes 786440 | tf_op jit(solution)/shard_map/ppermute | solution.py:11
  231.5 3.1 %collective-permute-start.25 = (f32[256,256]{1,0:T(8,128)S(1)}, f32[256,256]{1,0:T(8,128)S(1)}, u32[]{:S(2)}, u32[]{:S(2)}) collective-permute-start(f32[256,256]{1,0:T(8,128)S(1)} %fusion), channel_id=1, source_target_pairs={{0,24},{8,0},{16,8},{24,16},{1,25},{9,1},{17,9},{25,17},{2,26},{10... | collective-permute-start | bytes 786440 | tf_op jit(solution)/shard_map/ppermute | solution.py:11
  234.7 5.8 %collective-permute-done.22 = f32[256,256]{1,0:T(8,128)S(1)} collective-permute-done((f32[256,256]{1,0:T(8,128)S(1)}, f32[256,256]{1,0:T(8,128)S(1)}, u32[]{:S(2)}, u32[]{:S(2)}) %collective-permute-start.22) | collective-permute-done | bytes 262176 | tf_op jit(solution)/shard_map/ppermute | solution.py:11
  (107 shorter events, 49.8 us)
Async XLA Ops:
  7.2 82.2 %copy-start.3 = (f32[1,4,1,128,256]{4,3,2,1,0:T(8,128)S(1)}, f32[1,4,1,128,256]{4,3,2,1,0:T(8,128)}, u32[]{:S(2)}) copy-start(f32[1,4,1,128,256]{4,3,2,1,0:T(8,128)} %param.6) | copy-start | bytes 1572868
  7.2 97.3 %all-gather.7.cloned.1.call-start = ((), (), s32[]{:S(2)}) async-start(), calls=%async_computation.1 | async-start | bytes 2621440 | tf_op jit(solution)/shard_map/all_gather | solution.py:228
  7.9 96.6 %all-gather.5.cloned.1.call-start = ((), (), s32[]{:S(2)}) async-start(), calls=%async_computation | async-start | bytes 4718592 | tf_op jit(solution)/shard_map/all_gather | solution.py:227
  8.7 170.1 %all-gather.9.cloned.1.call-start = ((), (), s32[]{:S(2)}) async-start(), calls=%async_computation.2 | async-start | bytes 9437184 | tf_op jit(solution)/shard_map/all_gather | solution.py:260
  8.7 15.8 %collective-permute-start = (f32[1024,128]{1,0:T(8,128)}, f32[1024,128]{1,0:T(8,128)S(1)}, u32[]{:S(2)}, u32[]{:S(2)}) collective-permute-start(f32[1024,128]{1,0:T(8,128)} %bitcast.68), channel_id=1, source_target_pairs={{0,64},{64,128},{128,192},{192,256},{256,320},{320,384},{384,448},... | collective-permute-start | bytes 1572872 | tf_op jit(solution)/shard_map/ppermute | solution.py:233
  12.5 16.9 %collective-permute-start.1 = (f32[1024,128]{1,0:T(8,128)}, f32[1024,128]{1,0:T(8,128)S(1)}, u32[]{:S(2)}, u32[]{:S(2)}) collective-permute-start(f32[1024,128]{1,0:T(8,128)} %bitcast.69), channel_id=1, source_target_pairs={{64,0},{128,64},{192,128},{256,192},{320,256},{384,320},{448,384},... | collective-permute-start | bytes 1572872 | tf_op jit(solution)/shard_map/ppermute | solution.py:234
  24.5 80.1 %copy-start.4 = (f32[1024,128]{1,0:T(8,128)}, f32[1024,128]{1,0:T(8,128)S(1)}, u32[]{:S(2)}) copy-start(f32[1024,128]{1,0:T(8,128)S(1)} %collective-permute-done.refs_1_) | copy-start | bytes 1572868
  29.4 75.1 %copy-start.5 = (f32[1024,128]{1,0:T(8,128)}, f32[1024,128]{1,0:T(8,128)S(1)}, u32[]{:S(2)}) copy-start(f32[1024,128]{1,0:T(8,128)S(1)} %collective-permute-done.1.refs_2_) | copy-start | bytes 1572868
  29.4 14.8 %collective-permute-start.2 = (f32[1024,128]{1,0:T(8,128)S(1)}, f32[1024,128]{1,0:T(8,128)S(1)}, u32[]{:S(2)}, u32[]{:S(2)}) collective-permute-start(f32[1024,128]{1,0:T(8,128)S(1)} %collective-permute-done.refs_1_), channel_id=1, source_target_pairs={{0,64},{64,128},{128,192},{192,256},{256,320},{320,384},{384,448},... | collective-permute-start | bytes 1572872 | tf_op jit(solution)/shard_map/ppermute | solution.py:233
  34.3 14.1 %collective-permute-start.3 = (f32[1024,128]{1,0:T(8,128)S(1)}, f32[1024,128]{1,0:T(8,128)S(1)}, u32[]{:S(2)}, u32[]{:S(2)}) collective-permute-start(f32[1024,128]{1,0:T(8,128)S(1)} %collective-permute-done.1.refs_2_), channel_id=1, source_target_pairs={{64,0},{128,64},{192,128},{256,192},{320,256},{384,320},{448,384},... | collective-permute-start | bytes 1572872 | tf_op jit(solution)/shard_map/ppermute | solution.py:234
  48.4 13.4 %collective-permute-start.4 = (f32[1024,128]{1,0:T(8,128)S(1)}, f32[1024,128]{1,0:T(8,128)}, u32[]{:S(2)}, u32[]{:S(2)}) collective-permute-start(f32[1024,128]{1,0:T(8,128)S(1)} %collective-permute-done.2.refs_3_), channel_id=1, source_target_pairs={{0,64},{64,128},{128,192},{192,256},{256,320},{320,384},{384,448},... | collective-permute-start | bytes 1572872 | tf_op jit(solution)/shard_map/ppermute | solution.py:233
  52.6 13.2 %collective-permute-start.5 = (f32[1024,128]{1,0:T(8,128)S(1)}, f32[1024,128]{1,0:T(8,128)S(1)}, u32[]{:S(2)}, u32[]{:S(2)}) collective-permute-start(f32[1024,128]{1,0:T(8,128)S(1)} %collective-permute-done.3.refs_4_), channel_id=1, source_target_pairs={{64,0},{128,64},{192,128},{256,192},{320,256},{384,320},{448,384},... | collective-permute-start | bytes 1572872 | tf_op jit(solution)/shard_map/ppermute | solution.py:234
  66.6 12.5 %collective-permute-start.6 = (f32[1024,128]{1,0:T(8,128)}, f32[1024,128]{1,0:T(8,128)S(1)}, u32[]{:S(2)}, u32[]{:S(2)}) collective-permute-start(f32[1024,128]{1,0:T(8,128)} %collective-permute-done.4.refs_5_), channel_id=1, source_target_pairs={{0,64},{64,128},{128,192},{192,256},{256,320},{320,384},{384,448},... | collective-permute-start | bytes 1572872 | tf_op jit(solution)/shard_map/ppermute | solution.py:233
  70.4 12.2 %collective-permute-start.7 = (f32[1024,128]{1,0:T(8,128)}, f32[1024,128]{1,0:T(8,128)S(1)}, u32[]{:S(2)}, u32[]{:S(2)}) collective-permute-start(f32[1024,128]{1,0:T(8,128)} %copy-done.8), channel_id=1, source_target_pairs={{64,0},{128,64},{192,128},{256,192},{320,256},{384,320},{448,384},... | collective-permute-start | bytes 1572872 | tf_op jit(solution)/shard_map/ppermute | solution.py:234
  83.4 6.7 %collective-permute-start.10 = (f32[128,512]{1,0:T(8,128)S(1)}, f32[128,512]{1,0:T(8,128)S(1)}, u32[]{:S(2)}, u32[]{:S(2)}) collective-permute-start(f32[128,512]{1,0:T(8,128)S(1)} %get-tuple-element.53), channel_id=1, source_target_pairs={{256,448},{192,0},{257,449},{193,1},{258,450},{194,2},{259,451},{1... | collective-permute-start | bytes 786440 | tf_op jit(solution)/shard_map/ppermute | solution.py:241
  84.1 17.4 %collective-permute-start.8 = (f32[128,512]{1,0:T(8,128)S(1)}, f32[128,512]{1,0:T(8,128)S(1)}, u32[]{:S(2)}, u32[]{:S(2)}) collective-permute-start(f32[128,512]{1,0:T(8,128)S(1)} %get-tuple-element.51), channel_id=1, source_target_pairs={{256,320},{320,384},{384,448},{64,0},{128,64},{192,128},{257,321},... | collective-permute-start | bytes 786440 | tf_op jit(solution)/shard_map/ppermute | solution.py:241
  86.3 18.2 %collective-permute-start.9 = (f32[128,512]{1,0:T(8,128)S(1)}, f32[128,512]{1,0:T(8,128)}, u32[]{:S(2)}, u32[]{:S(2)}) collective-permute-start(f32[128,512]{1,0:T(8,128)S(1)} %get-tuple-element.52), channel_id=1, source_target_pairs={{256,384},{320,448},{128,0},{192,64},{257,385},{321,449},{129,1},{... | collective-permute-start | bytes 786440 | tf_op jit(solution)/shard_map/ppermute | solution.py:241
  111.0 30.4 %collective-permute-start.11 = (f32[256,256]{1,0:T(8,128)S(1)}, f32[256,256]{1,0:T(8,128)S(1)}, u32[]{:S(2)}, u32[]{:S(2)}) collective-permute-start(f32[256,256]{1,0:T(8,128)S(1)} %bitcast.72), channel_id=1, source_target_pairs={{0,32},{32,0},{1,33},{33,1},{2,34},{34,2},{3,35},{35,3},{4,36},{36... | collective-permute-start | bytes 786440 | tf_op jit(solution)/shard_map/ppermute | solution.py:11
  141.4 26.6 %collective-permute-start.12 = (f32[256,256]{1,0:T(8,128)S(1)}, f32[256,256]{1,0:T(8,128)S(1)}, u32[]{:S(2)}, u32[]{:S(2)}) collective-permute-start(f32[256,256]{1,0:T(8,128)S(1)} %bitcast.71), channel_id=1, source_target_pairs={{0,32},{32,0},{1,33},{33,1},{2,34},{34,2},{3,35},{35,3},{4,36},{36... | collective-permute-start | bytes 786440 | tf_op jit(solution)/shard_map/ppermute | solution.py:11
  148.3 27.0 %collective-permute-start.16 = (f32[256,256]{1,0:T(8,128)S(1)}, f32[256,256]{1,0:T(8,128)S(1)}, u32[]{:S(2)}, u32[]{:S(2)}) collective-permute-start(f32[256,256]{1,0:T(8,128)S(1)} %collective-permute-done.11.refs_2_), channel_id=1, source_target_pairs={{0,24},{8,0},{16,8},{24,16},{1,25},{9,1},{17,9},{25,17},{2,26},{10... | collective-permute-start | bytes 786440 | tf_op jit(solution)/shard_map/ppermute | solution.py:11
  152.9 25.9 %collective-permute-start.17 = (f32[256,256]{1,0:T(8,128)S(1)}, f32[256,256]{1,0:T(8,128)S(1)}, u32[]{:S(2)}, u32[]{:S(2)}) collective-permute-start(f32[256,256]{1,0:T(8,128)S(1)} %collective-permute-done.11.refs_2_), channel_id=1, source_target_pairs={{0,16},{8,24},{16,0},{24,8},{1,17},{9,25},{17,1},{25,9},{2,18},{10... | collective-permute-start | bytes 786440 | tf_op jit(solution)/shard_map/ppermute | solution.py:11
  155.6 23.2 %collective-permute-start.18 = (f32[256,256]{1,0:T(8,128)S(1)}, f32[256,256]{1,0:T(8,128)}, u32[]{:S(2)}, u32[]{:S(2)}) collective-permute-start(f32[256,256]{1,0:T(8,128)S(1)} %collective-permute-done.11.refs_2_), channel_id=1, source_target_pairs={{0,8},{8,16},{16,24},{24,0},{1,9},{9,17},{17,25},{25,1},{2,10},{10... | collective-permute-start | bytes 786440 | tf_op jit(solution)/shard_map/ppermute | solution.py:11
  168.0 19.6 %collective-permute-start.13 = (f32[256,256]{1,0:T(8,128)S(1)}, f32[256,256]{1,0:T(8,128)S(1)}, u32[]{:S(2)}, u32[]{:S(2)}) collective-permute-start(f32[256,256]{1,0:T(8,128)S(1)} %collective-permute-done.12.refs_1_), channel_id=1, source_target_pairs={{0,24},{8,0},{16,8},{24,16},{1,25},{9,1},{17,9},{25,17},{2,26},{10... | collective-permute-start | bytes 786440 | tf_op jit(solution)/shard_map/ppermute | solution.py:11
  172.6 15.0 %collective-permute-start.14 = (f32[256,256]{1,0:T(8,128)S(1)}, f32[256,256]{1,0:T(8,128)}, u32[]{:S(2)}, u32[]{:S(2)}) collective-permute-start(f32[256,256]{1,0:T(8,128)S(1)} %collective-permute-done.12.refs_1_), channel_id=1, source_target_pairs={{0,16},{8,24},{16,0},{24,8},{1,17},{9,25},{17,1},{25,9},{2,18},{10... | collective-permute-start | bytes 786440 | tf_op jit(solution)/shard_map/ppermute | solution.py:11
  175.3 14.3 %collective-permute-start.15 = (f32[256,256]{1,0:T(8,128)S(1)}, f32[256,256]{1,0:T(8,128)}, u32[]{:S(2)}, u32[]{:S(2)}) collective-permute-start(f32[256,256]{1,0:T(8,128)S(1)} %collective-permute-done.12.refs_1_), channel_id=1, source_target_pairs={{0,8},{8,16},{16,24},{24,0},{1,9},{9,17},{17,25},{25,1},{2,10},{10... | collective-permute-start | bytes 786440 | tf_op jit(solution)/shard_map/ppermute | solution.py:11
  196.2 17.3 %collective-permute-start.19 = (f32[256,256]{1,0:T(8,128)}, f32[256,256]{1,0:T(8,128)S(1)}, u32[]{:S(2)}, u32[]{:S(2)}) collective-permute-start(f32[256,256]{1,0:T(8,128)} %get-tuple-element.71), channel_id=1, source_target_pairs={{0,8},{8,16},{16,24},{24,0},{1,9},{9,17},{17,25},{25,1},{2,10},{10... | collective-permute-start | bytes 786440 | tf_op jit(solution)/shard_map/ppermute | solution.py:11
  198.6 19.4 %collective-permute-start.20 = (f32[256,256]{1,0:T(8,128)}, f32[256,256]{1,0:T(8,128)S(1)}, u32[]{:S(2)}, u32[]{:S(2)}) collective-permute-start(f32[256,256]{1,0:T(8,128)} %get-tuple-element.74), channel_id=1, source_target_pairs={{0,16},{8,24},{16,0},{24,8},{1,17},{9,25},{17,1},{25,9},{2,18},{10... | collective-permute-start | bytes 786440 | tf_op jit(solution)/shard_map/ppermute | solution.py:11
  202.6 15.5 %collective-permute-start.21 = (f32[256,256]{1,0:T(8,128)}, f32[256,256]{1,0:T(8,128)S(1)}, u32[]{:S(2)}, u32[]{:S(2)}) collective-permute-start(f32[256,256]{1,0:T(8,128)} %get-tuple-element.75), channel_id=1, source_target_pairs={{0,24},{8,0},{16,8},{24,16},{1,25},{9,1},{17,9},{25,17},{2,26},{10... | collective-permute-start | bytes 786440 | tf_op jit(solution)/shard_map/ppermute | solution.py:11
  218.1 22.4 %collective-permute-start.22 = (f32[256,256]{1,0:T(8,128)S(1)}, f32[256,256]{1,0:T(8,128)S(1)}, u32[]{:S(2)}, u32[]{:S(2)}) collective-permute-start(f32[256,256]{1,0:T(8,128)S(1)} %add_add_fusion.1), channel_id=1, source_target_pairs={{0,32},{32,0},{1,33},{33,1},{2,34},{34,2},{3,35},{35,3},{4,36},{36... | collective-permute-start | bytes 786440 | tf_op jit(solution)/shard_map/ppermute | solution.py:11
  225.7 15.8 %collective-permute-start.23 = (f32[256,256]{1,0:T(8,128)S(1)}, f32[256,256]{1,0:T(8,128)S(1)}, u32[]{:S(2)}, u32[]{:S(2)}) collective-permute-start(f32[256,256]{1,0:T(8,128)S(1)} %fusion.4), channel_id=1, source_target_pairs={{0,8},{8,16},{16,24},{24,0},{1,9},{9,17},{17,25},{25,1},{2,10},{10... | collective-permute-start | bytes 786440 | tf_op jit(solution)/shard_map/ppermute | solution.py:11
  227.6 13.9 %collective-permute-start.24 = (f32[256,256]{1,0:T(8,128)S(1)}, f32[256,256]{1,0:T(8,128)S(1)}, u32[]{:S(2)}, u32[]{:S(2)}) collective-permute-start(f32[256,256]{1,0:T(8,128)S(1)} %fusion.2), channel_id=1, source_target_pairs={{0,16},{8,24},{16,0},{24,8},{1,17},{9,25},{17,1},{25,9},{2,18},{10... | collective-permute-start | bytes 786440 | tf_op jit(solution)/shard_map/ppermute | solution.py:11
  231.5 12.5 %collective-permute-start.25 = (f32[256,256]{1,0:T(8,128)S(1)}, f32[256,256]{1,0:T(8,128)S(1)}, u32[]{:S(2)}, u32[]{:S(2)}) collective-permute-start(f32[256,256]{1,0:T(8,128)S(1)} %fusion), channel_id=1, source_target_pairs={{0,24},{8,0},{16,8},{24,16},{1,25},{9,1},{17,9},{25,17},{2,26},{10... | collective-permute-start | bytes 786440 | tf_op jit(solution)/shard_map/ppermute | solution.py:11
  (16 other events, 247.4 us)
Sparse Core Ops, SparseCore 0:
  10.1 42.1 all-gather.6
  54.4 38.8 all-gather.4
  108.0 58.0 all-gather.8

commit v7 on v6

--- a/solution.py
+++ b/solution.py
@@ -258,14 +258,14 @@
     far_lower = far_lower.transpose(0, 2, 1)
     own_lower = jnp.take(lower, half * 4 + to_x, axis=0, mode="clip")
     restricted = lax.all_gather(restricted, ("y", "core"), axis=0)
-    top, bottom, far_lower, own_lower = lax.optimization_barrier(
-        (shift(top, "zh", 2, 1), bottom, far_lower, own_lower)
+    number = jnp.arange(4, dtype=jnp.int32)
+    classes = jnp.concatenate([half * 4 + number, (1 - half) * 4 + to_x]).astype(jnp.int32)
+    top, bottom, far_lower, own_lower, classes = lax.optimization_barrier(
+        (shift(top, "zh", 2, 1), bottom, far_lower, own_lower, classes)
     )
     bottom = shift(bottom, "zh", 2, 1)
     far_top = [top] + [shift(top, "x", 4, j) for j in (1, 2, 3)]
 
-    number = jnp.arange(4, dtype=jnp.int32)
-    classes = jnp.concatenate([half * 4 + number, (1 - half) * 4 + to_x]).astype(jnp.int32)
     terms = [(j, 0, 512 * j + 256 * k, k) for j in range(4) for k in (0, 1)]
     terms += [(4 + j, 1 + j, 0, 0) for j in range(4)]
     (inverse_local,) = product(restricted, [near] + far_top, classes, terms)

time: 252 us -> 252 us (level)
  no operation moved by 1% of the time
where the time goes in v7:
time: 252 us; the launch traced here: 251 us
  waiting for transfers between devices  106 us (42%)
  starting transfers between devices  93 us (37%)
  Pallas kernels  18.7 us (7%)
  between operations  14.3 us (6%)
  local copies, waits for them, and re-layouts  12.5 us (5%)
  matrix products  4.52 us (2%)
  other arithmetic  2.57 us (1%)
    ppermute x15, starting transfers between devices, shift(): lax.ppermute(value, axis, [(i, (i - step) % count) for i in range(count)])  62.9 us
    ppermute x15, waiting for transfers between devices, shift(): lax.ppermute(value, axis, [(i, (i - step) % count) for i in range(count)])  44.4 us
    ppermute x4, waiting for transfers between devices, on_device(): up = lax.ppermute(up, 'zl', [(i, i + 1) for i in range(7)])  29.6 us
    ppermute x4, starting transfers between devices, on_device(): up = lax.ppermute(up, 'zl', [(i, i + 1) for i in range(7)])  16.7 us
    ppermute x4, waiting for transfers between devices, on_device(): down = lax.ppermute(down, 'zl', [(i + 1, i) for i in range(7)])  16.7 us
    pallas_call x2, Pallas kernels, product(): pl.pallas_call(functools.partial(product_kernel, terms, len(panels), last...  14.6 us
    ppermute x3, waiting for transfers between devices, on_device(): lax.ppermute(part, 'zl', [(i, i + d) for i in range(4, 8 - d)] + [(i, i -...  13.6 us
    ppermute x4, starting transfers between devices, on_device(): down = lax.ppermute(down, 'zl', [(i + 1, i) for i in range(7)])  7.88 us
  transfers between devices with their start and end apart: 29, of which 17 were waited for; matrix products, arithmetic and copies ran while one was open for 7% of the time, Pallas kernels for 4%

profile of v7, /device:TPU:72, one launch (start us, length us, event | category | flops | bytes accessed | tf_op | source)
XLA Modules:
  0.0 251.3 jit_solution(10534298002821889832)
XLA Ops:
  8.7 3.8 %collective-permute-start = (f32[1024,128]{1,0:T(8,128)}, f32[1024,128]{1,0:T(8,128)S(1)}, u32[]{:S(2)}, u32[]{:S(2)}) collective-permute-start(f32[1024,128]{1,0:T(8,128)} %bitcast.68), channel_id=1, source_target_pairs={{0,64},{64,128},{128,192},{192,256},{256,320},{320,384},{384,448},... | collective-permute-start | bytes 1572872 | tf_op jit(solution)/shard_map/ppermute | solution.py:233
  14.6 9.9 %collective-permute-done.refs_1_ = f32[1024,128]{1,0:T(8,128)S(1)} collective-permute-done((f32[1024,128]{1,0:T(8,128)}, f32[1024,128]{1,0:T(8,128)S(1)}, u32[]{:S(2)}, u32[]{:S(2)}) %collective-permute-start) | collective-permute-done | bytes 524320 | tf_op jit(solution)/shard_map/ppermute | solution.py:233
  24.5 4.9 %collective-permute-done.1.refs_2_ = f32[1024,128]{1,0:T(8,128)S(1)} collective-permute-done((f32[1024,128]{1,0:T(8,128)}, f32[1024,128]{1,0:T(8,128)S(1)}, u32[]{:S(2)}, u32[]{:S(2)}) %collective-permute-start.1) | collective-permute-done | bytes 524320 | tf_op jit(solution)/shard_map/ppermute | solution.py:234
  29.4 4.8 %collective-permute-start.2 = (f32[1024,128]{1,0:T(8,128)S(1)}, f32[1024,128]{1,0:T(8,128)S(1)}, u32[]{:S(2)}, u32[]{:S(2)}) collective-permute-start(f32[1024,128]{1,0:T(8,128)S(1)} %collective-permute-done.refs_1_), channel_id=1, source_target_pairs={{0,64},{64,128},{128,192},{192,256},{256,320},{320,384},{384,448},... | collective-permute-start | bytes 1572872 | tf_op jit(solution)/shard_map/ppermute | solution.py:233
  37.3 7.0 %collective-permute-done.2.refs_3_ = f32[1024,128]{1,0:T(8,128)S(1)} collective-permute-done((f32[1024,128]{1,0:T(8,128)S(1)}, f32[1024,128]{1,0:T(8,128)S(1)}, u32[]{:S(2)}, u32[]{:S(2)}) %collective-permute-start.2) | collective-permute-done | bytes 524320 | tf_op jit(solution)/shard_map/ppermute | solution.py:233
  44.2 4.1 %collective-permute-done.3.refs_4_ = f32[1024,128]{1,0:T(8,128)S(1)} collective-permute-done((f32[1024,128]{1,0:T(8,128)S(1)}, f32[1024,128]{1,0:T(8,128)S(1)}, u32[]{:S(2)}, u32[]{:S(2)}) %collective-permute-start.3) | collective-permute-done | bytes 524320 | tf_op jit(solution)/shard_map/ppermute | solution.py:234
  48.4 4.2 %collective-permute-start.4 = (f32[1024,128]{1,0:T(8,128)S(1)}, f32[1024,128]{1,0:T(8,128)}, u32[]{:S(2)}, u32[]{:S(2)}) collective-permute-start(f32[1024,128]{1,0:T(8,128)S(1)} %collective-permute-done.2.refs_3_), channel_id=1, source_target_pairs={{0,64},{64,128},{128,192},{192,256},{256,320},{320,384},{384,448},... | collective-permute-start | bytes 1572872 | tf_op jit(solution)/shard_map/ppermute | solution.py:233
  55.4 6.4 %collective-permute-done.4.refs_5_ = f32[1024,128]{1,0:T(8,128)} collective-permute-done((f32[1024,128]{1,0:T(8,128)S(1)}, f32[1024,128]{1,0:T(8,128)}, u32[]{:S(2)}, u32[]{:S(2)}) %collective-permute-start.4) | collective-permute-done | bytes 524320 | tf_op jit(solution)/shard_map/ppermute | solution.py:233
  61.7 4.0 %collective-permute-done.5.refs_6_ = f32[1024,128]{1,0:T(8,128)S(1)} collective-permute-done((f32[1024,128]{1,0:T(8,128)S(1)}, f32[1024,128]{1,0:T(8,128)S(1)}, u32[]{:S(2)}, u32[]{:S(2)}) %collective-permute-start.5) | collective-permute-done | bytes 524320 | tf_op jit(solution)/shard_map/ppermute | solution.py:234
  66.6 3.8 %collective-permute-start.6 = (f32[1024,128]{1,0:T(8,128)}, f32[1024,128]{1,0:T(8,128)S(1)}, u32[]{:S(2)}, u32[]{:S(2)}) collective-permute-start(f32[1024,128]{1,0:T(8,128)} %collective-permute-done.4.refs_5_), channel_id=1, source_target_pairs={{0,64},{64,128},{128,192},{192,256},{256,320},{320,384},{384,448},... | collective-permute-start | bytes 1572872 | tf_op jit(solution)/shard_map/ppermute | solution.py:233
  72.7 6.4 %collective-permute-done.6.up.refs_7_ = f32[1024,128]{1,0:T(8,128)S(1)} collective-permute-done((f32[1024,128]{1,0:T(8,128)}, f32[1024,128]{1,0:T(8,128)S(1)}, u32[]{:S(2)}, u32[]{:S(2)}) %collective-permute-start.6) | collective-permute-done | bytes 524320 | tf_op jit(solution)/shard_map/ppermute | solution.py:233
  79.1 3.6 %collective-permute-done.7.down.refs_8_ = f32[1024,128]{1,0:T(8,128)S(1)} collective-permute-done((f32[1024,128]{1,0:T(8,128)}, f32[1024,128]{1,0:T(8,128)S(1)}, u32[]{:S(2)}, u32[]{:S(2)}) %collective-permute-start.7) | collective-permute-done | bytes 524320 | tf_op jit(solution)/shard_map/ppermute | solution.py:234
  90.2 11.3 %collective-permute-done.8.refs_9_ = f32[128,512]{1,0:T(8,128)S(1)} collective-permute-done((f32[128,512]{1,0:T(8,128)S(1)}, f32[128,512]{1,0:T(8,128)S(1)}, u32[]{:S(2)}, u32[]{:S(2)}) %collective-permute-start.8) | collective-permute-done | bytes 262176 | tf_op jit(solution)/shard_map/ppermute | solution.py:241
  104.6 3.3 %pick.1 = f32[2,512,256]{2,1,0:T(8,128)} custom-call(s32[20]{0:T(128)} %pad_add_fusion.info, f32[1024,128]{1,0:T(8,128)} %bitcast.70, f32[1024,128]{1,0:T(8,128)} %copy-done.4, f32[1024,128]{1,0:T(8,128)} %copy-done.5, f32[1024,128]{1,0:T(8,128)} %copy-done.6, f32[1024,128]{1,0:T(8,128)} %copy-done.7, f32[1024,128]{1,0:T(8,128)} %collective-permute-done.4.refs_5_, ...), custom_call_target="tpu_custom_call" | custom-call | bytes 3145728 | tf_op jit(solution)/shard_map/pick/pallas_call | solution.py:98
  108.1 2.9 %gather_fusion.1 = f32[4,512,256]{2,1,0:T(8,128)S(1)} fusion(f32[8,512,256]{2,1,0:T(8,128)} %all-gather.5.cloned.1.call-done, s32[1024]{0:T(1024)S(1)} %pad_clamp_fusion.1), kind=kCustom, calls=%fused_computation.1 | custom fusion | bytes 4194320 | tf_op jit(solution)/shard_map/jit(_take)/gather | solution.py:256
  110.9 10.0 %collective-permute-start.11 = (f32[256,256]{1,0:T(8,128)S(1)}, f32[256,256]{1,0:T(8,128)S(1)}, u32[]{:S(2)}, u32[]{:S(2)}) collective-permute-start(f32[256,256]{1,0:T(8,128)S(1)} %bitcast.71), channel_id=1, source_target_pairs={{0,32},{32,0},{1,33},{33,1},{2,34},{34,2},{3,35},{35,3},{4,36},{36... | collective-permute-start | bytes 786440 | tf_op jit(solution)/shard_map/ppermute | solution.py:11
  123.5 2.9 %gather_fusion.2 = f32[4,512,256]{2,1,0:T(8,128)S(1)} fusion(f32[8,512,256]{2,1,0:T(8,128)} %all-gather.5.cloned.1.call-done, s32[1024]{0:T(1024)S(1)} %pad_clamp_fusion), kind=kCustom, calls=%fused_computation.2 | custom fusion | bytes 4194320 | tf_op jit(solution)/shard_map/jit(_take)/gather | solution.py:259
  126.3 14.9 %collective-permute-done.11.refs_2_ = f32[256,256]{1,0:T(8,128)S(1)} collective-permute-done((f32[256,256]{1,0:T(8,128)S(1)}, f32[256,256]{1,0:T(8,128)S(1)}, u32[]{:S(2)}, u32[]{:S(2)}) %collective-permute-start.11) | collective-permute-done | bytes 262176 | tf_op jit(solution)/shard_map/ppermute | solution.py:11
  141.3 6.9 %collective-permute-start.12 = (f32[256,256]{1,0:T(8,128)}, f32[256,256]{1,0:T(8,128)S(1)}, u32[]{:S(2)}, u32[]{:S(2)}) collective-permute-start(f32[256,256]{1,0:T(8,128)} %bitcast.7), channel_id=1, source_target_pairs={{0,32},{32,0},{1,33},{33,1},{2,34},{34,2},{3,35},{35,3},{4,36},{36... | collective-permute-start | bytes 786440 | tf_op jit(solution)/shard_map/ppermute | solution.py:11
  148.2 4.8 %collective-permute-start.16 = (f32[256,256]{1,0:T(8,128)S(1)}, f32[256,256]{1,0:T(8,128)S(1)}, u32[]{:S(2)}, u32[]{:S(2)}) collective-permute-start(f32[256,256]{1,0:T(8,128)S(1)} %collective-permute-done.11.refs_2_), channel_id=1, source_target_pairs={{0,24},{8,0},{16,8},{24,16},{1,25},{9,1},{17,9},{25,17},{2,26},{10... | collective-permute-start | bytes 786440 | tf_op jit(solution)/shard_map/ppermute | solution.py:11
  155.6 2.8 %collective-permute-start.18 = (f32[256,256]{1,0:T(8,128)S(1)}, f32[256,256]{1,0:T(8,128)}, u32[]{:S(2)}, u32[]{:S(2)}) collective-permute-start(f32[256,256]{1,0:T(8,128)S(1)} %collective-permute-done.11.refs_2_), channel_id=1, source_target_pairs={{0,8},{8,16},{16,24},{24,0},{1,9},{9,17},{17,25},{25,1},{2,10},{10... | collective-permute-start | bytes 786440 | tf_op jit(solution)/shard_map/ppermute | solution.py:11
  158.4 9.5 %collective-permute-done.12.refs_1_ = f32[256,256]{1,0:T(8,128)S(1)} collective-permute-done((f32[256,256]{1,0:T(8,128)}, f32[256,256]{1,0:T(8,128)S(1)}, u32[]{:S(2)}, u32[]{:S(2)}) %collective-permute-start.12) | collective-permute-done | bytes 262176 | tf_op jit(solution)/shard_map/ppermute | solution.py:11
  167.9 4.8 %collective-permute-start.13 = (f32[256,256]{1,0:T(8,128)S(1)}, f32[256,256]{1,0:T(8,128)S(1)}, u32[]{:S(2)}, u32[]{:S(2)}) collective-permute-start(f32[256,256]{1,0:T(8,128)S(1)} %collective-permute-done.12.refs_1_), channel_id=1, source_target_pairs={{0,24},{8,0},{16,8},{24,16},{1,25},{9,1},{17,9},{25,17},{2,26},{10... | collective-permute-start | bytes 786440 | tf_op jit(solution)/shard_map/ppermute | solution.py:11
  178.9 8.2 %product.2.refs_5_ = f32[512,256]{1,0:T(8,128)} custom-call(s32[8]{0:T(128)} %pad_add_fusion.3.classes, f32[8,2,512,256]{3,2,1,0:T(8,128)} %bitcast.61, f32[2048,256]{1,0:T(8,128)} %bitcast.67, f32[256,256]{1,0:T(8,128)} %copy-done.10, f32[256,256]{1,0:T(8,128)} %copy-done.14, f32[256,256]{1,0:T(8,128)} %copy-done.16, f32[256,256]{1,0:T(8,128)} %collective-permute-done.18.refs_5_), custom_call_target="tpu_custom_call" | custom-call | flops 2415919104 | bytes 9437184 | tf_op jit(solution)/shard_map/product/pallas_call | solution.py:184
  189.8 6.5 %product.3 = (f32[512,256]{1,0:T(8,128)}, f32[256,256]{1,0:T(8,128)}, f32[256,256]{1,0:T(8,128)}, f32[256,256]{1,0:T(8,128)}, f32[256,256]{1,0:T(8,128)}) custom-call(s32[8]{0:T(128)} %pad_add_fusion.3.classes, f32[8,2,512,256]{3,2,1,0:T(8,128)} %bitcast.62, f32[256,256]{1,0:T(8,128)} %copy-done.11, f32[256,256]{1,0:T(8,128)} %copy-done.12, ...), custom_call_target="tpu_custom_call" | custom-call | flops 805306368 | bytes 3145728 | tf_op jit(solution)/shard_map/product/pallas_call | solution.py:184
  198.3 4.0 %collective-permute-start.20 = (f32[256,256]{1,0:T(8,128)}, f32[256,256]{1,0:T(8,128)S(1)}, u32[]{:S(2)}, u32[]{:S(2)}) collective-permute-start(f32[256,256]{1,0:T(8,128)} %get-tuple-element.76), channel_id=1, source_target_pairs={{0,16},{8,24},{16,0},{24,8},{1,17},{9,25},{17,1},{25,9},{2,18},{10... | collective-permute-start | bytes 786440 | tf_op jit(solution)/shard_map/ppermute | solution.py:11
  202.3 3.3 %collective-permute-start.21 = (f32[256,256]{1,0:T(8,128)}, f32[256,256]{1,0:T(8,128)S(1)}, u32[]{:S(2)}, u32[]{:S(2)}) collective-permute-start(f32[256,256]{1,0:T(8,128)} %get-tuple-element.77), channel_id=1, source_target_pairs={{0,24},{8,0},{16,8},{24,16},{1,25},{9,1},{17,9},{25,17},{2,26},{10... | collective-permute-start | bytes 786440 | tf_op jit(solution)/shard_map/ppermute | solution.py:11
  205.6 7.9 %collective-permute-done.19 = f32[256,256]{1,0:T(8,128)S(1)} collective-permute-done((f32[256,256]{1,0:T(8,128)}, f32[256,256]{1,0:T(8,128)S(1)}, u32[]{:S(2)}, u32[]{:S(2)}) %collective-permute-start.19) | collective-permute-done | bytes 262176 | tf_op jit(solution)/shard_map/ppermute | solution.py:11
  218.2 7.4 %collective-permute-start.22 = (f32[256,256]{1,0:T(8,128)S(1)}, f32[256,256]{1,0:T(8,128)S(1)}, u32[]{:S(2)}, u32[]{:S(2)}) collective-permute-start(f32[256,256]{1,0:T(8,128)S(1)} %add_add_fusion.1), channel_id=1, source_target_pairs={{0,32},{32,0},{1,33},{33,1},{2,34},{34,2},{3,35},{35,3},{4,36},{36... | collective-permute-start | bytes 786440 | tf_op jit(solution)/shard_map/ppermute | solution.py:11
  227.6 3.9 %collective-permute-start.24 = (f32[256,256]{1,0:T(8,128)S(1)}, f32[256,256]{1,0:T(8,128)S(1)}, u32[]{:S(2)}, u32[]{:S(2)}) collective-permute-start(f32[256,256]{1,0:T(8,128)S(1)} %fusion.2), channel_id=1, source_target_pairs={{0,16},{8,24},{16,0},{24,8},{1,17},{9,25},{17,1},{25,9},{2,18},{10... | collective-permute-start | bytes 786440 | tf_op jit(solution)/shard_map/ppermute | solution.py:11
  231.5 3.1 %collective-permute-start.25 = (f32[256,256]{1,0:T(8,128)S(1)}, f32[256,256]{1,0:T(8,128)S(1)}, u32[]{:S(2)}, u32[]{:S(2)}) collective-permute-start(f32[256,256]{1,0:T(8,128)S(1)} %fusion), channel_id=1, source_target_pairs={{0,24},{8,0},{16,8},{24,16},{1,25},{9,1},{17,9},{25,17},{2,26},{10... | collective-permute-start | bytes 786440 | tf_op jit(solution)/shard_map/ppermute | solution.py:11
  234.6 5.9 %collective-permute-done.22 = f32[256,256]{1,0:T(8,128)S(1)} collective-permute-done((f32[256,256]{1,0:T(8,128)S(1)}, f32[256,256]{1,0:T(8,128)S(1)}, u32[]{:S(2)}, u32[]{:S(2)}) %collective-permute-start.22) | collective-permute-done | bytes 262176 | tf_op jit(solution)/shard_map/ppermute | solution.py:11
  (107 shorter events, 49.7 us)
Async XLA Ops:
  7.2 82.3 %copy-start.3 = (f32[1,4,1,128,256]{4,3,2,1,0:T(8,128)S(1)}, f32[1,4,1,128,256]{4,3,2,1,0:T(8,128)}, u32[]{:S(2)}) copy-start(f32[1,4,1,128,256]{4,3,2,1,0:T(8,128)} %param.6) | copy-start | bytes 1572868
  7.2 97.4 %all-gather.7.cloned.1.call-start = ((), (), s32[]{:S(2)}) async-start(), calls=%async_computation.1 | async-start | bytes 2621440 | tf_op jit(solution)/shard_map/all_gather | solution.py:228
  7.9 96.6 %all-gather.5.cloned.1.call-start = ((), (), s32[]{:S(2)}) async-start(), calls=%async_computation | async-start | bytes 4718592 | tf_op jit(solution)/shard_map/all_gather | solution.py:227
  8.7 170.2 %all-gather.9.cloned.1.call-start = ((), (), s32[]{:S(2)}) async-start(), calls=%async_computation.2 | async-start | bytes 9437184 | tf_op jit(solution)/shard_map/all_gather | solution.py:260
  8.7 15.8 %collective-permute-start = (f32[1024,128]{1,0:T(8,128)}, f32[1024,128]{1,0:T(8,128)S(1)}, u32[]{:S(2)}, u32[]{:S(2)}) collective-permute-start(f32[1024,128]{1,0:T(8,128)} %bitcast.68), channel_id=1, source_target_pairs={{0,64},{64,128},{128,192},{192,256},{256,320},{320,384},{384,448},... | collective-permute-start | bytes 1572872 | tf_op jit(solution)/shard_map/ppermute | solution.py:233
  12.5 16.9 %collective-permute-start.1 = (f32[1024,128]{1,0:T(8,128)}, f32[1024,128]{1,0:T(8,128)S(1)}, u32[]{:S(2)}, u32[]{:S(2)}) collective-permute-start(f32[1024,128]{1,0:T(8,128)} %bitcast.69), channel_id=1, source_target_pairs={{64,0},{128,64},{192,128},{256,192},{320,256},{384,320},{448,384},... | collective-permute-start | bytes 1572872 | tf_op jit(solution)/shard_map/ppermute | solution.py:234
  24.5 80.1 %copy-start.4 = (f32[1024,128]{1,0:T(8,128)}, f32[1024,128]{1,0:T(8,128)S(1)}, u32[]{:S(2)}) copy-start(f32[1024,128]{1,0:T(8,128)S(1)} %collective-permute-done.refs_1_) | copy-start | bytes 1572868
  29.4 75.1 %copy-start.5 = (f32[1024,128]{1,0:T(8,128)}, f32[1024,128]{1,0:T(8,128)S(1)}, u32[]{:S(2)}) copy-start(f32[1024,128]{1,0:T(8,128)S(1)} %collective-permute-done.1.refs_2_) | copy-start | bytes 1572868
  29.4 14.8 %collective-permute-start.2 = (f32[1024,128]{1,0:T(8,128)S(1)}, f32[1024,128]{1,0:T(8,128)S(1)}, u32[]{:S(2)}, u32[]{:S(2)}) collective-permute-start(f32[1024,128]{1,0:T(8,128)S(1)} %collective-permute-done.refs_1_), channel_id=1, source_target_pairs={{0,64},{64,128},{128,192},{192,256},{256,320},{320,384},{384,448},... | collective-permute-start | bytes 1572872 | tf_op jit(solution)/shard_map/ppermute | solution.py:233
  34.3 14.1 %collective-permute-start.3 = (f32[1024,128]{1,0:T(8,128)S(1)}, f32[1024,128]{1,0:T(8,128)S(1)}, u32[]{:S(2)}, u32[]{:S(2)}) collective-permute-start(f32[1024,128]{1,0:T(8,128)S(1)} %collective-permute-done.1.refs_2_), channel_id=1, source_target_pairs={{64,0},{128,64},{192,128},{256,192},{320,256},{384,320},{448,384},... | collective-permute-start | bytes 1572872 | tf_op jit(solution)/shard_map/ppermute | solution.py:234
  48.4 13.4 %collective-permute-start.4 = (f32[1024,128]{1,0:T(8,128)S(1)}, f32[1024,128]{1,0:T(8,128)}, u32[]{:S(2)}, u32[]{:S(2)}) collective-permute-start(f32[1024,128]{1,0:T(8,128)S(1)} %collective-permute-done.2.refs_3_), channel_id=1, source_target_pairs={{0,64},{64,128},{128,192},{192,256},{256,320},{320,384},{384,448},... | collective-permute-start | bytes 1572872 | tf_op jit(solution)/shard_map/ppermute | solution.py:233
  52.6 13.2 %collective-permute-start.5 = (f32[1024,128]{1,0:T(8,128)S(1)}, f32[1024,128]{1,0:T(8,128)S(1)}, u32[]{:S(2)}, u32[]{:S(2)}) collective-permute-start(f32[1024,128]{1,0:T(8,128)S(1)} %collective-permute-done.3.refs_4_), channel_id=1, source_target_pairs={{64,0},{128,64},{192,128},{256,192},{320,256},{384,320},{448,384},... | collective-permute-start | bytes 1572872 | tf_op jit(solution)/shard_map/ppermute | solution.py:234
  66.6 12.5 %collective-permute-start.6 = (f32[1024,128]{1,0:T(8,128)}, f32[1024,128]{1,0:T(8,128)S(1)}, u32[]{:S(2)}, u32[]{:S(2)}) collective-permute-start(f32[1024,128]{1,0:T(8,128)} %collective-permute-done.4.refs_5_), channel_id=1, source_target_pairs={{0,64},{64,128},{128,192},{192,256},{256,320},{320,384},{384,448},... | collective-permute-start | bytes 1572872 | tf_op jit(solution)/shard_map/ppermute | solution.py:233
  70.4 12.2 %collective-permute-start.7 = (f32[1024,128]{1,0:T(8,128)}, f32[1024,128]{1,0:T(8,128)S(1)}, u32[]{:S(2)}, u32[]{:S(2)}) collective-permute-start(f32[1024,128]{1,0:T(8,128)} %copy-done.8), channel_id=1, source_target_pairs={{64,0},{128,64},{192,128},{256,192},{320,256},{384,320},{448,384},... | collective-permute-start | bytes 1572872 | tf_op jit(solution)/shard_map/ppermute | solution.py:234
  83.4 6.8 %collective-permute-start.10 = (f32[128,512]{1,0:T(8,128)S(1)}, f32[128,512]{1,0:T(8,128)S(1)}, u32[]{:S(2)}, u32[]{:S(2)}) collective-permute-start(f32[128,512]{1,0:T(8,128)S(1)} %get-tuple-element.54), channel_id=1, source_target_pairs={{256,448},{192,0},{257,449},{193,1},{258,450},{194,2},{259,451},{1... | collective-permute-start | bytes 786440 | tf_op jit(solution)/shard_map/ppermute | solution.py:241
  84.1 17.4 %collective-permute-start.8 = (f32[128,512]{1,0:T(8,128)S(1)}, f32[128,512]{1,0:T(8,128)S(1)}, u32[]{:S(2)}, u32[]{:S(2)}) collective-permute-start(f32[128,512]{1,0:T(8,128)S(1)} %get-tuple-element.52), channel_id=1, source_target_pairs={{256,320},{320,384},{384,448},{64,0},{128,64},{192,128},{257,321},... | collective-permute-start | bytes 786440 | tf_op jit(solution)/shard_map/ppermute | solution.py:241
  86.3 18.2 %collective-permute-start.9 = (f32[128,512]{1,0:T(8,128)S(1)}, f32[128,512]{1,0:T(8,128)}, u32[]{:S(2)}, u32[]{:S(2)}) collective-permute-start(f32[128,512]{1,0:T(8,128)S(1)} %get-tuple-element.53), channel_id=1, source_target_pairs={{256,384},{320,448},{128,0},{192,64},{257,385},{321,449},{129,1},{... | collective-permute-start | bytes 786440 | tf_op jit(solution)/shard_map/ppermute | solution.py:241
  110.9 30.3 %collective-permute-start.11 = (f32[256,256]{1,0:T(8,128)S(1)}, f32[256,256]{1,0:T(8,128)S(1)}, u32[]{:S(2)}, u32[]{:S(2)}) collective-permute-start(f32[256,256]{1,0:T(8,128)S(1)} %bitcast.71), channel_id=1, source_target_pairs={{0,32},{32,0},{1,33},{33,1},{2,34},{34,2},{3,35},{35,3},{4,36},{36... | collective-permute-start | bytes 786440 | tf_op jit(solution)/shard_map/ppermute | solution.py:11
  141.3 26.7 %collective-permute-start.12 = (f32[256,256]{1,0:T(8,128)}, f32[256,256]{1,0:T(8,128)S(1)}, u32[]{:S(2)}, u32[]{:S(2)}) collective-permute-start(f32[256,256]{1,0:T(8,128)} %bitcast.7), channel_id=1, source_target_pairs={{0,32},{32,0},{1,33},{33,1},{2,34},{34,2},{3,35},{35,3},{4,36},{36... | collective-permute-start | bytes 786440 | tf_op jit(solution)/shard_map/ppermute | solution.py:11
  148.2 27.1 %collective-permute-start.16 = (f32[256,256]{1,0:T(8,128)S(1)}, f32[256,256]{1,0:T(8,128)S(1)}, u32[]{:S(2)}, u32[]{:S(2)}) collective-permute-start(f32[256,256]{1,0:T(8,128)S(1)} %collective-permute-done.11.refs_2_), channel_id=1, source_target_pairs={{0,24},{8,0},{16,8},{24,16},{1,25},{9,1},{17,9},{25,17},{2,26},{10... | collective-permute-start | bytes 786440 | tf_op jit(solution)/shard_map/ppermute | solution.py:11
  153.0 25.2 %collective-permute-start.17 = (f32[256,256]{1,0:T(8,128)S(1)}, f32[256,256]{1,0:T(8,128)S(1)}, u32[]{:S(2)}, u32[]{:S(2)}) collective-permute-start(f32[256,256]{1,0:T(8,128)S(1)} %collective-permute-done.11.refs_2_), channel_id=1, source_target_pairs={{0,16},{8,24},{16,0},{24,8},{1,17},{9,25},{17,1},{25,9},{2,18},{10... | collective-permute-start | bytes 786440 | tf_op jit(solution)/shard_map/ppermute | solution.py:11
  155.6 23.3 %collective-permute-start.18 = (f32[256,256]{1,0:T(8,128)S(1)}, f32[256,256]{1,0:T(8,128)}, u32[]{:S(2)}, u32[]{:S(2)}) collective-permute-start(f32[256,256]{1,0:T(8,128)S(1)} %collective-permute-done.11.refs_2_), channel_id=1, source_target_pairs={{0,8},{8,16},{16,24},{24,0},{1,9},{9,17},{17,25},{25,1},{2,10},{10... | collective-permute-start | bytes 786440 | tf_op jit(solution)/shard_map/ppermute | solution.py:11
  167.9 19.1 %collective-permute-start.13 = (f32[256,256]{1,0:T(8,128)S(1)}, f32[256,256]{1,0:T(8,128)S(1)}, u32[]{:S(2)}, u32[]{:S(2)}) collective-permute-start(f32[256,256]{1,0:T(8,128)S(1)} %collective-permute-done.12.refs_1_), channel_id=1, source_target_pairs={{0,24},{8,0},{16,8},{24,16},{1,25},{9,1},{17,9},{25,17},{2,26},{10... | collective-permute-start | bytes 786440 | tf_op jit(solution)/shard_map/ppermute | solution.py:11
  172.7 14.4 %collective-permute-start.14 = (f32[256,256]{1,0:T(8,128)S(1)}, f32[256,256]{1,0:T(8,128)S(1)}, u32[]{:S(2)}, u32[]{:S(2)}) collective-permute-start(f32[256,256]{1,0:T(8,128)S(1)} %collective-permute-done.12.refs_1_), channel_id=1, source_target_pairs={{0,16},{8,24},{16,0},{24,8},{1,17},{9,25},{17,1},{25,9},{2,18},{10... | collective-permute-start | bytes 786440 | tf_op jit(solution)/shard_map/ppermute | solution.py:11
  175.3 14.5 %collective-permute-start.15 = (f32[256,256]{1,0:T(8,128)S(1)}, f32[256,256]{1,0:T(8,128)}, u32[]{:S(2)}, u32[]{:S(2)}) collective-permute-start(f32[256,256]{1,0:T(8,128)S(1)} %collective-permute-done.12.refs_1_), channel_id=1, source_target_pairs={{0,8},{8,16},{16,24},{24,0},{1,9},{9,17},{17,25},{25,1},{2,10},{10... | collective-permute-start | bytes 786440 | tf_op jit(solution)/shard_map/ppermute | solution.py:11
  196.3 17.3 %collective-permute-start.19 = (f32[256,256]{1,0:T(8,128)}, f32[256,256]{1,0:T(8,128)S(1)}, u32[]{:S(2)}, u32[]{:S(2)}) collective-permute-start(f32[256,256]{1,0:T(8,128)} %get-tuple-element.73), channel_id=1, source_target_pairs={{0,8},{8,16},{16,24},{24,0},{1,9},{9,17},{17,25},{25,1},{2,10},{10... | collective-permute-start | bytes 786440 | tf_op jit(solution)/shard_map/ppermute | solution.py:11
  198.3 19.8 %collective-permute-start.20 = (f32[256,256]{1,0:T(8,128)}, f32[256,256]{1,0:T(8,128)S(1)}, u32[]{:S(2)}, u32[]{:S(2)}) collective-permute-start(f32[256,256]{1,0:T(8,128)} %get-tuple-element.76), channel_id=1, source_target_pairs={{0,16},{8,24},{16,0},{24,8},{1,17},{9,25},{17,1},{25,9},{2,18},{10... | collective-permute-start | bytes 786440 | tf_op jit(solution)/shard_map/ppermute | solution.py:11
  202.3 15.9 %collective-permute-start.21 = (f32[256,256]{1,0:T(8,128)}, f32[256,256]{1,0:T(8,128)S(1)}, u32[]{:S(2)}, u32[]{:S(2)}) collective-permute-start(f32[256,256]{1,0:T(8,128)} %get-tuple-element.77), channel_id=1, source_target_pairs={{0,24},{8,0},{16,8},{24,16},{1,25},{9,1},{17,9},{25,17},{2,26},{10... | collective-permute-start | bytes 786440 | tf_op jit(solution)/shard_map/ppermute | solution.py:11
  218.2 22.3 %collective-permute-start.22 = (f32[256,256]{1,0:T(8,128)S(1)}, f32[256,256]{1,0:T(8,128)S(1)}, u32[]{:S(2)}, u32[]{:S(2)}) collective-permute-start(f32[256,256]{1,0:T(8,128)S(1)} %add_add_fusion.1), channel_id=1, source_target_pairs={{0,32},{32,0},{1,33},{33,1},{2,34},{34,2},{3,35},{35,3},{4,36},{36... | collective-permute-start | bytes 786440 | tf_op jit(solution)/shard_map/ppermute | solution.py:11
  225.6 15.8 %collective-permute-start.23 = (f32[256,256]{1,0:T(8,128)S(1)}, f32[256,256]{1,0:T(8,128)S(1)}, u32[]{:S(2)}, u32[]{:S(2)}) collective-permute-start(f32[256,256]{1,0:T(8,128)S(1)} %fusion.4), channel_id=1, source_target_pairs={{0,8},{8,16},{16,24},{24,0},{1,9},{9,17},{17,25},{25,1},{2,10},{10... | collective-permute-start | bytes 786440 | tf_op jit(solution)/shard_map/ppermute | solution.py:11
  227.6 13.9 %collective-permute-start.24 = (f32[256,256]{1,0:T(8,128)S(1)}, f32[256,256]{1,0:T(8,128)S(1)}, u32[]{:S(2)}, u32[]{:S(2)}) collective-permute-start(f32[256,256]{1,0:T(8,128)S(1)} %fusion.2), channel_id=1, source_target_pairs={{0,16},{8,24},{16,0},{24,8},{1,17},{9,25},{17,1},{25,9},{2,18},{10... | collective-permute-start | bytes 786440 | tf_op jit(solution)/shard_map/ppermute | solution.py:11
  231.5 12.5 %collective-permute-start.25 = (f32[256,256]{1,0:T(8,128)S(1)}, f32[256,256]{1,0:T(8,128)S(1)}, u32[]{:S(2)}, u32[]{:S(2)}) collective-permute-start(f32[256,256]{1,0:T(8,128)S(1)} %fusion), channel_id=1, source_target_pairs={{0,24},{8,0},{16,8},{24,16},{1,25},{9,1},{17,9},{25,17},{2,26},{10... | collective-permute-start | bytes 786440 | tf_op jit(solution)/shard_map/ppermute | solution.py:11
  (16 other events, 247.5 us)
Sparse Core Ops, SparseCore 0:
  10.1 42.1 all-gather.6
  54.4 38.8 all-gather.4
  108.1 58.0 all-gather.8

commit v8 on v7

--- a/solution.py
+++ b/solution.py
@@ -252,9 +252,8 @@
     )
 
     restricted = pick(rows, cut, source, places)
-    restricted, lower = lax.optimization_barrier((restricted, lower))
+    restricted, lower, top = lax.optimization_barrier((restricted, lower, top))
     far_lower = jnp.take(lower, (1 - half) * 4 + to_x, axis=0, mode="clip")
-    far_lower, lower, top = lax.optimization_barrier((far_lower, lower, top))
     far_lower = far_lower.transpose(0, 2, 1)
     own_lower = jnp.take(lower, half * 4 + to_x, axis=0, mode="clip")
     restricted = lax.all_gather(restricted, ("y", "core"), axis=0)

time: 252 us -> 253 us (level)
  the two profiles are of different devices: /device:TPU:72 before, /device:TPU:65 now
where the time goes in v8:
time: 253 us; the launch traced here: 252 us
  waiting for transfers between devices  111 us (44%)
  starting transfers between devices  88.1 us (35%)
  Pallas kernels  18.9 us (7%)
  between operations  14.3 us (6%)
  local copies, waits for them, and re-layouts  12.5 us (5%)
  matrix products  4.52 us (2%)
  other arithmetic  2.56 us (1%)
    ppermute x15, starting transfers between devices, shift(): lax.ppermute(value, axis, [(i, (i - step) % count) for i in range(count)])  59.5 us
    ppermute x15, waiting for transfers between devices, shift(): lax.ppermute(value, axis, [(i, (i - step) % count) for i in range(count)])  50.7 us
    ppermute x4, waiting for transfers between devices, on_device(): up = lax.ppermute(up, 'zl', [(i, i + 1) for i in range(7)])  27.5 us
    ppermute x4, waiting for transfers between devices, on_device(): down = lax.ppermute(down, 'zl', [(i + 1, i) for i in range(7)])  15.8 us
    ppermute x3, waiting for transfers between devices, on_device(): lax.ppermute(part, 'zl', [(i, i + d) for i in range(4, 8 - d)] + [(i, i -...  15.7 us
    ppermute x4, starting transfers between devices, on_device(): up = lax.ppermute(up, 'zl', [(i, i + 1) for i in range(7)])  15.5 us
    pallas_call x2, Pallas kernels, product(): pl.pallas_call(functools.partial(product_kernel, terms, len(panels), last...  14.6 us
    ppermute x4, starting transfers between devices, on_device(): down = lax.ppermute(down, 'zl', [(i + 1, i) for i in range(7)])  7.68 us
  transfers between devices with their start and end apart: 29, of which 15 were waited for; matrix products, arithmetic and copies ran while one was open for 7% of the time, Pallas kernels for 4%

profile of v8, /device:TPU:65, one launch (start us, length us, event | category | flops | bytes accessed | tf_op | source)
XLA Modules:
  0.0 252.0 jit_solution(2115751824021015798)
XLA Ops:
  8.7 3.5 %collective-permute-start = (f32[1024,128]{1,0:T(8,128)}, f32[1024,128]{1,0:T(8,128)S(1)}, u32[]{:S(2)}, u32[]{:S(2)}) collective-permute-start(f32[1024,128]{1,0:T(8,128)} %bitcast.68), channel_id=1, source_target_pairs={{0,64},{64,128},{128,192},{192,256},{256,320},{320,384},{384,448},... | collective-permute-start | bytes 1572872 | tf_op jit(solution)/shard_map/ppermute | solution.py:233
  14.2 9.4 %collective-permute-done.refs_1_ = f32[1024,128]{1,0:T(8,128)S(1)} collective-permute-done((f32[1024,128]{1,0:T(8,128)}, f32[1024,128]{1,0:T(8,128)S(1)}, u32[]{:S(2)}, u32[]{:S(2)}) %collective-permute-start) | collective-permute-done | bytes 524320 | tf_op jit(solution)/shard_map/ppermute | solution.py:233
  23.6 4.9 %collective-permute-done.1.refs_2_ = f32[1024,128]{1,0:T(8,128)S(1)} collective-permute-done((f32[1024,128]{1,0:T(8,128)}, f32[1024,128]{1,0:T(8,128)S(1)}, u32[]{:S(2)}, u32[]{:S(2)}) %collective-permute-start.1) | collective-permute-done | bytes 524320 | tf_op jit(solution)/shard_map/ppermute | solution.py:234
  28.6 4.2 %collective-permute-start.2 = (f32[1024,128]{1,0:T(8,128)S(1)}, f32[1024,128]{1,0:T(8,128)S(1)}, u32[]{:S(2)}, u32[]{:S(2)}) collective-permute-start(f32[1024,128]{1,0:T(8,128)S(1)} %collective-permute-done.refs_1_), channel_id=1, source_target_pairs={{0,64},{64,128},{128,192},{192,256},{256,320},{320,384},{384,448},... | collective-permute-start | bytes 1572872 | tf_op jit(solution)/shard_map/ppermute | solution.py:233
  35.8 6.6 %collective-permute-done.2.refs_3_ = f32[1024,128]{1,0:T(8,128)S(1)} collective-permute-done((f32[1024,128]{1,0:T(8,128)S(1)}, f32[1024,128]{1,0:T(8,128)S(1)}, u32[]{:S(2)}, u32[]{:S(2)}) %collective-permute-start.2) | collective-permute-done | bytes 524320 | tf_op jit(solution)/shard_map/ppermute | solution.py:233
  42.4 3.7 %collective-permute-done.3.refs_4_ = f32[1024,128]{1,0:T(8,128)S(1)} collective-permute-done((f32[1024,128]{1,0:T(8,128)S(1)}, f32[1024,128]{1,0:T(8,128)S(1)}, u32[]{:S(2)}, u32[]{:S(2)}) %collective-permute-start.3) | collective-permute-done | bytes 524320 | tf_op jit(solution)/shard_map/ppermute | solution.py:234
  46.1 4.1 %collective-permute-start.4 = (f32[1024,128]{1,0:T(8,128)S(1)}, f32[1024,128]{1,0:T(8,128)}, u32[]{:S(2)}, u32[]{:S(2)}) collective-permute-start(f32[1024,128]{1,0:T(8,128)S(1)} %collective-permute-done.2.refs_3_), channel_id=1, source_target_pairs={{0,64},{64,128},{128,192},{192,256},{256,320},{320,384},{384,448},... | collective-permute-start | bytes 1572872 | tf_op jit(solution)/shard_map/ppermute | solution.py:233
  53.0 5.7 %collective-permute-done.4.refs_5_ = f32[1024,128]{1,0:T(8,128)} collective-permute-done((f32[1024,128]{1,0:T(8,128)S(1)}, f32[1024,128]{1,0:T(8,128)}, u32[]{:S(2)}, u32[]{:S(2)}) %collective-permute-start.4) | collective-permute-done | bytes 524320 | tf_op jit(solution)/shard_map/ppermute | solution.py:233
  58.7 3.8 %collective-permute-done.5.refs_6_ = f32[1024,128]{1,0:T(8,128)S(1)} collective-permute-done((f32[1024,128]{1,0:T(8,128)S(1)}, f32[1024,128]{1,0:T(8,128)S(1)}, u32[]{:S(2)}, u32[]{:S(2)}) %collective-permute-start.5) | collective-permute-done | bytes 524320 | tf_op jit(solution)/shard_map/ppermute | solution.py:234
  63.3 3.5 %collective-permute-start.6 = (f32[1024,128]{1,0:T(8,128)}, f32[1024,128]{1,0:T(8,128)S(1)}, u32[]{:S(2)}, u32[]{:S(2)}) collective-permute-start(f32[1024,128]{1,0:T(8,128)} %collective-permute-done.4.refs_5_), channel_id=1, source_target_pairs={{0,64},{64,128},{128,192},{192,256},{256,320},{320,384},{384,448},... | collective-permute-start | bytes 1572872 | tf_op jit(solution)/shard_map/ppermute | solution.py:233
  69.0 5.8 %collective-permute-done.6.up.refs_7_ = f32[1024,128]{1,0:T(8,128)S(1)} collective-permute-done((f32[1024,128]{1,0:T(8,128)}, f32[1024,128]{1,0:T(8,128)S(1)}, u32[]{:S(2)}, u32[]{:S(2)}) %collective-permute-start.6) | collective-permute-done | bytes 524320 | tf_op jit(solution)/shard_map/ppermute | solution.py:233
  74.9 3.4 %collective-permute-done.7.down.refs_8_ = f32[1024,128]{1,0:T(8,128)S(1)} collective-permute-done((f32[1024,128]{1,0:T(8,128)}, f32[1024,128]{1,0:T(8,128)S(1)}, u32[]{:S(2)}, u32[]{:S(2)}) %collective-permute-start.7) | collective-permute-done | bytes 524320 | tf_op jit(solution)/shard_map/ppermute | solution.py:234
  81.9 2.6 %collective-permute-start.9 = (f32[128,512]{1,0:T(8,128)S(1)}, f32[128,512]{1,0:T(8,128)}, u32[]{:S(2)}, u32[]{:S(2)}) collective-permute-start(f32[128,512]{1,0:T(8,128)S(1)} %get-tuple-element.51), channel_id=1, source_target_pairs={{256,384},{320,448},{128,0},{192,64},{257,385},{321,449},{129,1},{... | collective-permute-start | bytes 786440 | tf_op jit(solution)/shard_map/ppermute | solution.py:241
  85.9 3.8 %collective-permute-done.8.refs_9_ = f32[128,512]{1,0:T(8,128)S(1)} collective-permute-done((f32[128,512]{1,0:T(8,128)S(1)}, f32[128,512]{1,0:T(8,128)S(1)}, u32[]{:S(2)}, u32[]{:S(2)}) %collective-permute-start.8) | collective-permute-done | bytes 262176 | tf_op jit(solution)/shard_map/ppermute | solution.py:241
  90.4 11.9 %collective-permute-done.9.refs_10_ = f32[128,512]{1,0:T(8,128)} collective-permute-done((f32[128,512]{1,0:T(8,128)S(1)}, f32[128,512]{1,0:T(8,128)}, u32[]{:S(2)}, u32[]{:S(2)}) %collective-permute-start.9) | collective-permute-done | bytes 262176 | tf_op jit(solution)/shard_map/ppermute | solution.py:241
  102.3 3.5 %pick.1 = f32[2,512,256]{2,1,0:T(8,128)} custom-call(s32[20]{0:T(128)} %pad_add_fusion.info, f32[1024,128]{1,0:T(8,128)} %bitcast.70, f32[1024,128]{1,0:T(8,128)} %copy-done.4, f32[1024,128]{1,0:T(8,128)} %copy-done.5, f32[1024,128]{1,0:T(8,128)} %copy-done.6, f32[1024,128]{1,0:T(8,128)} %copy-done.7, f32[1024,128]{1,0:T(8,128)} %collective-permute-done.4.refs_5_, ...), custom_call_target="tpu_custom_call" | custom-call | bytes 3145728 | tf_op jit(solution)/shard_map/pick/pallas_call | solution.py:98
  106.0 9.8 %collective-permute-start.11 = (f32[256,256]{1,0:T(8,128)S(1)}, f32[256,256]{1,0:T(8,128)S(1)}, u32[]{:S(2)}, u32[]{:S(2)}) collective-permute-start(f32[256,256]{1,0:T(8,128)S(1)} %bitcast.71), channel_id=1, source_target_pairs={{0,32},{32,0},{1,33},{33,1},{2,34},{34,2},{3,35},{35,3},{4,36},{36... | collective-permute-start | bytes 786440 | tf_op jit(solution)/shard_map/ppermute | solution.py:11
  116.4 2.9 %gather_fusion.1 = f32[4,512,256]{2,1,0:T(8,128)S(1)} fusion(f32[8,512,256]{2,1,0:T(8,128)} %all-gather.5.cloned.1.call-done, s32[1024]{0:T(1024)S(1)} %pad_clamp_fusion.1), kind=kCustom, calls=%fused_computation.1 | custom fusion | bytes 4194320 | tf_op jit(solution)/shard_map/jit(_take)/gather | solution.py:256
  121.1 2.9 %gather_fusion.2 = f32[4,512,256]{2,1,0:T(8,128)S(1)} fusion(f32[8,512,256]{2,1,0:T(8,128)} %all-gather.5.cloned.1.call-done, s32[1024]{0:T(1024)S(1)} %pad_clamp_fusion), kind=kCustom, calls=%fused_computation.2 | custom fusion | bytes 4194320 | tf_op jit(solution)/shard_map/jit(_take)/gather | solution.py:258
  124.0 14.5 %collective-permute-done.11.refs_2_ = f32[256,256]{1,0:T(8,128)S(1)} collective-permute-done((f32[256,256]{1,0:T(8,128)S(1)}, f32[256,256]{1,0:T(8,128)S(1)}, u32[]{:S(2)}, u32[]{:S(2)}) %collective-permute-start.11) | collective-permute-done | bytes 262176 | tf_op jit(solution)/shard_map/ppermute | solution.py:11
  138.5 7.7 %collective-permute-start.12 = (f32[256,256]{1,0:T(8,128)}, f32[256,256]{1,0:T(8,128)S(1)}, u32[]{:S(2)}, u32[]{:S(2)}) collective-permute-start(f32[256,256]{1,0:T(8,128)} %bitcast.7), channel_id=1, source_target_pairs={{0,32},{32,0},{1,33},{33,1},{2,34},{34,2},{3,35},{35,3},{4,36},{36... | collective-permute-start | bytes 786440 | tf_op jit(solution)/shard_map/ppermute | solution.py:11
  146.2 4.3 %collective-permute-start.16 = (f32[256,256]{1,0:T(8,128)S(1)}, f32[256,256]{1,0:T(8,128)S(1)}, u32[]{:S(2)}, u32[]{:S(2)}) collective-permute-start(f32[256,256]{1,0:T(8,128)S(1)} %collective-permute-done.11.refs_2_), channel_id=1, source_target_pairs={{0,24},{8,0},{16,8},{24,16},{1,25},{9,1},{17,9},{25,17},{2,26},{10... | collective-permute-start | bytes 786440 | tf_op jit(solution)/shard_map/ppermute | solution.py:11
  155.5 10.9 %collective-permute-done.12.refs_1_ = f32[256,256]{1,0:T(8,128)S(1)} collective-permute-done((f32[256,256]{1,0:T(8,128)}, f32[256,256]{1,0:T(8,128)S(1)}, u32[]{:S(2)}, u32[]{:S(2)}) %collective-permute-start.12) | collective-permute-done | bytes 262176 | tf_op jit(solution)/shard_map/ppermute | solution.py:11
  166.4 4.3 %collective-permute-start.13 = (f32[256,256]{1,0:T(8,128)S(1)}, f32[256,256]{1,0:T(8,128)S(1)}, u32[]{:S(2)}, u32[]{:S(2)}) collective-permute-start(f32[256,256]{1,0:T(8,128)S(1)} %collective-permute-done.12.refs_1_), channel_id=1, source_target_pairs={{0,24},{8,0},{16,8},{24,16},{1,25},{9,1},{17,9},{25,17},{2,26},{10... | collective-permute-start | bytes 786440 | tf_op jit(solution)/shard_map/ppermute | solution.py:11
  176.5 8.1 %product.2.refs_5_ = f32[512,256]{1,0:T(8,128)} custom-call(s32[8]{0:T(128)} %pad_add_fusion.3.classes, f32[8,2,512,256]{3,2,1,0:T(8,128)} %bitcast.61, f32[2048,256]{1,0:T(8,128)} %bitcast.67, f32[256,256]{1,0:T(8,128)} %copy-done.10, f32[256,256]{1,0:T(8,128)} %copy-done.14, f32[256,256]{1,0:T(8,128)} %copy-done.16, f32[256,256]{1,0:T(8,128)} %collective-permute-done.18.refs_5_), custom_call_target="tpu_custom_call" | custom-call | flops 2415919104 | bytes 9437184 | tf_op jit(solution)/shard_map/product/pallas_call | solution.py:184
  184.7 3.4 %collective-permute-done.15.refs_4_ = f32[256,256]{1,0:T(8,128)} collective-permute-done((f32[256,256]{1,0:T(8,128)S(1)}, f32[256,256]{1,0:T(8,128)}, u32[]{:S(2)}, u32[]{:S(2)}) %collective-permute-start.15) | collective-permute-done | bytes 262176 | tf_op jit(solution)/shard_map/ppermute | solution.py:11
  188.1 6.5 %product.3 = (f32[512,256]{1,0:T(8,128)}, f32[256,256]{1,0:T(8,128)}, f32[256,256]{1,0:T(8,128)}, f32[256,256]{1,0:T(8,128)}, f32[256,256]{1,0:T(8,128)}) custom-call(s32[8]{0:T(128)} %pad_add_fusion.3.classes, f32[8,2,512,256]{3,2,1,0:T(8,128)} %bitcast.62, f32[256,256]{1,0:T(8,128)} %copy-done.11, f32[256,256]{1,0:T(8,128)} %copy-done.12, ...), custom_call_target="tpu_custom_call" | custom-call | flops 805306368 | bytes 3145728 | tf_op jit(solution)/shard_map/product/pallas_call | solution.py:184
  199.2 4.1 %collective-permute-start.21 = (f32[256,256]{1,0:T(8,128)}, f32[256,256]{1,0:T(8,128)S(1)}, u32[]{:S(2)}, u32[]{:S(2)}) collective-permute-start(f32[256,256]{1,0:T(8,128)} %get-tuple-element.73), channel_id=1, source_target_pairs={{0,24},{8,0},{16,8},{24,16},{1,25},{9,1},{17,9},{25,17},{2,26},{10... | collective-permute-start | bytes 786440 | tf_op jit(solution)/shard_map/ppermute | solution.py:11
  203.3 7.7 %collective-permute-done.19 = f32[256,256]{1,0:T(8,128)S(1)} collective-permute-done((f32[256,256]{1,0:T(8,128)}, f32[256,256]{1,0:T(8,128)S(1)}, u32[]{:S(2)}, u32[]{:S(2)}) %collective-permute-start.19) | collective-permute-done | bytes 262176 | tf_op jit(solution)/shard_map/ppermute | solution.py:11
  215.7 6.3 %collective-permute-start.22 = (f32[256,256]{1,0:T(8,128)S(1)}, f32[256,256]{1,0:T(8,128)S(1)}, u32[]{:S(2)}, u32[]{:S(2)}) collective-permute-start(f32[256,256]{1,0:T(8,128)S(1)} %add_add_fusion.1), channel_id=1, source_target_pairs={{0,32},{32,0},{1,33},{33,1},{2,34},{34,2},{3,35},{35,3},{4,36},{36... | collective-permute-start | bytes 786440 | tf_op jit(solution)/shard_map/ppermute | solution.py:11
  223.9 4.2 %collective-permute-start.24 = (f32[256,256]{1,0:T(8,128)S(1)}, f32[256,256]{1,0:T(8,128)S(1)}, u32[]{:S(2)}, u32[]{:S(2)}) collective-permute-start(f32[256,256]{1,0:T(8,128)S(1)} %fusion.2), channel_id=1, source_target_pairs={{0,16},{8,24},{16,0},{24,8},{1,17},{9,25},{17,1},{25,9},{2,18},{10... | collective-permute-start | bytes 786440 | tf_op jit(solution)/shard_map/ppermute | solution.py:11
  230.4 14.1 %collective-permute-done.22 = f32[256,256]{1,0:T(8,128)S(1)} collective-permute-done((f32[256,256]{1,0:T(8,128)S(1)}, f32[256,256]{1,0:T(8,128)S(1)}, u32[]{:S(2)}, u32[]{:S(2)}) %collective-permute-start.22) | collective-permute-done | bytes 262176 | tf_op jit(solution)/shard_map/ppermute | solution.py:11
  (107 shorter events, 45.4 us)
Async XLA Ops:
  7.2 77.9 %copy-start.3 = (f32[1,4,1,128,256]{4,3,2,1,0:T(8,128)S(1)}, f32[1,4,1,128,256]{4,3,2,1,0:T(8,128)}, u32[]{:S(2)}) copy-start(f32[1,4,1,128,256]{4,3,2,1,0:T(8,128)} %param.6) | copy-start | bytes 1572868
  7.2 95.0 %all-gather.7.cloned.1.call-start = ((), (), s32[]{:S(2)}) async-start(), calls=%async_computation.1 | async-start | bytes 2621440 | tf_op jit(solution)/shard_map/all_gather | solution.py:228
  7.9 94.3 %all-gather.5.cloned.1.call-start = ((), (), s32[]{:S(2)}) async-start(), calls=%async_computation | async-start | bytes 4718592 | tf_op jit(solution)/shard_map/all_gather | solution.py:227
  8.7 167.8 %all-gather.9.cloned.1.call-start = ((), (), s32[]{:S(2)}) async-start(), calls=%async_computation.2 | async-start | bytes 9437184 | tf_op jit(solution)/shard_map/all_gather | solution.py:259
  8.7 14.9 %collective-permute-start = (f32[1024,128]{1,0:T(8,128)}, f32[1024,128]{1,0:T(8,128)S(1)}, u32[]{:S(2)}, u32[]{:S(2)}) collective-permute-start(f32[1024,128]{1,0:T(8,128)} %bitcast.68), channel_id=1, source_target_pairs={{0,64},{64,128},{128,192},{192,256},{256,320},{320,384},{384,448},... | collective-permute-start | bytes 1572872 | tf_op jit(solution)/shard_map/ppermute | solution.py:233
  12.3 16.3 %collective-permute-start.1 = (f32[1024,128]{1,0:T(8,128)}, f32[1024,128]{1,0:T(8,128)S(1)}, u32[]{:S(2)}, u32[]{:S(2)}) collective-permute-start(f32[1024,128]{1,0:T(8,128)} %bitcast.69), channel_id=1, source_target_pairs={{64,0},{128,64},{192,128},{256,192},{320,256},{384,320},{448,384},... | collective-permute-start | bytes 1572872 | tf_op jit(solution)/shard_map/ppermute | solution.py:234
  23.6 78.6 %copy-start.4 = (f32[1024,128]{1,0:T(8,128)}, f32[1024,128]{1,0:T(8,128)S(1)}, u32[]{:S(2)}) copy-start(f32[1024,128]{1,0:T(8,128)S(1)} %collective-permute-done.refs_1_) | copy-start | bytes 1572868
  28.6 73.7 %copy-start.5 = (f32[1024,128]{1,0:T(8,128)}, f32[1024,128]{1,0:T(8,128)S(1)}, u32[]{:S(2)}) copy-start(f32[1024,128]{1,0:T(8,128)S(1)} %collective-permute-done.1.refs_2_) | copy-start | bytes 1572868
  28.6 13.9 %collective-permute-start.2 = (f32[1024,128]{1,0:T(8,128)S(1)}, f32[1024,128]{1,0:T(8,128)S(1)}, u32[]{:S(2)}, u32[]{:S(2)}) collective-permute-start(f32[1024,128]{1,0:T(8,128)S(1)} %collective-permute-done.refs_1_), channel_id=1, source_target_pairs={{0,64},{64,128},{128,192},{192,256},{256,320},{320,384},{384,448},... | collective-permute-start | bytes 1572872 | tf_op jit(solution)/shard_map/ppermute | solution.py:233
  32.8 13.3 %collective-permute-start.3 = (f32[1024,128]{1,0:T(8,128)S(1)}, f32[1024,128]{1,0:T(8,128)S(1)}, u32[]{:S(2)}, u32[]{:S(2)}) collective-permute-start(f32[1024,128]{1,0:T(8,128)S(1)} %collective-permute-done.1.refs_2_), channel_id=1, source_target_pairs={{64,0},{128,64},{192,128},{256,192},{320,256},{384,320},{448,384},... | collective-permute-start | bytes 1572872 | tf_op jit(solution)/shard_map/ppermute | solution.py:234
  46.1 12.6 %collective-permute-start.4 = (f32[1024,128]{1,0:T(8,128)S(1)}, f32[1024,128]{1,0:T(8,128)}, u32[]{:S(2)}, u32[]{:S(2)}) collective-permute-start(f32[1024,128]{1,0:T(8,128)S(1)} %collective-permute-done.2.refs_3_), channel_id=1, source_target_pairs={{0,64},{64,128},{128,192},{192,256},{256,320},{320,384},{384,448},... | collective-permute-start | bytes 1572872 | tf_op jit(solution)/shard_map/ppermute | solution.py:233
  50.2 12.3 %collective-permute-start.5 = (f32[1024,128]{1,0:T(8,128)S(1)}, f32[1024,128]{1,0:T(8,128)S(1)}, u32[]{:S(2)}, u32[]{:S(2)}) collective-permute-start(f32[1024,128]{1,0:T(8,128)S(1)} %collective-permute-done.3.refs_4_), channel_id=1, source_target_pairs={{64,0},{128,64},{192,128},{256,192},{320,256},{384,320},{448,384},... | collective-permute-start | bytes 1572872 | tf_op jit(solution)/shard_map/ppermute | solution.py:234
  63.3 11.6 %collective-permute-start.6 = (f32[1024,128]{1,0:T(8,128)}, f32[1024,128]{1,0:T(8,128)S(1)}, u32[]{:S(2)}, u32[]{:S(2)}) collective-permute-start(f32[1024,128]{1,0:T(8,128)} %collective-permute-done.4.refs_5_), channel_id=1, source_target_pairs={{0,64},{64,128},{128,192},{192,256},{256,320},{320,384},{384,448},... | collective-permute-start | bytes 1572872 | tf_op jit(solution)/shard_map/ppermute | solution.py:233
  66.8 11.4 %collective-permute-start.7 = (f32[1024,128]{1,0:T(8,128)}, f32[1024,128]{1,0:T(8,128)S(1)}, u32[]{:S(2)}, u32[]{:S(2)}) collective-permute-start(f32[1024,128]{1,0:T(8,128)} %copy-done.8), channel_id=1, source_target_pairs={{64,0},{128,64},{192,128},{256,192},{320,256},{384,320},{448,384},... | collective-permute-start | bytes 1572872 | tf_op jit(solution)/shard_map/ppermute | solution.py:234
  79.1 6.8 %collective-permute-start.10 = (f32[128,512]{1,0:T(8,128)S(1)}, f32[128,512]{1,0:T(8,128)S(1)}, u32[]{:S(2)}, u32[]{:S(2)}) collective-permute-start(f32[128,512]{1,0:T(8,128)S(1)} %get-tuple-element.52), channel_id=1, source_target_pairs={{256,448},{192,0},{257,449},{193,1},{258,450},{194,2},{259,451},{1... | collective-permute-start | bytes 786440 | tf_op jit(solution)/shard_map/ppermute | solution.py:241
  79.7 9.9 %collective-permute-start.8 = (f32[128,512]{1,0:T(8,128)S(1)}, f32[128,512]{1,0:T(8,128)S(1)}, u32[]{:S(2)}, u32[]{:S(2)}) collective-permute-start(f32[128,512]{1,0:T(8,128)S(1)} %get-tuple-element.50), channel_id=1, source_target_pairs={{256,320},{320,384},{384,448},{64,0},{128,64},{192,128},{257,321},... | collective-permute-start | bytes 786440 | tf_op jit(solution)/shard_map/ppermute | solution.py:241
  81.9 20.4 %collective-permute-start.9 = (f32[128,512]{1,0:T(8,128)S(1)}, f32[128,512]{1,0:T(8,128)}, u32[]{:S(2)}, u32[]{:S(2)}) collective-permute-start(f32[128,512]{1,0:T(8,128)S(1)} %get-tuple-element.51), channel_id=1, source_target_pairs={{256,384},{320,448},{128,0},{192,64},{257,385},{321,449},{129,1},{... | collective-permute-start | bytes 786440 | tf_op jit(solution)/shard_map/ppermute | solution.py:241
  106.0 32.5 %collective-permute-start.11 = (f32[256,256]{1,0:T(8,128)S(1)}, f32[256,256]{1,0:T(8,128)S(1)}, u32[]{:S(2)}, u32[]{:S(2)}) collective-permute-start(f32[256,256]{1,0:T(8,128)S(1)} %bitcast.71), channel_id=1, source_target_pairs={{0,32},{32,0},{1,33},{33,1},{2,34},{34,2},{3,35},{35,3},{4,36},{36... | collective-permute-start | bytes 786440 | tf_op jit(solution)/shard_map/ppermute | solution.py:11
  138.5 28.0 %collective-permute-start.12 = (f32[256,256]{1,0:T(8,128)}, f32[256,256]{1,0:T(8,128)S(1)}, u32[]{:S(2)}, u32[]{:S(2)}) collective-permute-start(f32[256,256]{1,0:T(8,128)} %bitcast.7), channel_id=1, source_target_pairs={{0,32},{32,0},{1,33},{33,1},{2,34},{34,2},{3,35},{35,3},{4,36},{36... | collective-permute-start | bytes 786440 | tf_op jit(solution)/shard_map/ppermute | solution.py:11
  146.2 27.1 %collective-permute-start.16 = (f32[256,256]{1,0:T(8,128)S(1)}, f32[256,256]{1,0:T(8,128)S(1)}, u32[]{:S(2)}, u32[]{:S(2)}) collective-permute-start(f32[256,256]{1,0:T(8,128)S(1)} %collective-permute-done.11.refs_2_), channel_id=1, source_target_pairs={{0,24},{8,0},{16,8},{24,16},{1,25},{9,1},{17,9},{25,17},{2,26},{10... | collective-permute-start | bytes 786440 | tf_op jit(solution)/shard_map/ppermute | solution.py:11
  150.5 25.2 %collective-permute-start.17 = (f32[256,256]{1,0:T(8,128)S(1)}, f32[256,256]{1,0:T(8,128)S(1)}, u32[]{:S(2)}, u32[]{:S(2)}) collective-permute-start(f32[256,256]{1,0:T(8,128)S(1)} %collective-permute-done.11.refs_2_), channel_id=1, source_target_pairs={{0,16},{8,24},{16,0},{24,8},{1,17},{9,25},{17,1},{25,9},{2,18},{10... | collective-permute-start | bytes 786440 | tf_op jit(solution)/shard_map/ppermute | solution.py:11
  153.1 23.4 %collective-permute-start.18 = (f32[256,256]{1,0:T(8,128)S(1)}, f32[256,256]{1,0:T(8,128)}, u32[]{:S(2)}, u32[]{:S(2)}) collective-permute-start(f32[256,256]{1,0:T(8,128)S(1)} %collective-permute-done.11.refs_2_), channel_id=1, source_target_pairs={{0,8},{8,16},{16,24},{24,0},{1,9},{9,17},{17,25},{25,1},{2,10},{10... | collective-permute-start | bytes 786440 | tf_op jit(solution)/shard_map/ppermute | solution.py:11
  166.4 18.2 %collective-permute-start.13 = (f32[256,256]{1,0:T(8,128)S(1)}, f32[256,256]{1,0:T(8,128)S(1)}, u32[]{:S(2)}, u32[]{:S(2)}) collective-permute-start(f32[256,256]{1,0:T(8,128)S(1)} %collective-permute-done.12.refs_1_), channel_id=1, source_target_pairs={{0,24},{8,0},{16,8},{24,16},{1,25},{9,1},{17,9},{25,17},{2,26},{10... | collective-permute-start | bytes 786440 | tf_op jit(solution)/shard_map/ppermute | solution.py:11
  170.8 13.9 %collective-permute-start.14 = (f32[256,256]{1,0:T(8,128)S(1)}, f32[256,256]{1,0:T(8,128)S(1)}, u32[]{:S(2)}, u32[]{:S(2)}) collective-permute-start(f32[256,256]{1,0:T(8,128)S(1)} %collective-permute-done.12.refs_1_), channel_id=1, source_target_pairs={{0,16},{8,24},{16,0},{24,8},{1,17},{9,25},{17,1},{25,9},{2,18},{10... | collective-permute-start | bytes 786440 | tf_op jit(solution)/shard_map/ppermute | solution.py:11
  173.3 14.8 %collective-permute-start.15 = (f32[256,256]{1,0:T(8,128)S(1)}, f32[256,256]{1,0:T(8,128)}, u32[]{:S(2)}, u32[]{:S(2)}) collective-permute-start(f32[256,256]{1,0:T(8,128)S(1)} %collective-permute-done.12.refs_1_), channel_id=1, source_target_pairs={{0,8},{8,16},{16,24},{24,0},{1,9},{9,17},{17,25},{25,1},{2,10},{10... | collective-permute-start | bytes 786440 | tf_op jit(solution)/shard_map/ppermute | solution.py:11
  194.6 16.4 %collective-permute-start.19 = (f32[256,256]{1,0:T(8,128)}, f32[256,256]{1,0:T(8,128)S(1)}, u32[]{:S(2)}, u32[]{:S(2)}) collective-permute-start(f32[256,256]{1,0:T(8,128)} %get-tuple-element.69), channel_id=1, source_target_pairs={{0,8},{8,16},{16,24},{24,0},{1,9},{9,17},{17,25},{25,1},{2,10},{10... | collective-permute-start | bytes 786440 | tf_op jit(solution)/shard_map/ppermute | solution.py:11
  196.6 19.0 %collective-permute-start.20 = (f32[256,256]{1,0:T(8,128)}, f32[256,256]{1,0:T(8,128)S(1)}, u32[]{:S(2)}, u32[]{:S(2)}) collective-permute-start(f32[256,256]{1,0:T(8,128)} %get-tuple-element.72), channel_id=1, source_target_pairs={{0,16},{8,24},{16,0},{24,8},{1,17},{9,25},{17,1},{25,9},{2,18},{10... | collective-permute-start | bytes 786440 | tf_op jit(solution)/shard_map/ppermute | solution.py:11
  199.2 16.4 %collective-permute-start.21 = (f32[256,256]{1,0:T(8,128)}, f32[256,256]{1,0:T(8,128)S(1)}, u32[]{:S(2)}, u32[]{:S(2)}) collective-permute-start(f32[256,256]{1,0:T(8,128)} %get-tuple-element.73), channel_id=1, source_target_pairs={{0,24},{8,0},{16,8},{24,16},{1,25},{9,1},{17,9},{25,17},{2,26},{10... | collective-permute-start | bytes 786440 | tf_op jit(solution)/shard_map/ppermute | solution.py:11
  215.7 28.9 %collective-permute-start.22 = (f32[256,256]{1,0:T(8,128)S(1)}, f32[256,256]{1,0:T(8,128)S(1)}, u32[]{:S(2)}, u32[]{:S(2)}) collective-permute-start(f32[256,256]{1,0:T(8,128)S(1)} %add_add_fusion.1), channel_id=1, source_target_pairs={{0,32},{32,0},{1,33},{33,1},{2,34},{34,2},{3,35},{35,3},{4,36},{36... | collective-permute-start | bytes 786440 | tf_op jit(solution)/shard_map/ppermute | solution.py:11
  222.0 22.6 %collective-permute-start.23 = (f32[256,256]{1,0:T(8,128)S(1)}, f32[256,256]{1,0:T(8,128)S(1)}, u32[]{:S(2)}, u32[]{:S(2)}) collective-permute-start(f32[256,256]{1,0:T(8,128)S(1)} %fusion.4), channel_id=1, source_target_pairs={{0,8},{8,16},{16,24},{24,0},{1,9},{9,17},{17,25},{25,1},{2,10},{10... | collective-permute-start | bytes 786440 | tf_op jit(solution)/shard_map/ppermute | solution.py:11
  223.9 20.7 %collective-permute-start.24 = (f32[256,256]{1,0:T(8,128)S(1)}, f32[256,256]{1,0:T(8,128)S(1)}, u32[]{:S(2)}, u32[]{:S(2)}) collective-permute-start(f32[256,256]{1,0:T(8,128)S(1)} %fusion.2), channel_id=1, source_target_pairs={{0,16},{8,24},{16,0},{24,8},{1,17},{9,25},{17,1},{25,9},{2,18},{10... | collective-permute-start | bytes 786440 | tf_op jit(solution)/shard_map/ppermute | solution.py:11
  228.1 16.5 %collective-permute-start.25 = (f32[256,256]{1,0:T(8,128)S(1)}, f32[256,256]{1,0:T(8,128)S(1)}, u32[]{:S(2)}, u32[]{:S(2)}) collective-permute-start(f32[256,256]{1,0:T(8,128)S(1)} %fusion), channel_id=1, source_target_pairs={{0,24},{8,0},{16,8},{24,16},{1,25},{9,1},{17,9},{25,17},{2,26},{10... | collective-permute-start | bytes 786440 | tf_op jit(solution)/shard_map/ppermute | solution.py:11
  (16 other events, 249.1 us)
Sparse Core Ops, SparseCore 0:
  10.1 42.2 all-gather.6
  54.5 40.3 all-gather.4
  105.9 64.4 all-gather.8
